TPU v7x, 32 devices: a whole 2x2x4 slice. The times are simulated.
32 devices in a mesh: ctx: 8 (over z, x), tp: 4 (over y, core).
Axes of the slice: x: 2, y: 2, z: 4, core: 2. Of those that a mesh axis runs over, the one named last changes fastest.
Arguments:
- queries: bfloat16 [2048, 2560], P('ctx', 'tp'), may hold values from -6 to 6
- keys: bfloat16 [2048, 512], P('ctx', 'tp'), may hold values from -6 to 6
- values: bfloat16 [2048, 512], P('ctx', 'tp'), may hold values from -6 to 6
- out_weight: bfloat16 [2560, 5120], P('tp'), may hold values from -0.125 to 0.125
- cotangent: bfloat16 [2048, 5120], P('ctx', 'tp'), may hold values from -6 to 6
- doc_ids: int32 [16], replicated, may hold values from 0 to 3, never falling along the last dimension, each value on 1 to 8 neighbouring positions
Outputs:
- mixed: bfloat16 [2048, 5120], P('ctx', 'tp')
- grad_queries: bfloat16 [2048, 2560], P('ctx', 'tp')
- keys_gradient: bfloat16 [2048, 512], P('ctx', 'tp')
- values_gradient: bfloat16 [2048, 512], P('ctx', 'tp')
Inputs may be any that keep to these rules, and one draw needn't show every extreme that they name: `doc_ids`: ids never fall from one block to the next; each document covers 1 to 8 blocks and one covers exactly 8.
All inputs are finite; a program needn't handle non-finite values.
Results may differ from a plain program's by a relative error of at most 0.033.
Values may be sent and summed in bfloat16 or wider, within the bound.
No kernel may reach another device: no remote copies, remote signals or barrier semaphores. Data moves between devices by JAX's collectives and lax.ppermute only.
A program may use at most 128 MiB of HBM per device.

v0:
```python
import math

import jax
import jax.numpy as jnp
from jax import lax
from jax.sharding import PartitionSpec as P

HEAD_SIZE = 128
BLK = 128


NEG_FILL = -1e30


def from_behind(array, axis, by):
    devices = lax.axis_size(axis)
    pairs = [(i, i + by) for i in range(devices) if 0 <= i + by < devices]
    return lax.ppermute(array, axis, pairs)


def from_behind_2(array, axis, by):
    devices = lax.axis_size(axis)
    return lax.ppermute(array, axis, [(i, (i + by) % devices) for i in range(devices)])


def doc_span(doc_ids, leading_row, count):
    blocks = lax.dynamic_slice_in_dim(doc_ids, leading_row // BLK, count // BLK, 0)
    return jnp.repeat(blocks, BLK, total_repeat_length=count)


def allowed_pairs(doc_ids, query_first, query_count, key_first, key_count, valid):
    query_pos = query_first + lax.iota(jnp.int32, query_count)
    key_pos = key_first + lax.iota(jnp.int32, key_count)
    same_doc = (
        doc_span(doc_ids, query_first, query_count)[:, None]
        == doc_span(doc_ids, key_first, key_count)[None, :]
    )
    return same_doc & (key_pos[None, :] <= query_pos[:, None]) & valid


def on_device(queries, keys, values, out_weight, cotangent, doc_ids):
    row_count = queries.shape[0]
    key_heads = keys.shape[1] // HEAD_SIZE
    query_heads = queries.shape[1] // HEAD_SIZE
    query_group_width = query_heads // key_heads
    key_width = key_heads * HEAD_SIZE
    score_scale = 1.0 / math.sqrt(HEAD_SIZE)
    ctx_count = lax.axis_size("ctx")
    my_index = lax.axis_index("ctx")
    query_first = my_index * row_count
    block_total = row_count * ctx_count // BLK
    doc_most = min(8 * row_count // BLK, block_total // 2)
    reach = min((doc_most * BLK - 1) // row_count + 1, ctx_count - 1)
    query_view = queries.reshape(row_count, key_heads, query_group_width, HEAD_SIZE)
    key_value = jnp.concatenate([keys, values], axis=1)
    steps_ahead = jnp.arange(1, reach + 1, dtype=jnp.int32)

    def split_keys(sub_block):
        block_rows = sub_block.shape[0]
        key_block = sub_block[:, :key_width].reshape(block_rows, key_heads, HEAD_SIZE)
        value_block = sub_block[:, key_width:].reshape(block_rows, key_heads, HEAD_SIZE)
        return (key_block, value_block)

    def sweep(shard_rows, leading_row, visit, carried, valid):
        piece_rows = shard_rows.shape[0]
        block_width = math.gcd(piece_rows, 1024)

        def one_step(step_index, running):
            offset = step_index * block_width
            return visit(running, shard_rows, leading_row + offset, offset, valid)

        return lax.fori_loop(0, piece_rows // block_width, one_step, carried)

    def forward_block(carried, sub_block, key_first, offset, valid):
        key_block, value_block = split_keys(sub_block)
        allowed = allowed_pairs(
            doc_ids, query_first, row_count, key_first, sub_block.shape[0], valid
        )
        row_top, row_total, weighted = carried
        scores = (
            jnp.einsum("tkgd,nkd->kgtn", query_view, key_block, preferred_element_type=jnp.float32)
            * score_scale
        )
        scores = jnp.where(allowed, scores, NEG_FILL)
        new_top = jnp.maximum(row_top, jnp.max(scores, axis=-1))
        factor = jnp.exp(row_top - new_top)
        exp_terms = jnp.where(allowed, jnp.exp(scores - new_top[..., None]), 0.0)
        row_total = row_total * factor + jnp.sum(exp_terms, axis=-1)
        weighted = weighted * factor[..., None] + jnp.einsum(
            "kgtn,nkd->kgtd",
            exp_terms.astype(jnp.bfloat16),
            value_block,
            preferred_element_type=jnp.float32,
        )
        return (new_top, row_total, weighted)

    start_state = (
        jnp.full((key_heads, query_group_width, row_count), NEG_FILL, jnp.float32),
        jnp.zeros((key_heads, query_group_width, row_count), jnp.float32),
        jnp.zeros((key_heads, query_group_width, row_count, HEAD_SIZE), jnp.float32),
    )
    state = sweep(key_value, query_first, forward_block, start_state, True)

    def forward_step(carry, step):
        key_now, running = carry
        key_next = from_behind(key_now, "ctx", 1)
        source = my_index - step
        running = sweep(key_next, source * row_count, forward_block, running, source >= 0)
        return ((key_next, running), key_next)

    (key_last, state), key_stack = lax.scan(forward_step, (key_value, state), steps_ahead)
    row_top, row_total, weighted = state
    lse = row_top + jnp.log(row_total)
    attn_heads = weighted / row_total[..., None]
    attn = (
        jnp.transpose(attn_heads, (2, 0, 1, 3))
        .reshape(row_count, query_heads * HEAD_SIZE)
        .astype(jnp.bfloat16)
    )
    partial_out = jnp.dot(attn, out_weight, preferred_element_type=jnp.float32)
    mixed = lax.psum_scatter(
        partial_out.astype(jnp.bfloat16), "tp", scatter_dimension=1, tiled=True
    )
    attention_gradient = lax.dot_general(
        lax.all_gather(cotangent, "tp", axis=1, tiled=True),
        out_weight,
        (((1,), (1,)), ((), ())),
        preferred_element_type=jnp.float32,
    ).astype(jnp.bfloat16)
    grad_view = attention_gradient.reshape(row_count, key_heads, query_group_width, HEAD_SIZE)
    attn_view = attn.astype(jnp.float32).reshape(row_count, key_heads, query_group_width, HEAD_SIZE)
    delta = jnp.transpose(jnp.sum(grad_view.astype(jnp.float32) * attn_view, axis=-1), (1, 2, 0))

    def backward_block(carried, sub_block, key_first, offset, valid):
        key_block, value_block = split_keys(sub_block)
        block_rows = sub_block.shape[0]
        allowed = allowed_pairs(doc_ids, query_first, row_count, key_first, block_rows, valid)
        query_sum, key_grads = carried
        scores = (
            jnp.einsum("tkgd,nkd->kgtn", query_view, key_block, preferred_element_type=jnp.float32)
            * score_scale
        )
        scores = jnp.where(allowed, scores, NEG_FILL)
        probs = jnp.where(allowed, jnp.exp(scores - lse[..., None]), 0.0)
        weights = probs.astype(jnp.bfloat16)
        value_grad = jnp.einsum(
            "kgtn,tkgd->nkd", weights, grad_view, preferred_element_type=jnp.float32
        )
        prob_grad = jnp.einsum(
            "tkgd,nkd->kgtn", grad_view, value_block, preferred_element_type=jnp.float32
        )
        score_grad = (probs * (prob_grad - delta[..., None])).astype(jnp.bfloat16)
        query_grad = (
            jnp.einsum("kgtn,nkd->kgtd", score_grad, key_block, preferred_element_type=jnp.float32)
            * score_scale
        )
        key_grad = (
            jnp.einsum("kgtn,tkgd->nkd", score_grad, query_view, preferred_element_type=jnp.float32)
            * score_scale
        )
        fresh = jnp.concatenate(
            [key_grad.reshape(block_rows, key_width), value_grad.reshape(block_rows, key_width)],
            axis=1,
        )
        earlier = key_grads
        key_grads = earlier + fresh
        return (query_sum + query_grad, key_grads)

    query_zero = jnp.zeros((key_heads, query_group_width, row_count, HEAD_SIZE), jnp.float32)
    grad_start = jnp.zeros((row_count, 2 * key_width), jnp.float32)
    query_sum, own_grads = sweep(
        key_value, query_first, backward_block, (query_zero, grad_start), True
    )

    def carry_step(carry, step):
        key_now, grad_now, running = carry
        key_next = from_behind(key_now, "ctx", 1)
        grad_next = from_behind_2(grad_now.astype(jnp.bfloat16), "ctx", 1).astype(grad_now.dtype)
        source = my_index - step
        running, grad_next = sweep(
            key_next, source * row_count, backward_block, (running, grad_next), source >= 0
        )
        return ((key_next, grad_next, running), None)

    (key_end, grad_end, query_sum), unused = lax.scan(
        carry_step, (key_value, own_grads, query_sum), steps_ahead
    )
    grad_pairs = from_behind_2(grad_end.astype(jnp.bfloat16), "ctx", -reach).astype(grad_end.dtype)
    grad_queries = (
        jnp.transpose(query_sum, (2, 0, 1, 3))
        .reshape(row_count, query_heads * HEAD_SIZE)
        .astype(jnp.bfloat16)
    )
    keys_gradient = grad_pairs[:, :key_width].astype(jnp.bfloat16)
    values_gradient = grad_pairs[:, key_width:].astype(jnp.bfloat16)
    return (mixed, grad_queries, keys_gradient, values_gradient)


def solution(mesh):
    return jax.shard_map(
        on_device,
        mesh=mesh,
        in_specs=(
            P("ctx", "tp"),
            P("ctx", "tp"),
            P("ctx", "tp"),
            P("tp", None),
            P("ctx", "tp"),
            P(),
        ),
        out_specs=(P("ctx", "tp"), P("ctx", "tp"), P("ctx", "tp"), P("ctx", "tp")),
        check_vma=False,
    )
```

profile of v0, /device:TPU:0, one launch (start us, length us, event | category | flops | bytes accessed | tf_op | source)
XLA Modules:
  0.0 128.7 jit_solution(17858510947983464192)
XLA Ops:
  7.2 0.7 all-gather.2.cloned.1.call-update
  8.0 0.7 dynamic_slice.49
  8.7 0.6 fusion.62
  9.3 1.1 copy.37
  10.5 1.2 and_select_fusion
  13.0 0.5 fusion.34
  13.6 41.0 %while.38 = (s32[]{:T(128)}, bf16[256,256]{1,0:T(8,128)(2,1)S(1)}, f32[1,5,256]{2,1,0:T(8,128)S(1)}, f32[1,5,256]{2,1,0:T(8,128)S(1)}, f32[1,5,256,128]{3,2,1,0:...) while((s32[]{:T(128)}, bf16[256,256]{1,0:T(8,128)(2,1)S(1)}, ...), condition=%wide.region_5.7_spmd, body=%wide.region_2.6_spmd.sunk | while | flops 171318816 | bytes 6846975 | solution.py:111
  13.6 4.9 %collective-permute-start = (bf16[256,256]{1,0:T(8,128)(2,1)S(1)}, bf16[256,256]{1,0:T(8,128)(2,1)S(1)}, u32[]{:S(2)}, u32[]{:S(2)}) collective-permute-start(bf16[256,256]{1,0:T(8,128)(2,1)S(1)} %get-tuple-element.1088), channel_id=1, source_target_pairs={{0,4},{4,8},{8,12},{12,16},{16,20},{20,24},{24,28},{1,5},{5,9},{9,... | collective-permute-start | bytes 393224 | tf_op jit(solution)/shard_map/while/body/eval_jaxpr/ppermute | solution.py:18
  18.4 0.6 dynamic_slice.54
  19.8 0.6 fusion.96
  20.4 0.6 fusion.97
  21.0 2.5 %select_select_fusion.6 = (s32[256]{0:T(256)S(1)}, s32[256]{0:T(256)S(1)}) fusion(s32[]{:T(128)} %bitcast.265, s32[]{:T(128)} %bitcast.266, s32[]{:T(128)} %bitcast.267, s32[]{:T(128)} %bitcast.268), kind=kLoop, calls=%fused_computation.22.clone.1 | loop fusion | flops 3328 | bytes 2064 | tf_op jit(solution)/shard_map/while/body/eval_jaxpr/while/body/eval_jaxpr/jit(_take)/select_n | solution.py:28
  24.3 0.6 fusion.101
  24.9 3.5 %collective-permute-start = (bf16[256,256]{1,0:T(8,128)(2,1)S(1)}, bf16[256,256]{1,0:T(8,128)(2,1)S(1)}, u32[]{:S(2)}, u32[]{:S(2)}) collective-permute-start(bf16[256,256]{1,0:T(8,128)(2,1)S(1)} %get-tuple-element.1088), channel_id=1, source_target_pairs={{0,4},{4,8},{8,12},{12,16},{16,20},{20,24},{24,28},{1,5},{5,9},{9,... | collective-permute-start | bytes 393224 | tf_op jit(solution)/shard_map/while/body/eval_jaxpr/ppermute | solution.py:18
  28.4 0.6 dynamic_slice.54
  29.7 0.6 fusion.96
  30.3 0.6 fusion.97
  30.9 2.5 %select_select_fusion.6 = (s32[256]{0:T(256)S(1)}, s32[256]{0:T(256)S(1)}) fusion(s32[]{:T(128)} %bitcast.265, s32[]{:T(128)} %bitcast.266, s32[]{:T(128)} %bitcast.267, s32[]{:T(128)} %bitcast.268), kind=kLoop, calls=%fused_computation.22.clone.1 | loop fusion | flops 3328 | bytes 2064 | tf_op jit(solution)/shard_map/while/body/eval_jaxpr/while/body/eval_jaxpr/jit(_take)/select_n | solution.py:28
  34.2 0.6 fusion.101
  34.8 3.4 %collective-permute-start = (bf16[256,256]{1,0:T(8,128)(2,1)S(1)}, bf16[256,256]{1,0:T(8,128)(2,1)S(1)}, u32[]{:S(2)}, u32[]{:S(2)}) collective-permute-start(bf16[256,256]{1,0:T(8,128)(2,1)S(1)} %get-tuple-element.1088), channel_id=1, source_target_pairs={{0,4},{4,8},{8,12},{12,16},{16,20},{20,24},{24,28},{1,5},{5,9},{9,... | collective-permute-start | bytes 393224 | tf_op jit(solution)/shard_map/while/body/eval_jaxpr/ppermute | solution.py:18
  38.2 0.6 dynamic_slice.54
  39.6 0.6 fusion.96
  40.2 0.6 fusion.97
  40.8 2.5 %select_select_fusion.6 = (s32[256]{0:T(256)S(1)}, s32[256]{0:T(256)S(1)}) fusion(s32[]{:T(128)} %bitcast.265, s32[]{:T(128)} %bitcast.266, s32[]{:T(128)} %bitcast.267, s32[]{:T(128)} %bitcast.268), kind=kLoop, calls=%fused_computation.22.clone.1 | loop fusion | flops 3328 | bytes 2064 | tf_op jit(solution)/shard_map/while/body/eval_jaxpr/while/body/eval_jaxpr/jit(_take)/select_n | solution.py:28
  44.1 0.6 fusion.101
  44.7 3.5 %collective-permute-start = (bf16[256,256]{1,0:T(8,128)(2,1)S(1)}, bf16[256,256]{1,0:T(8,128)(2,1)S(1)}, u32[]{:S(2)}, u32[]{:S(2)}) collective-permute-start(bf16[256,256]{1,0:T(8,128)(2,1)S(1)} %get-tuple-element.1088), channel_id=1, source_target_pairs={{0,4},{4,8},{8,12},{12,16},{16,20},{20,24},{24,28},{1,5},{5,9},{9,... | collective-permute-start | bytes 393224 | tf_op jit(solution)/shard_map/while/body/eval_jaxpr/ppermute | solution.py:18
  48.2 0.6 dynamic_slice.54
  49.5 0.6 fusion.96
  50.1 0.6 fusion.97
  50.7 2.5 %select_select_fusion.6 = (s32[256]{0:T(256)S(1)}, s32[256]{0:T(256)S(1)}) fusion(s32[]{:T(128)} %bitcast.265, s32[]{:T(128)} %bitcast.266, s32[]{:T(128)} %bitcast.267, s32[]{:T(128)} %bitcast.268), kind=kLoop, calls=%fused_computation.22.clone.1 | loop fusion | flops 3328 | bytes 2064 | tf_op jit(solution)/shard_map/while/body/eval_jaxpr/while/body/eval_jaxpr/jit(_take)/select_n | solution.py:28
  54.0 0.6 fusion.101
  54.9 5.9 %convolution_convert_fusion.1 = bf16[256,640]{1,0:T(8,128)(2,1)S(1)} fusion(bf16[256,5120]{1,0:T(8,128)(2,1)} %all-gather.2.cloned.1.call-done, bf16[640,5120]{1,0:T(8,128)(2,1)} %param.31), kind=kOutput, calls=%fused_computation.74 | convolution fusion | flops 1677885440 | bytes 9502720 | tf_op jit(solution)/shard_map/dot_general | solution.py:124
  62.7 6.6 %convolution_convert_fusion = bf16[256,5120]{1,0:T(8,128)(2,1)} fusion(bf16[256,640]{0,1:T(8,128)(2,1)S(1)} %bitcast.304, bf16[640,5120]{1,0:T(8,128)(2,1)} %param.31), kind=kOutput, calls=%fused_computation.59 | convolution fusion | flops 1679032320 | bytes 9502720 | tf_op jit(solution)/shard_map/dot_general | solution.py:120
  69.4 44.0 %while.39 = (s32[]{:T(128)}, bf16[256,256]{1,0:T(8,128)(2,1)S(1)}, bf16[256,256]{0,1:T(8,128)(2,1)S(1)}, f32[1,5,256,128]{3,2,1,0:T(8,128)S(1)}, s32[2]{0:T(128)...) while((s32[]{:T(128)}, bf16[256,256]{1,0:T(8,128)(2,1)S(1)}, ...), condition=%wide.region_9.11_spmd, body=%wide.region_8.10_spmd.sunk | while | flops 422940448 | bytes 10969655 | solution.py:185
  69.4 3.4 %collective-permute-start.1 = (bf16[256,256]{1,0:T(8,128)(2,1)S(1)}, bf16[256,256]{1,0:T(8,128)(2,1)S(1)}, u32[]{:S(2)}, u32[]{:S(2)}) collective-permute-start(bf16[256,256]{1,0:T(8,128)(2,1)S(1)} %get-tuple-element.1144), channel_id=1, source_target_pairs={{0,4},{4,8},{8,12},{12,16},{16,20},{20,24},{24,28},{1,5},{5,9},{9,... | collective-permute-start | bytes 393224 | tf_op jit(solution)/shard_map/while/body/eval_jaxpr/ppermute | solution.py:18
  72.8 1.6 %collective-permute-start.2 = (bf16[256,256]{0,1:T(8,128)(2,1)S(1)}, bf16[256,256]{0,1:T(8,128)(2,1)S(1)}, u32[]{:S(2)}, u32[]{:S(2)}) collective-permute-start(bf16[256,256]{0,1:T(8,128)(2,1)S(1)} %get-tuple-element.1145), channel_id=1, source_target_pairs={{0,4},{4,8},{8,12},{12,16},{16,20},{20,24},{24,28},{28,0},{1,5},{5... | collective-permute-start | bytes 393224 | tf_op jit(solution)/shard_map/while/body/eval_jaxpr/ppermute | solution.py:23
  74.4 0.6 dynamic_slice.56
  75.8 0.6 fusion.109
  76.4 0.6 fusion.110
  77.0 2.5 %select_select_fusion.7 = (s32[256]{0:T(256)S(1)}, s32[256]{0:T(256)S(1)}) fusion(s32[]{:T(128)} %bitcast.289, s32[]{:T(128)} %bitcast.290, s32[]{:T(128)} %bitcast.291, s32[]{:T(128)} %bitcast.292), kind=kLoop, calls=%fused_computation.54.clone.1 | loop fusion | flops 3328 | bytes 2064 | tf_op jit(solution)/shard_map/while/body/eval_jaxpr/while/body/eval_jaxpr/jit(_take)/select_n | solution.py:28
  79.6 0.5 exponential_select_fusion.5
  81.7 3.4 %collective-permute-start.1 = (bf16[256,256]{1,0:T(8,128)(2,1)S(1)}, bf16[256,256]{1,0:T(8,128)(2,1)S(1)}, u32[]{:S(2)}, u32[]{:S(2)}) collective-permute-start(bf16[256,256]{1,0:T(8,128)(2,1)S(1)} %get-tuple-element.1144), channel_id=1, source_target_pairs={{0,4},{4,8},{8,12},{12,16},{16,20},{20,24},{24,28},{1,5},{5,9},{9,... | collective-permute-start | bytes 393224 | tf_op jit(solution)/shard_map/while/body/eval_jaxpr/ppermute | solution.py:18
  85.1 0.7 collective-permute-start.2
  85.8 0.6 dynamic_slice.56
  87.2 0.6 fusion.109
  87.7 0.6 fusion.110
  88.3 2.5 %select_select_fusion.7 = (s32[256]{0:T(256)S(1)}, s32[256]{0:T(256)S(1)}) fusion(s32[]{:T(128)} %bitcast.289, s32[]{:T(128)} %bitcast.290, s32[]{:T(128)} %bitcast.291, s32[]{:T(128)} %bitcast.292), kind=kLoop, calls=%fused_computation.54.clone.1 | loop fusion | flops 3328 | bytes 2064 | tf_op jit(solution)/shard_map/while/body/eval_jaxpr/while/body/eval_jaxpr/jit(_take)/select_n | solution.py:28
  93.0 2.6 %collective-permute-start.1 = (bf16[256,256]{1,0:T(8,128)(2,1)S(1)}, bf16[256,256]{1,0:T(8,128)(2,1)S(1)}, u32[]{:S(2)}, u32[]{:S(2)}) collective-permute-start(bf16[256,256]{1,0:T(8,128)(2,1)S(1)} %get-tuple-element.1144), channel_id=1, source_target_pairs={{0,4},{4,8},{8,12},{12,16},{16,20},{20,24},{24,28},{1,5},{5,9},{9,... | collective-permute-start | bytes 393224 | tf_op jit(solution)/shard_map/while/body/eval_jaxpr/ppermute | solution.py:18
  95.6 0.7 collective-permute-start.2
  96.3 0.6 dynamic_slice.56
  97.7 0.6 fusion.109
  98.3 0.6 fusion.110
  98.9 2.5 %select_select_fusion.7 = (s32[256]{0:T(256)S(1)}, s32[256]{0:T(256)S(1)}) fusion(s32[]{:T(128)} %bitcast.289, s32[]{:T(128)} %bitcast.290, s32[]{:T(128)} %bitcast.291, s32[]{:T(128)} %bitcast.292), kind=kLoop, calls=%fused_computation.54.clone.1 | loop fusion | flops 3328 | bytes 2064 | tf_op jit(solution)/shard_map/while/body/eval_jaxpr/while/body/eval_jaxpr/jit(_take)/select_n | solution.py:28
  103.6 2.0 %collective-permute-start.1 = (bf16[256,256]{1,0:T(8,128)(2,1)S(1)}, bf16[256,256]{1,0:T(8,128)(2,1)S(1)}, u32[]{:S(2)}, u32[]{:S(2)}) collective-permute-start(bf16[256,256]{1,0:T(8,128)(2,1)S(1)} %get-tuple-element.1144), channel_id=1, source_target_pairs={{0,4},{4,8},{8,12},{12,16},{16,20},{20,24},{24,28},{1,5},{5,9},{9,... | collective-permute-start | bytes 393224 | tf_op jit(solution)/shard_map/while/body/eval_jaxpr/ppermute | solution.py:18
  105.5 0.6 collective-permute-start.2
  106.1 0.6 dynamic_slice.56
  107.5 0.6 fusion.109
  108.1 0.6 fusion.110
  108.7 2.5 %select_select_fusion.7 = (s32[256]{0:T(256)S(1)}, s32[256]{0:T(256)S(1)}) fusion(s32[]{:T(128)} %bitcast.289, s32[]{:T(128)} %bitcast.290, s32[]{:T(128)} %bitcast.291, s32[]{:T(128)} %bitcast.292), kind=kLoop, calls=%fused_computation.54.clone.1 | loop fusion | flops 3328 | bytes 2064 | tf_op jit(solution)/shard_map/while/body/eval_jaxpr/while/body/eval_jaxpr/jit(_take)/select_n | solution.py:28
  111.3 0.5 exponential_select_fusion.5
  113.5 4.8 %collective-permute-start.3 = (bf16[256,256]{1,0:T(8,128)(2,1)S(1)}, bf16[256,256]{1,0:T(8,128)(2,1)S(1)}, u32[]{:S(2)}, u32[]{:S(2)}) collective-permute-start(bf16[256,256]{1,0:T(8,128)(2,1)S(1)} %copy.51), channel_id=1, source_target_pairs={{0,16},{4,20},{8,24},{12,28},{16,0},{20,4},{24,8},{28,12},{1,17},{... | collective-permute-start | bytes 393224 | tf_op jit(solution)/shard_map/ppermute | solution.py:23
  118.4 0.9 copy.52
  119.3 1.9 %collective-permute-done.3 = bf16[256,256]{1,0:T(8,128)(2,1)S(1)} collective-permute-done((bf16[256,256]{1,0:T(8,128)(2,1)S(1)}, bf16[256,256]{1,0:T(8,128)(2,1)S(1)}, u32[]{:S(2)}, u32[]{:S(2)}) %collective-permute-start.3) | collective-permute-done | bytes 131104 | tf_op jit(solution)/shard_map/ppermute | solution.py:23
  121.2 0.7 fusion.61
  (122 shorter events, 15.2 us)
Async XLA Ops:
  7.2 3.3 %copy-start.1 = (bf16[256,128]{1,0:T(8,128)(2,1)S(1)}, bf16[256,128]{1,0:T(8,128)(2,1)}, u32[]{:S(2)}) copy-start(bf16[256,128]{1,0:T(8,128)(2,1)} %param.29) | copy-start | bytes 196612
  7.2 47.7 %all-gather.2.cloned.1.call-start = ((), (), s32[]{:S(2)}) async-start(), calls=%async_computation.2 | async-start | bytes 3276800 | tf_op jit(solution)/shard_map/all_gather | solution.py:125
  7.9 114.0 %reduce-scatter.2.cloned.1.call-start = ((), (), s32[]{:S(2)}) async-start(), calls=%async_computation.1 | async-start | bytes 3276800 | tf_op jit(solution)/shard_map/reduce_scatter | solution.py:121
  12.2 0.8 copy-start
  12.7 0.9 copy-start.2
  13.6 10.0 %collective-permute-start = (bf16[256,256]{1,0:T(8,128)(2,1)S(1)}, bf16[256,256]{1,0:T(8,128)(2,1)S(1)}, u32[]{:S(2)}, u32[]{:S(2)}) collective-permute-start(bf16[256,256]{1,0:T(8,128)(2,1)S(1)} %get-tuple-element.1088), channel_id=1, source_target_pairs={{0,4},{4,8},{8,12},{12,16},{16,20},{20,24},{24,28},{1,5},{5,9},{9,... | collective-permute-start | bytes 393224 | tf_op jit(solution)/shard_map/while/body/eval_jaxpr/ppermute | solution.py:18
  24.9 8.6 %collective-permute-start = (bf16[256,256]{1,0:T(8,128)(2,1)S(1)}, bf16[256,256]{1,0:T(8,128)(2,1)S(1)}, u32[]{:S(2)}, u32[]{:S(2)}) collective-permute-start(bf16[256,256]{1,0:T(8,128)(2,1)S(1)} %get-tuple-element.1088), channel_id=1, source_target_pairs={{0,4},{4,8},{8,12},{12,16},{16,20},{20,24},{24,28},{1,5},{5,9},{9,... | collective-permute-start | bytes 393224 | tf_op jit(solution)/shard_map/while/body/eval_jaxpr/ppermute | solution.py:18
  34.8 8.6 %collective-permute-start = (bf16[256,256]{1,0:T(8,128)(2,1)S(1)}, bf16[256,256]{1,0:T(8,128)(2,1)S(1)}, u32[]{:S(2)}, u32[]{:S(2)}) collective-permute-start(bf16[256,256]{1,0:T(8,128)(2,1)S(1)} %get-tuple-element.1088), channel_id=1, source_target_pairs={{0,4},{4,8},{8,12},{12,16},{16,20},{20,24},{24,28},{1,5},{5,9},{9,... | collective-permute-start | bytes 393224 | tf_op jit(solution)/shard_map/while/body/eval_jaxpr/ppermute | solution.py:18
  44.7 8.6 %collective-permute-start = (bf16[256,256]{1,0:T(8,128)(2,1)S(1)}, bf16[256,256]{1,0:T(8,128)(2,1)S(1)}, u32[]{:S(2)}, u32[]{:S(2)}) collective-permute-start(bf16[256,256]{1,0:T(8,128)(2,1)S(1)} %get-tuple-element.1088), channel_id=1, source_target_pairs={{0,4},{4,8},{8,12},{12,16},{16,20},{20,24},{24,28},{1,5},{5,9},{9,... | collective-permute-start | bytes 393224 | tf_op jit(solution)/shard_map/while/body/eval_jaxpr/ppermute | solution.py:18
  69.4 10.2 %collective-permute-start.1 = (bf16[256,256]{1,0:T(8,128)(2,1)S(1)}, bf16[256,256]{1,0:T(8,128)(2,1)S(1)}, u32[]{:S(2)}, u32[]{:S(2)}) collective-permute-start(bf16[256,256]{1,0:T(8,128)(2,1)S(1)} %get-tuple-element.1144), channel_id=1, source_target_pairs={{0,4},{4,8},{8,12},{12,16},{16,20},{20,24},{24,28},{1,5},{5,9},{9,... | collective-permute-start | bytes 393224 | tf_op jit(solution)/shard_map/while/body/eval_jaxpr/ppermute | solution.py:18
  72.8 8.8 %collective-permute-start.2 = (bf16[256,256]{0,1:T(8,128)(2,1)S(1)}, bf16[256,256]{0,1:T(8,128)(2,1)S(1)}, u32[]{:S(2)}, u32[]{:S(2)}) collective-permute-start(bf16[256,256]{0,1:T(8,128)(2,1)S(1)} %get-tuple-element.1145), channel_id=1, source_target_pairs={{0,4},{4,8},{8,12},{12,16},{16,20},{20,24},{24,28},{28,0},{1,5},{5... | collective-permute-start | bytes 393224 | tf_op jit(solution)/shard_map/while/body/eval_jaxpr/ppermute | solution.py:23
  81.7 9.3 %collective-permute-start.1 = (bf16[256,256]{1,0:T(8,128)(2,1)S(1)}, bf16[256,256]{1,0:T(8,128)(2,1)S(1)}, u32[]{:S(2)}, u32[]{:S(2)}) collective-permute-start(bf16[256,256]{1,0:T(8,128)(2,1)S(1)} %get-tuple-element.1144), channel_id=1, source_target_pairs={{0,4},{4,8},{8,12},{12,16},{16,20},{20,24},{24,28},{1,5},{5,9},{9,... | collective-permute-start | bytes 393224 | tf_op jit(solution)/shard_map/while/body/eval_jaxpr/ppermute | solution.py:18
  85.1 7.9 %collective-permute-start.2 = (bf16[256,256]{0,1:T(8,128)(2,1)S(1)}, bf16[256,256]{0,1:T(8,128)(2,1)S(1)}, u32[]{:S(2)}, u32[]{:S(2)}) collective-permute-start(bf16[256,256]{0,1:T(8,128)(2,1)S(1)} %get-tuple-element.1145), channel_id=1, source_target_pairs={{0,4},{4,8},{8,12},{12,16},{16,20},{20,24},{24,28},{28,0},{1,5},{5... | collective-permute-start | bytes 393224 | tf_op jit(solution)/shard_map/while/body/eval_jaxpr/ppermute | solution.py:23
  93.0 8.5 %collective-permute-start.1 = (bf16[256,256]{1,0:T(8,128)(2,1)S(1)}, bf16[256,256]{1,0:T(8,128)(2,1)S(1)}, u32[]{:S(2)}, u32[]{:S(2)}) collective-permute-start(bf16[256,256]{1,0:T(8,128)(2,1)S(1)} %get-tuple-element.1144), channel_id=1, source_target_pairs={{0,4},{4,8},{8,12},{12,16},{16,20},{20,24},{24,28},{1,5},{5,9},{9,... | collective-permute-start | bytes 393224 | tf_op jit(solution)/shard_map/while/body/eval_jaxpr/ppermute | solution.py:18
  95.6 7.9 %collective-permute-start.2 = (bf16[256,256]{0,1:T(8,128)(2,1)S(1)}, bf16[256,256]{0,1:T(8,128)(2,1)S(1)}, u32[]{:S(2)}, u32[]{:S(2)}) collective-permute-start(bf16[256,256]{0,1:T(8,128)(2,1)S(1)} %get-tuple-element.1145), channel_id=1, source_target_pairs={{0,4},{4,8},{8,12},{12,16},{16,20},{20,24},{24,28},{28,0},{1,5},{5... | collective-permute-start | bytes 393224 | tf_op jit(solution)/shard_map/while/body/eval_jaxpr/ppermute | solution.py:23
  103.6 7.8 %collective-permute-start.1 = (bf16[256,256]{1,0:T(8,128)(2,1)S(1)}, bf16[256,256]{1,0:T(8,128)(2,1)S(1)}, u32[]{:S(2)}, u32[]{:S(2)}) collective-permute-start(bf16[256,256]{1,0:T(8,128)(2,1)S(1)} %get-tuple-element.1144), channel_id=1, source_target_pairs={{0,4},{4,8},{8,12},{12,16},{16,20},{20,24},{24,28},{1,5},{5,9},{9,... | collective-permute-start | bytes 393224 | tf_op jit(solution)/shard_map/while/body/eval_jaxpr/ppermute | solution.py:18
  105.5 7.8 %collective-permute-start.2 = (bf16[256,256]{0,1:T(8,128)(2,1)S(1)}, bf16[256,256]{0,1:T(8,128)(2,1)S(1)}, u32[]{:S(2)}, u32[]{:S(2)}) collective-permute-start(bf16[256,256]{0,1:T(8,128)(2,1)S(1)} %get-tuple-element.1145), channel_id=1, source_target_pairs={{0,4},{4,8},{8,12},{12,16},{16,20},{20,24},{24,28},{28,0},{1,5},{5... | collective-permute-start | bytes 393224 | tf_op jit(solution)/shard_map/while/body/eval_jaxpr/ppermute | solution.py:23
  113.5 7.8 %collective-permute-start.3 = (bf16[256,256]{1,0:T(8,128)(2,1)S(1)}, bf16[256,256]{1,0:T(8,128)(2,1)S(1)}, u32[]{:S(2)}, u32[]{:S(2)}) collective-permute-start(bf16[256,256]{1,0:T(8,128)(2,1)S(1)} %copy.51), channel_id=1, source_target_pairs={{0,16},{4,20},{8,24},{12,28},{16,0},{20,4},{24,8},{28,12},{1,17},{... | collective-permute-start | bytes 393224 | tf_op jit(solution)/shard_map/ppermute | solution.py:23
Sparse Core Ops, SparseCore 0:
  9.6 28.2 all-gather.1
  69.5 33.9 reduce-scatter.1
where the time goes:
time: 131 us; the launch traced here: 129 us
  starting transfers between devices  35 us (27%)
  matrix products  26.5 us (20%)
  other arithmetic  23.9 us (18%)
  local copies, waits for them, and re-layouts  20.1 us (15%)
  between operations  14.3 us (11%)
  loops' own time  6.28 us (5%)
  waiting for transfers between devices  2.64 us (2%)
    ppermute x8, starting transfers between devices, from_behind(): return lax.ppermute(array, axis, pairs)  26.5 us
    select_n x9, other arithmetic, doc_span(): return jnp.repeat(blocks, BLK, total_repeat_length=count)  21.1 us
    gather x17, local copies, waits for them, and re-layouts, doc_span(): return jnp.repeat(blocks, BLK, total_repeat_length=count)  10 us
    ppermute x5, starting transfers between devices, from_behind_2(): lax.ppermute(array, axis, [(i, (i + by) % devices) for i in range(devices)])  8.45 us
    dot_general x1, matrix products, on_device(): partial_out = jnp.dot(attn, out_weight, preferred_element_type=jnp.float32)  6.62 us
    dot_general x1, matrix products, on_device(): lax.dot_general(lax.all_gather(cotangent, 'tp', axis=1, tiled=True), out_...  5.89 us
    dynamic_slice x8, local copies, waits for them, and re-layouts, on_device(): lax.scan(forward_step, (key_value, state), steps_ahead)  4.68 us
    another operation x1, loops' own time, on_device(): lax.scan(carry_step, (key_value, own_grads, query_sum), steps_ahead)  3.16 us
  transfers between devices with their start and end apart: 15, of which 1 were waited for; matrix products, arithmetic and copies ran while one was open for 43% of the time, Pallas kernels for 0%

commit v1 on v0

v1 whole, which is shorter than its diff:
```python
import functools
import math

import jax
import jax.numpy as jnp
from jax import lax
from jax.experimental import pallas as pl
from jax.experimental.pallas import tpu as pltpu
from jax.sharding import PartitionSpec as P

HEAD_SIZE = 128
BLK = 128
SCALE = 1.0 / math.sqrt(HEAD_SIZE)
SCALE2 = SCALE * math.log2(math.e)
LOW = -1e30
HIGH = 1e30
VMEM_LIMIT = 48 * 1024 * 1024

VMEM = pl.BlockSpec(memory_space=pltpu.VMEM)
SMEM = pl.BlockSpec(memory_space=pltpu.SMEM)


def dot(a, b):
    return jnp.dot(a, b, preferred_element_type=jnp.float32)


def shift(array, axis, by):
    devices = lax.axis_size(axis)
    pairs = [(i, i + by) for i in range(devices) if 0 <= i + by < devices]
    return lax.ppermute(array, axis, pairs)


def swap(array, bit):
    return lax.ppermute(array, "tp", [(i, i ^ bit) for i in range(lax.axis_size("tp"))])


def block(i, n=1):
    return pl.ds(i * BLK, n * BLK)


def allowed(doc_ref, key_block, query_block):
    return (key_block >= 0) & (doc_ref[jnp.maximum(key_block, 0)] == doc_ref[query_block])


def causal(width):
    key = lax.broadcasted_iota(jnp.int32, (BLK, width), 0)
    query = lax.broadcasted_iota(jnp.int32, (BLK, width), 1) % BLK
    return key <= query


def forward_kernel(window, blocks, doc_ref, q_ref, *refs):
    kv_refs = refs[:-8]
    attn_ref, qt_ref, ot_ref, lse_ref, k_all, vt_all, s_all, p_all = refs[-8:]
    heads = q_ref.shape[1] // HEAD_SIZE
    first = lax.axis_index("ctx") * blocks
    at = 0
    for ref in kv_refs:
        rows = ref.shape[0]
        k_all[pl.ds(at, rows), :] = ref[:, :HEAD_SIZE]
        vt_all[:, pl.ds(at, rows)] = ref[:, HEAD_SIZE:].T
        at += rows
    for b in range(blocks):
        for h in range(heads):
            qt_ref[block(b), block(h)] = q_ref[block(b), block(h)].T
        qt = qt_ref[block(b), :]
        width = qt.shape[1]
        top = jnp.full((1, width), LOW, jnp.float32)
        ok = [allowed(doc_ref, first + b - (window - 1) + w, first + b) for w in range(window)]
        for w in range(window):
            s = dot(k_all[block(b + w), :], qt) * SCALE2
            if w == window - 1:
                s = jnp.where(causal(width), s, LOW)
            s_all[block(w), :] = s
            top = jnp.maximum(top, jnp.max(s, axis=0, keepdims=True) + jnp.where(ok[w], 0.0, LOW))
        total = jnp.zeros((1, width), jnp.float32)
        for w in range(window):
            p = jnp.exp2(s_all[block(w), :] - jnp.where(ok[w], top, HIGH))
            total += jnp.sum(p, axis=0, keepdims=True)
            p_all[block(w), :] = p.astype(jnp.bfloat16)
        out = dot(vt_all[:, block(b, window)], p_all[...]) / total
        ot_ref[block(b), :] = out.astype(jnp.bfloat16)
        lse_ref[pl.ds(b, 1), :] = top + jnp.log2(total)
        for h in range(heads):
            attn_ref[block(b), block(h)] = out[:, h * BLK:(h + 1) * BLK].T.astype(jnp.bfloat16)


def forward(doc_ids, q, kvs, window):
    rows, width = q.shape
    blocks = rows // BLK
    held = (window - 1 + blocks) * BLK
    return pl.pallas_call(
        functools.partial(forward_kernel, window, blocks),
        out_shape=[
            jax.ShapeDtypeStruct((rows, width), jnp.bfloat16),
            jax.ShapeDtypeStruct((rows, width), jnp.bfloat16),
            jax.ShapeDtypeStruct((rows, width), jnp.bfloat16),
            jax.ShapeDtypeStruct((blocks, width), jnp.float32),
        ],
        in_specs=[SMEM] + [VMEM] * (1 + len(kvs)),
        out_specs=[VMEM] * 4,
        scratch_shapes=[
            pltpu.VMEM((held, HEAD_SIZE), jnp.bfloat16),
            pltpu.VMEM((HEAD_SIZE, held), jnp.bfloat16),
            pltpu.VMEM((window * BLK, width), jnp.float32),
            pltpu.VMEM((window * BLK, width), jnp.bfloat16),
        ],
        compiler_params=pltpu.CompilerParams(vmem_limit_bytes=VMEM_LIMIT),
        cost_estimate=pl.CostEstimate(
            flops=4 * rows * width * window * BLK * 2, bytes_accessed=2 * 2**20, transcendentals=0
        ),
        name="forward",
    )(doc_ids, q, *kvs)


def backward_kernel(window, blocks, doc_ref, q_ref, qt_ref, ot_ref, lse_ref, g_ref, *refs):
    n = (len(refs) - 10) // 2
    kv_refs, dkv_refs = refs[:n], refs[n + 1:2 * n + 1]
    dq_ref = refs[n]
    k_all, kt_all, v_all, q_rows, g_rows, gt, p_all, ds_all, dk_all = refs[2 * n + 1:]
    heads = q_ref.shape[1] // HEAD_SIZE
    width = q_ref.shape[1]
    first = lax.axis_index("ctx") * blocks
    at = 0
    for ref in kv_refs:
        rows = ref.shape[0]
        k_all[pl.ds(at, rows), :] = ref[:, :HEAD_SIZE]
        kt_all[:, pl.ds(at, rows)] = ref[:, :HEAD_SIZE].T
        v_all[pl.ds(at, rows), :] = ref[:, HEAD_SIZE:]
        at += rows
    dk_all[...] = jnp.zeros_like(dk_all)
    for b in range(blocks):
        for h in range(heads):
            g = g_ref[block(b), block(h)]
            q_rows[block(h), :] = q_ref[block(b), block(h)]
            g_rows[block(h), :] = g
            gt[:, block(h)] = g.T
        qt = qt_ref[block(b), :]
        delta = jnp.sum(
            gt[...].astype(jnp.float32) * ot_ref[block(b), :].astype(jnp.float32),
            axis=0, keepdims=True,
        )
        lse = lse_ref[pl.ds(b, 1), :]
        for w in range(window):
            ok = allowed(doc_ref, first + b - (window - 1) + w, first + b)
            s = dot(k_all[block(b + w), :], qt) * SCALE2
            if w == window - 1:
                s = jnp.where(causal(width), s, LOW)
            p = jnp.exp2(s - jnp.where(ok, lse, HIGH))
            p_all[block(w), :] = p.astype(jnp.bfloat16)
            dp = dot(v_all[block(b + w), :], gt[...])
            ds_all[block(w), :] = (p * (dp - delta)).astype(jnp.bfloat16)
        dk_all[block(b, window), :HEAD_SIZE] += dot(ds_all[...], q_rows[...]) * SCALE
        dk_all[block(b, window), HEAD_SIZE:] += dot(p_all[...], g_rows[...])
        dqt = dot(kt_all[:, block(b, window)], ds_all[...]) * SCALE
        for h in range(heads):
            dq_ref[block(b), block(h)] = dqt[:, h * BLK:(h + 1) * BLK].T.astype(jnp.bfloat16)
    at = 0
    for ref in dkv_refs:
        rows = ref.shape[0]
        ref[...] = dk_all[pl.ds(at, rows), :].astype(ref.dtype)
        at += rows


def backward(doc_ids, q, qt, ot, lse, g, kvs, window):
    rows, width = q.shape
    blocks = rows // BLK
    held = (window - 1 + blocks) * BLK
    types = [jnp.bfloat16] * (len(kvs) - 1) + [jnp.float32]
    return pl.pallas_call(
        functools.partial(backward_kernel, window, blocks),
        out_shape=[jax.ShapeDtypeStruct((rows, width), jnp.bfloat16)]
        + [jax.ShapeDtypeStruct(kv.shape, t) for kv, t in zip(kvs, types)],
        in_specs=[SMEM] + [VMEM] * (5 + len(kvs)),
        out_specs=[VMEM] * (1 + len(kvs)),
        scratch_shapes=[
            pltpu.VMEM((held, HEAD_SIZE), jnp.bfloat16),
            pltpu.VMEM((HEAD_SIZE, held), jnp.bfloat16),
            pltpu.VMEM((held, HEAD_SIZE), jnp.bfloat16),
            pltpu.VMEM((width, HEAD_SIZE), jnp.bfloat16),
            pltpu.VMEM((width, HEAD_SIZE), jnp.bfloat16),
            pltpu.VMEM((HEAD_SIZE, width), jnp.bfloat16),
            pltpu.VMEM((window * BLK, width), jnp.bfloat16),
            pltpu.VMEM((window * BLK, width), jnp.bfloat16),
            pltpu.VMEM((held, 2 * HEAD_SIZE), jnp.float32),
        ],
        compiler_params=pltpu.CompilerParams(vmem_limit_bytes=VMEM_LIMIT),
        cost_estimate=pl.CostEstimate(
            flops=10 * rows * width * window * BLK * 2, bytes_accessed=4 * 2**20, transcendentals=0
        ),
        name="backward",
    )(doc_ids, q, qt, ot, lse, g, *kvs)


def features_in_kernel(ids_ref, *refs):
    *cots, w_ref, out_ref, total = refs
    step = pl.program_id(0)
    base = None
    if len(cots) == 3:
        base, cots = cots[2], cots[:2]

    @pl.when(step == 0)
    def _():
        part = lax.dot_general(
            cots[0][...], w_ref[...], (((1,), (1,)), ((), ())), preferred_element_type=jnp.float32
        )
        total[...] = part if base is None else part + base[...]

    @pl.when(step == 1)
    def _():
        out_ref[...] = (
            total[...]
            + lax.dot_general(
                cots[1][...], w_ref[...], (((1,), (1,)), ((), ())),
                preferred_element_type=jnp.float32,
            )
        ).astype(out_ref.dtype)


def features_in(ids, cots, weight, base, dtype):
    rows, part = cots[0].shape
    depth = weight.shape[0]
    extra = [] if base is None else [base]
    whole = lambda j, ids: (0, 0)
    return pl.pallas_call(
        features_in_kernel,
        out_shape=jax.ShapeDtypeStruct((rows, depth), dtype),
        grid_spec=pltpu.PrefetchScalarGridSpec(
            num_scalar_prefetch=1,
            grid=(2,),
            in_specs=[pl.BlockSpec((rows, part), whole)] * 2
            + [pl.BlockSpec((rows, depth), whole)] * len(extra)
            + [pl.BlockSpec((depth, part), lambda j, ids: (0, ids[j]))],
            out_specs=pl.BlockSpec((rows, depth), whole),
            scratch_shapes=[pltpu.VMEM((rows, depth), jnp.float32)],
        ),
        compiler_params=pltpu.CompilerParams(vmem_limit_bytes=VMEM_LIMIT),
        cost_estimate=pl.CostEstimate(
            flops=4 * rows * part * depth, bytes_accessed=5 * 2**20, transcendentals=0
        ),
        name="features_in",
    )(ids, *cots, *extra, weight)


def features_out_kernel(ids_ref, attn_ref, *refs):
    *extra, w_ref, out_ref = refs
    total = dot(attn_ref[...], w_ref[...])
    for ref in extra:
        total = total + ref[...].astype(jnp.float32)
    out_ref[...] = total.astype(out_ref.dtype)


def features_out(ids, which, attn, weight, part, extra=(), dtype=jnp.bfloat16):
    rows, depth = attn.shape
    tiles = 2
    tile = part // tiles
    return pl.pallas_call(
        features_out_kernel,
        out_shape=jax.ShapeDtypeStruct((rows, part), dtype),
        grid_spec=pltpu.PrefetchScalarGridSpec(
            num_scalar_prefetch=1,
            grid=(tiles,),
            in_specs=[pl.BlockSpec((rows, depth), lambda j, ids: (0, 0))]
            + [pl.BlockSpec((rows, tile), lambda j, ids: (0, j))] * len(extra)
            + [pl.BlockSpec((depth, tile), lambda j, ids: (0, ids[which] * tiles + j))],
            out_specs=pl.BlockSpec((rows, tile), lambda j, ids: (0, j)),
        ),
        compiler_params=pltpu.CompilerParams(vmem_limit_bytes=VMEM_LIMIT),
        cost_estimate=pl.CostEstimate(
            flops=2 * rows * part * depth, bytes_accessed=3 * 2**20, transcendentals=0
        ),
        name="features_out",
    )(ids, attn, *extra, weight)


def on_device(queries, keys, values, out_weight, cotangent, doc_ids):
    rows = queries.shape[0]
    part = cotangent.shape[1]
    ctx_count = lax.axis_size("ctx")
    blocks = rows // BLK
    window = min(8 * blocks, blocks * ctx_count // 2)
    needs = []
    left = window - 1
    while left > 0:
        needs.append(min(left, blocks))
        left -= needs[-1]
    me = lax.axis_index("tp")
    ids = jnp.stack([me, me ^ 1, me ^ 2, me ^ 3]).astype(jnp.int32)

    cot_y = swap(cotangent, 2)
    key_value = jnp.concatenate([keys, values], axis=1)
    kvs = [shift(key_value[rows - n * BLK:], "ctx", s + 1) for s, n in enumerate(needs)]
    kvs = kvs[::-1] + [key_value]
    cot_c = swap(cotangent, 1)
    near = features_in(ids[:2], [cotangent, cot_c], out_weight, None, jnp.float32)
    attn, qt, ot, lse = forward(doc_ids, queries, kvs, window)
    out_a = features_out(ids, 3, attn, out_weight, part)
    out_b = features_out(ids, 2, attn, out_weight, part, [swap(out_a, 1)])
    from_y = swap(out_b, 2)
    out_c = features_out(ids, 1, attn, out_weight, part)
    out_d = features_out(ids, 0, attn, out_weight, part, [swap(out_c, 1)], jnp.float32)

    grad_attn = features_in(ids[2:], [cot_y, swap(cot_y, 1)], out_weight, near, jnp.bfloat16)
    dq, *dkvs = backward(doc_ids, queries, qt, ot, lse, grad_attn, kvs, window)
    own = dkvs[-1]
    for s, (n, dkv) in enumerate(zip(needs, dkvs[-2::-1])):
        back = shift(dkv, "ctx", -(s + 1)).astype(jnp.float32)
        if n < blocks:
            back = jnp.pad(back, ((rows - n * BLK, 0), (0, 0)))
        own = own + back
    mixed = (out_d + from_y.astype(jnp.float32)).astype(jnp.bfloat16)
    return (
        mixed,
        dq,
        own[:, :HEAD_SIZE].astype(jnp.bfloat16),
        own[:, HEAD_SIZE:].astype(jnp.bfloat16),
    )


def solution(mesh):
    return jax.shard_map(
        on_device,
        mesh=mesh,
        in_specs=(
            P("ctx", "tp"),
            P("ctx", "tp"),
            P("ctx", "tp"),
            P("tp", None),
            P("ctx", "tp"),
            P(),
        ),
        out_specs=(P("ctx", "tp"), P("ctx", "tp"), P("ctx", "tp"), P("ctx", "tp")),
        check_vma=False,
    )
```

time: 131 us -> 72.4 us (0.55); the launches traced: 129 us -> 71.9 us
  matrix products: 26.5 us -> 0 us
  Pallas kernels: 0 us -> 25.9 us
  other arithmetic: 23.9 us -> 1.3 us
  local copies, waits for them, and re-layouts: 20.1 us -> 4 us
  waiting for transfers between devices: 2.64 us -> 16.8 us
  between operations: 14.3 us -> 0.82 us
  starting transfers between devices: 35 us -> 23.2 us
  loops' own time: 6.28 us -> 0 us
    dot_general x36 -> x0, matrix products: 26.5 us -> none  [the longest x1 6.62 us: on_device(): partial_out = jnp.dot(attn, out_weight, preferred_element_type=jnp.float32)]
    pallas_call x0 -> x8, Pallas kernels: none -> 25.9 us  [the longest x4 10.9 us: features_out(): pl.pallas_call(features_out_kernel, out_shape=jax.ShapeDtypeStruct((rows,...]
    select_n x9 -> x0, other arithmetic: 21.1 us -> none  [doc_span(): return jnp.repeat(blocks, BLK, total_repeat_length=count)]
    ppermute x13 -> x14, waiting for transfers between devices: 1.92 us -> 16.8 us  [the longest x8 16.7 us: shift(): return lax.ppermute(array, axis, pairs)]
    ppermute x13 -> x14, starting transfers between devices: 34.9 us -> 23.2 us  [the longest x8 18.5 us: shift(): return lax.ppermute(array, axis, pairs)]
    gather x17 -> x0, local copies, waits for them, and re-layouts: 10 us -> none  [doc_span(): return jnp.repeat(blocks, BLK, total_repeat_length=count)]
    another operation x2 -> x0, loops' own time: 6.28 us -> none  [the longest x1 3.16 us: on_device(): lax.scan(carry_step, (key_value, own_grads, query_sum), steps_ahead)]
    dynamic_slice x17 -> x0, local copies, waits for them, and re-layouts: 6.03 us -> none  [the longest x8 4.68 us: on_device(): lax.scan(forward_step, (key_value, state), steps_ahead)]
  transfers between devices with their start and end apart: 15 -> 14, of which waited for: 1 -> 2; matrix products, arithmetic and copies ran while one was open for 43% -> 4% of each run, Pallas kernels for 0% -> 36%
where the time goes in v1:
time: 72.4 us; the launch traced here: 71.9 us
  Pallas kernels  25.9 us (36%)
  starting transfers between devices  23.2 us (32%)
  waiting for transfers between devices  16.8 us (23%)
  local copies, waits for them, and re-layouts  4 us (6%)
  other arithmetic  1.3 us (2%)
  between operations  0.82 us (1%)
    ppermute x8, starting transfers between devices, shift(): return lax.ppermute(array, axis, pairs)  18.5 us
    ppermute x8, waiting for transfers between devices, shift(): return lax.ppermute(array, axis, pairs)  16.7 us
    pallas_call x4, Pallas kernels, features_out(): pl.pallas_call(features_out_kernel, out_shape=jax.ShapeDtypeStruct((rows,...  10.9 us
    pallas_call x2, Pallas kernels, features_in(): pl.pallas_call(features_in_kernel, out_shape=jax.ShapeDtypeStruct((rows,...  6.93 us
    pallas_call x1, Pallas kernels, backward(): pl.pallas_call(functools.partial(backward_kernel, window, blocks), out_sh...  4.85 us
    ppermute x6, starting transfers between devices, swap(): lax.ppermute(array, 'tp', [(i, i ^ bit) for i in range(lax.axis_size('tp'...  4.72 us
    pallas_call x1, Pallas kernels, forward(): pl.pallas_call(functools.partial(forward_kernel, window, blocks), out_sha...  3.22 us
    unnamed x7, local copies, waits for them, and re-layouts  2.48 us
  transfers between devices with their start and end apart: 14, of which 2 were waited for; matrix products, arithmetic and copies ran while one was open for 4% of the time, Pallas kernels for 36%

profile of v1, /device:TPU:0, one launch (start us, length us, event | category | flops | bytes accessed | tf_op | source)
XLA Modules:
  0.0 71.9 jit_solution(10330406762023155877)
XLA Ops:
  0.6 3.0 %collective-permute-start.7 = (bf16[256,1280]{1,0:T(8,128)(2,1)}, bf16[256,1280]{1,0:T(8,128)(2,1)S(1)}, u32[]{:S(2)}, u32[]{:S(2)}) collective-permute-start(bf16[256,1280]{1,0:T(8,128)(2,1)} %refs_0_.5), channel_id=1, source_target_pairs={{0,2},{1,3},{2,0},{3,1},{4,6},{5,7},{6,4},{7,5},{8,10},{9,11},{10,... | collective-permute-start | bytes 1966088 | tf_op jit(solution)/shard_map/ppermute | solution.py:34
  3.7 0.9 %constant_dynamic-update-slice_fusion.1 = bf16[256,256]{1,0:T(8,128)(2,1)S(1)} fusion(bf16[256,128]{1,0:T(8,128)(2,1)} %param.7), kind=kLoop, calls=%fused_computation.3 | loop fusion | bytes 131072
  4.5 0.9 %constant_dynamic-update-slice_fusion.refs_4_ = bf16[256,256]{1,0:T(8,128)(2,1)S(1)} fusion(bf16[256,256]{1,0:T(8,128)(2,1)S(1)} %constant_dynamic-update-slice_fusion.1, bf16[256,128]{1,0:T(8,128)(2,1)} %param.8), kind=kLoop, calls=%fused_computation.2 | loop fusion | bytes 131072 | tf_op jit(solution)/shard_map/concatenate | solution.py:290
  5.4 3.4 %collective-permute-start.3 = (bf16[256,256]{1,0:T(8,128)(2,1)S(1)}, bf16[256,256]{1,0:T(8,128)(2,1)S(1)}, u32[]{:S(2)}, u32[]{:S(2)}) collective-permute-start(bf16[256,256]{1,0:T(8,128)(2,1)S(1)} %constant_dynamic-update-slice_fusion.refs_4_), channel_id=1, source_target_pairs={{0,4},{4,8},{8,12},{12,16},{16,20},{20,24},{24,28},{1,5},{5,9},{9,... | collective-permute-start | bytes 393224 | tf_op jit(solution)/shard_map/ppermute | solution.py:30
  8.8 3.5 %collective-permute-start.2 = (bf16[256,256]{1,0:T(8,128)(2,1)S(1)}, bf16[256,256]{1,0:T(8,128)(2,1)S(1)}, u32[]{:S(2)}, u32[]{:S(2)}) collective-permute-start(bf16[256,256]{1,0:T(8,128)(2,1)S(1)} %constant_dynamic-update-slice_fusion.refs_4_), channel_id=1, source_target_pairs={{0,8},{4,12},{8,16},{12,20},{16,24},{20,28},{1,9},{5,13},{9,17},{1... | collective-permute-start | bytes 393224 | tf_op jit(solution)/shard_map/ppermute | solution.py:30
  12.3 4.5 %collective-permute-start.1 = (bf16[256,256]{1,0:T(8,128)(2,1)S(1)}, bf16[256,256]{1,0:T(8,128)(2,1)S(1)}, u32[]{:S(2)}, u32[]{:S(2)}) collective-permute-start(bf16[256,256]{1,0:T(8,128)(2,1)S(1)} %constant_dynamic-update-slice_fusion.refs_4_), channel_id=1, source_target_pairs={{0,12},{4,16},{8,20},{12,24},{16,28},{1,13},{5,17},{9,21},{13,25},... | collective-permute-start | bytes 393224 | tf_op jit(solution)/shard_map/ppermute | solution.py:30
  16.8 1.9 %collective-permute-start = (bf16[128,256]{1,0:T(8,128)(2,1)S(1)}, bf16[128,256]{1,0:T(8,128)(2,1)S(1)}, u32[]{:S(2)}, u32[]{:S(2)}) collective-permute-start(bf16[128,256]{1,0:T(8,128)(2,1)S(1)} %slice.18), channel_id=1, source_target_pairs={{0,16},{4,20},{8,24},{12,28},{1,17},{5,21},{9,25},{13,29},{2,18},{... | collective-permute-start | bytes 196616 | tf_op jit(solution)/shard_map/ppermute | solution.py:30
  18.7 0.1 pad_add_fusion.ids_ref
  18.8 1.8 %collective-permute-done.refs_0_ = bf16[128,256]{1,0:T(8,128)(2,1)S(1)} collective-permute-done((bf16[128,256]{1,0:T(8,128)(2,1)S(1)}, bf16[128,256]{1,0:T(8,128)(2,1)S(1)}, u32[]{:S(2)}, u32[]{:S(2)}) %collective-permute-start) | collective-permute-done | bytes 65568 | tf_op jit(solution)/shard_map/ppermute | solution.py:30
  20.6 0.0 collective-permute-start.9
  20.6 0.0 collective-permute-done.3.refs_3_
  20.6 0.0 collective-permute-done.2.refs_2_
  20.6 0.0 collective-permute-done.1.refs_1_
  20.6 0.0 copy-start.1
  20.7 1.0 %copy-done.1 = bf16[256,640]{1,0:T(8,128)(2,1)S(1)} copy-done((bf16[256,640]{1,0:T(8,128)(2,1)S(1)}, bf16[256,640]{1,0:T(8,128)(2,1)}, u32[]{:S(2)}) %copy-start.1) | copy-done | bytes 327704
  21.6 0.0 copy-start.2
  21.6 0.7 copy-done.2
  22.3 3.2 %forward.1 = (bf16[256,640]{1,0:T(8,128)(2,1)S(1)}, bf16[256,640]{1,0:T(8,128)(2,1)S(1)}, bf16[256,640]{1,0:T(8,128)(2,1)S(1)}, f32[2,640]{1,0:T(2,128)S(1)}) custom-call(s32[16]{0:T(128)S(1)} %copy-done.2, bf16[256,640]{1,0:T(8,128)(2,1)S(1)} %copy-done.1, bf16[128,256]{1,0:T(8,128)(2,1)S(1)} %collective-permute-done.refs_0_, ...), custom_call_target="tpu_custom_call" | custom-call | flops 1342177280 | bytes 2097152 | tf_op jit(solution)/shard_map/forward/pallas_call | solution.py:91
  25.5 2.7 %features_out.6 = bf16[256,1280]{1,0:T(8,128)(2,1)S(1)} custom-call(s32[4]{0:T(128)S(1)} %pad_add_fusion.ids_ref, bf16[256,640]{1,0:T(8,128)(2,1)S(1)} %get-tuple-element.14.attn_ref, bf16[640,5120]{1,0:T(8,128)(2,1)} %refs_3_.1), custom_call_target="tpu_custom_call" | custom-call | flops 419430400 | bytes 3145728 | tf_op jit(solution)/shard_map/features_out/pallas_call | solution.py:256
  28.2 0.6 collective-permute-start.5
  28.8 0.0 collective-permute-done.7.refs_0_
  28.8 0.1 collective-permute-start.8
  28.9 0.1 pad_add_fusion.2.ids_ref
  28.9 0.0 copy-start
  28.9 2.7 %features_out.4 = bf16[256,1280]{1,0:T(8,128)(2,1)S(1)} custom-call(s32[4]{0:T(128)S(1)} %pad_add_fusion.ids_ref, bf16[256,640]{1,0:T(8,128)(2,1)S(1)} %get-tuple-element.14.attn_ref, bf16[640,5120]{1,0:T(8,128)(2,1)} %refs_3_.1), custom_call_target="tpu_custom_call" | custom-call | flops 419430400 | bytes 3145728 | tf_op jit(solution)/shard_map/features_out/pallas_call | solution.py:256
  31.6 0.5 collective-permute-start.4
  32.1 0.1 pad_add_fusion.1.ids_ref
  32.2 0.0 collective-permute-done.9.refs_1_
  32.2 0.0 copy-done
  32.2 3.5 %features_in.2.refs_2_ = f32[256,640]{1,0:T(8,128)S(1)} custom-call(s32[2]{0:T(128)S(1)} %pad_add_fusion.2.ids_ref, bf16[256,1280]{1,0:T(8,128)(2,1)S(1)} %copy-done, bf16[256,1280]{1,0:T(8,128)(2,1)S(1)} %collective-permute-done.9.refs_1_, bf16[640,5120]{1,0:T(8,128)(2,1)} %refs_3_.1), custom_call_target="tpu_custom_call" | custom-call | flops 838860800 | bytes 5242880 | tf_op jit(solution)/shard_map/features_in/pallas_call | solution.py:224
  35.7 0.0 collective-permute-done.5.refs_0_
  35.7 2.7 %features_out.7 = bf16[256,1280]{1,0:T(8,128)(2,1)S(1)} custom-call(s32[4]{0:T(128)S(1)} %pad_add_fusion.ids_ref, bf16[256,640]{1,0:T(8,128)(2,1)S(1)} %get-tuple-element.14.attn_ref, bf16[256,1280]{1,0:T(8,128)(2,1)S(1)} %collective-permute-done.5.refs_0_, bf16[640,5120]{1,0:T(8,128)(2,1)} %refs_3_.1), custom_call_target="tpu_custom_call" | custom-call | flops 419430400 | bytes 3145728 | tf_op jit(solution)/shard_map/features_out/pallas_call | solution.py:256
  38.4 0.5 collective-permute-start.6
  39.0 0.0 collective-permute-done.8.refs_1_
  39.0 3.5 %features_in.3.g_ref = bf16[256,640]{1,0:T(8,128)(2,1)S(1)} custom-call(s32[2]{0:T(128)S(1)} %pad_add_fusion.1.ids_ref, bf16[256,1280]{1,0:T(8,128)(2,1)S(1)} %collective-permute-done.7.refs_0_, bf16[256,1280]{1,0:T(8,128)(2,1)S(1)} %collective-permute-done.8.refs_1_, f32[256,640]{1,0:T(8,128)S(1)} %features_in.2.refs_2_, bf16[640,5120]{1,0:T(8,128)(2,1)} %refs_3_.1), custom_call_target="tpu_custom_call" | custom-call | flops 838860800 | bytes 5242880 | tf_op jit(solution)/shard_map/features_in/pallas_call | solution.py:224
  42.4 4.8 %backward.1 = (bf16[256,640]{1,0:T(8,128)(2,1)}, bf16[128,256]{1,0:T(8,128)(2,1)S(1)}, bf16[256,256]{1,0:T(8,128)(2,1)S(1)}, bf16[256,256]{1,0:T(8,128)(2,1)S(1)...) custom-call(s32[16]{0:T(128)S(1)} %copy-done.2, bf16[256,640]{1,0:T(8,128)(2,1)S(1)} %copy-done.1, ...), custom_call_target="tpu_custom_call" | custom-call | flops 3355443200 | bytes 4194304 | tf_op jit(solution)/shard_map/backward/pallas_call | solution.py:169
  47.3 1.3 %collective-permute-start.10 = (bf16[256,256]{1,0:T(8,128)(2,1)S(1)}, bf16[256,256]{1,0:T(8,128)(2,1)S(1)}, u32[]{:S(2)}, u32[]{:S(2)}) collective-permute-start(bf16[256,256]{1,0:T(8,128)(2,1)S(1)} %get-tuple-element.20), channel_id=1, source_target_pairs={{4,0},{8,4},{12,8},{16,12},{20,16},{24,20},{28,24},{5,1},{9,5},{13... | collective-permute-start | bytes 393224 | tf_op jit(solution)/shard_map/ppermute | solution.py:30
  48.6 1.3 %collective-permute-start.11 = (bf16[256,256]{1,0:T(8,128)(2,1)S(1)}, bf16[256,256]{1,0:T(8,128)(2,1)S(1)}, u32[]{:S(2)}, u32[]{:S(2)}) collective-permute-start(bf16[256,256]{1,0:T(8,128)(2,1)S(1)} %get-tuple-element.21), channel_id=1, source_target_pairs={{8,0},{12,4},{16,8},{20,12},{24,16},{28,20},{9,1},{13,5},{17,9},{2... | collective-permute-start | bytes 393224 | tf_op jit(solution)/shard_map/ppermute | solution.py:30
  49.9 1.3 %collective-permute-start.12 = (bf16[256,256]{1,0:T(8,128)(2,1)S(1)}, bf16[256,256]{1,0:T(8,128)(2,1)S(1)}, u32[]{:S(2)}, u32[]{:S(2)}) collective-permute-start(bf16[256,256]{1,0:T(8,128)(2,1)S(1)} %get-tuple-element.22), channel_id=1, source_target_pairs={{12,0},{16,4},{20,8},{24,12},{28,16},{13,1},{17,5},{21,9},{25,13},... | collective-permute-start | bytes 393224 | tf_op jit(solution)/shard_map/ppermute | solution.py:30
  51.2 0.0 collective-permute-done.4.refs_0_
  51.2 1.3 %collective-permute-start.13 = (bf16[128,256]{1,0:T(8,128)(2,1)S(1)}, bf16[128,256]{1,0:T(8,128)(2,1)S(1)}, u32[]{:S(2)}, u32[]{:S(2)}) collective-permute-start(bf16[128,256]{1,0:T(8,128)(2,1)S(1)} %get-tuple-element.23), channel_id=1, source_target_pairs={{16,0},{20,4},{24,8},{28,12},{17,1},{21,5},{25,9},{29,13},{18,2},{... | collective-permute-start | bytes 196616 | tf_op jit(solution)/shard_map/ppermute | solution.py:30
  52.5 2.8 %features_out.5 = f32[256,1280]{1,0:T(8,128)S(1)} custom-call(s32[4]{0:T(128)S(1)} %pad_add_fusion.ids_ref, bf16[256,640]{1,0:T(8,128)(2,1)S(1)} %get-tuple-element.14.attn_ref, bf16[256,1280]{1,0:T(8,128)(2,1)S(1)} %collective-permute-done.4.refs_0_, bf16[640,5120]{1,0:T(8,128)(2,1)} %refs_3_.1), custom_call_target="tpu_custom_call" | custom-call | flops 419430400 | bytes 3145728 | tf_op jit(solution)/shard_map/features_out/pallas_call | solution.py:256
  55.3 14.9 %collective-permute-done.13 = bf16[128,256]{1,0:T(8,128)(2,1)S(1)} collective-permute-done((bf16[128,256]{1,0:T(8,128)(2,1)S(1)}, bf16[128,256]{1,0:T(8,128)(2,1)S(1)}, u32[]{:S(2)}, u32[]{:S(2)}) %collective-permute-start.13) | collective-permute-done | bytes 65568 | tf_op jit(solution)/shard_map/ppermute | solution.py:30
  70.2 0.0 collective-permute-done.10
  70.2 0.0 collective-permute-done.11
  70.2 0.0 collective-permute-done.12
  70.2 0.1 add_convert_fusion.1
  70.3 0.7 fusion
  70.9 0.0 collective-permute-done.6
  70.9 1.0 %add_convert_fusion = bf16[256,1280]{1,0:T(8,128)(2,1)} fusion(f32[256,1280]{1,0:T(8,128)S(1)} %features_out.5, bf16[256,1280]{1,0:T(8,128)(2,1)S(1)} %collective-permute-done.6), kind=kLoop, calls=%fused_computation | loop fusion | flops 983040 | bytes 2621440 | tf_op jit(solution)/shard_map/convert_element_type | solution.py:310
  (1 shorter events, 0.0 us)
Async XLA Ops:
  0.6 28.1 %collective-permute-start.7 = (bf16[256,1280]{1,0:T(8,128)(2,1)}, bf16[256,1280]{1,0:T(8,128)(2,1)S(1)}, u32[]{:S(2)}, u32[]{:S(2)}) collective-permute-start(bf16[256,1280]{1,0:T(8,128)(2,1)} %refs_0_.5), channel_id=1, source_target_pairs={{0,2},{1,3},{2,0},{3,1},{4,6},{5,7},{6,4},{7,5},{8,10},{9,11},{10,... | collective-permute-start | bytes 1966088 | tf_op jit(solution)/shard_map/ppermute | solution.py:34
  5.4 15.2 %collective-permute-start.3 = (bf16[256,256]{1,0:T(8,128)(2,1)S(1)}, bf16[256,256]{1,0:T(8,128)(2,1)S(1)}, u32[]{:S(2)}, u32[]{:S(2)}) collective-permute-start(bf16[256,256]{1,0:T(8,128)(2,1)S(1)} %constant_dynamic-update-slice_fusion.refs_4_), channel_id=1, source_target_pairs={{0,4},{4,8},{8,12},{12,16},{16,20},{20,24},{24,28},{1,5},{5,9},{9,... | collective-permute-start | bytes 393224 | tf_op jit(solution)/shard_map/ppermute | solution.py:30
  8.8 11.8 %collective-permute-start.2 = (bf16[256,256]{1,0:T(8,128)(2,1)S(1)}, bf16[256,256]{1,0:T(8,128)(2,1)S(1)}, u32[]{:S(2)}, u32[]{:S(2)}) collective-permute-start(bf16[256,256]{1,0:T(8,128)(2,1)S(1)} %constant_dynamic-update-slice_fusion.refs_4_), channel_id=1, source_target_pairs={{0,8},{4,12},{8,16},{12,20},{16,24},{20,28},{1,9},{5,13},{9,17},{1... | collective-permute-start | bytes 393224 | tf_op jit(solution)/shard_map/ppermute | solution.py:30
  12.3 8.4 %collective-permute-start.1 = (bf16[256,256]{1,0:T(8,128)(2,1)S(1)}, bf16[256,256]{1,0:T(8,128)(2,1)S(1)}, u32[]{:S(2)}, u32[]{:S(2)}) collective-permute-start(bf16[256,256]{1,0:T(8,128)(2,1)S(1)} %constant_dynamic-update-slice_fusion.refs_4_), channel_id=1, source_target_pairs={{0,12},{4,16},{8,20},{12,24},{16,28},{1,13},{5,17},{9,21},{13,25},... | collective-permute-start | bytes 393224 | tf_op jit(solution)/shard_map/ppermute | solution.py:30
  16.8 3.8 %collective-permute-start = (bf16[128,256]{1,0:T(8,128)(2,1)S(1)}, bf16[128,256]{1,0:T(8,128)(2,1)S(1)}, u32[]{:S(2)}, u32[]{:S(2)}) collective-permute-start(bf16[128,256]{1,0:T(8,128)(2,1)S(1)} %slice.18), channel_id=1, source_target_pairs={{0,16},{4,20},{8,24},{12,28},{1,17},{5,21},{9,25},{13,29},{2,18},{... | collective-permute-start | bytes 196616 | tf_op jit(solution)/shard_map/ppermute | solution.py:30
  20.6 11.6 %collective-permute-start.9 = (bf16[256,1280]{1,0:T(8,128)(2,1)}, bf16[256,1280]{1,0:T(8,128)(2,1)S(1)}, u32[]{:S(2)}, u32[]{:S(2)}) collective-permute-start(bf16[256,1280]{1,0:T(8,128)(2,1)} %refs_0_.5), channel_id=1, source_target_pairs={{0,1},{1,0},{2,3},{3,2},{4,5},{5,4},{6,7},{7,6},{8,9},{9,8},{10,11... | collective-permute-start | bytes 1966088 | tf_op jit(solution)/shard_map/ppermute | solution.py:34
  20.6 1.0 %copy-start.1 = (bf16[256,640]{1,0:T(8,128)(2,1)S(1)}, bf16[256,640]{1,0:T(8,128)(2,1)}, u32[]{:S(2)}) copy-start(bf16[256,640]{1,0:T(8,128)(2,1)} %q_ref.3) | copy-start | bytes 983044
  21.6 0.7 copy-start.2
  28.2 7.5 %collective-permute-start.5 = (bf16[256,1280]{1,0:T(8,128)(2,1)S(1)}, bf16[256,1280]{1,0:T(8,128)(2,1)S(1)}, u32[]{:S(2)}, u32[]{:S(2)}) collective-permute-start(bf16[256,1280]{1,0:T(8,128)(2,1)S(1)} %features_out.6), channel_id=1, source_target_pairs={{0,1},{1,0},{2,3},{3,2},{4,5},{5,4},{6,7},{7,6},{8,9},{9,8},{10,11... | collective-permute-start | bytes 1966088 | tf_op jit(solution)/shard_map/ppermute | solution.py:34
  28.8 10.2 %collective-permute-start.8 = (bf16[256,1280]{1,0:T(8,128)(2,1)S(1)}, bf16[256,1280]{1,0:T(8,128)(2,1)S(1)}, u32[]{:S(2)}, u32[]{:S(2)}) collective-permute-start(bf16[256,1280]{1,0:T(8,128)(2,1)S(1)} %collective-permute-done.7.refs_0_), channel_id=1, source_target_pairs={{0,1},{1,0},{2,3},{3,2},{4,5},{5,4},{6,7},{7,6},{8,9},{9,8},{10,11... | collective-permute-start | bytes 1966088 | tf_op jit(solution)/shard_map/ppermute | solution.py:34
  28.9 3.3 %copy-start = (bf16[256,1280]{1,0:T(8,128)(2,1)S(1)}, bf16[256,1280]{1,0:T(8,128)(2,1)}, u32[]{:S(2)}) copy-start(bf16[256,1280]{1,0:T(8,128)(2,1)} %refs_0_.5) | copy-start | bytes 1966084
  31.6 19.5 %collective-permute-start.4 = (bf16[256,1280]{1,0:T(8,128)(2,1)S(1)}, bf16[256,1280]{1,0:T(8,128)(2,1)S(1)}, u32[]{:S(2)}, u32[]{:S(2)}) collective-permute-start(bf16[256,1280]{1,0:T(8,128)(2,1)S(1)} %features_out.4), channel_id=1, source_target_pairs={{0,1},{1,0},{2,3},{3,2},{4,5},{5,4},{6,7},{7,6},{8,9},{9,8},{10,11... | collective-permute-start | bytes 1966088 | tf_op jit(solution)/shard_map/ppermute | solution.py:34
  38.4 32.5 %collective-permute-start.6 = (bf16[256,1280]{1,0:T(8,128)(2,1)S(1)}, bf16[256,1280]{1,0:T(8,128)(2,1)S(1)}, u32[]{:S(2)}, u32[]{:S(2)}) collective-permute-start(bf16[256,1280]{1,0:T(8,128)(2,1)S(1)} %features_out.7), channel_id=1, source_target_pairs={{0,2},{1,3},{2,0},{3,1},{4,6},{5,7},{6,4},{7,5},{8,10},{9,11},{10,... | collective-permute-start | bytes 1966088 | tf_op jit(solution)/shard_map/ppermute | solution.py:34
  47.3 22.9 %collective-permute-start.10 = (bf16[256,256]{1,0:T(8,128)(2,1)S(1)}, bf16[256,256]{1,0:T(8,128)(2,1)S(1)}, u32[]{:S(2)}, u32[]{:S(2)}) collective-permute-start(bf16[256,256]{1,0:T(8,128)(2,1)S(1)} %get-tuple-element.20), channel_id=1, source_target_pairs={{4,0},{8,4},{12,8},{16,12},{20,16},{24,20},{28,24},{5,1},{9,5},{13... | collective-permute-start | bytes 393224 | tf_op jit(solution)/shard_map/ppermute | solution.py:30
  48.6 21.6 %collective-permute-start.11 = (bf16[256,256]{1,0:T(8,128)(2,1)S(1)}, bf16[256,256]{1,0:T(8,128)(2,1)S(1)}, u32[]{:S(2)}, u32[]{:S(2)}) collective-permute-start(bf16[256,256]{1,0:T(8,128)(2,1)S(1)} %get-tuple-element.21), channel_id=1, source_target_pairs={{8,0},{12,4},{16,8},{20,12},{24,16},{28,20},{9,1},{13,5},{17,9},{2... | collective-permute-start | bytes 393224 | tf_op jit(solution)/shard_map/ppermute | solution.py:30
  49.9 20.3 %collective-permute-start.12 = (bf16[256,256]{1,0:T(8,128)(2,1)S(1)}, bf16[256,256]{1,0:T(8,128)(2,1)S(1)}, u32[]{:S(2)}, u32[]{:S(2)}) collective-permute-start(bf16[256,256]{1,0:T(8,128)(2,1)S(1)} %get-tuple-element.22), channel_id=1, source_target_pairs={{12,0},{16,4},{20,8},{24,12},{28,16},{13,1},{17,5},{21,9},{25,13},... | collective-permute-start | bytes 393224 | tf_op jit(solution)/shard_map/ppermute | solution.py:30
  51.2 19.0 %collective-permute-start.13 = (bf16[128,256]{1,0:T(8,128)(2,1)S(1)}, bf16[128,256]{1,0:T(8,128)(2,1)S(1)}, u32[]{:S(2)}, u32[]{:S(2)}) collective-permute-start(bf16[128,256]{1,0:T(8,128)(2,1)S(1)} %get-tuple-element.23), channel_id=1, source_target_pairs={{16,0},{20,4},{24,8},{28,12},{17,1},{21,5},{25,9},{29,13},{18,2},{... | collective-permute-start | bytes 196616 | tf_op jit(solution)/shard_map/ppermute | solution.py:30

commit v2 on v1

v2 whole, which is shorter than its diff:
```python
import functools
import math

import jax
import jax.numpy as jnp
from jax import lax
from jax.experimental import pallas as pl
from jax.experimental.pallas import tpu as pltpu
from jax.sharding import PartitionSpec as P

HEAD_SIZE = 128
BLK = 128
SCALE = 1.0 / math.sqrt(HEAD_SIZE)
SCALE2 = SCALE * math.log2(math.e)
LOW = -1e30
HIGH = 1e30
VMEM_LIMIT = 16 * 1024 * 1024

COST = pl.CostEstimate(flops=2**20, bytes_accessed=2**10, transcendentals=0)
LONG = pl.CostEstimate(flops=2**31, bytes_accessed=2**10, transcendentals=0)

HBM = pl.BlockSpec(memory_space=pltpu.HBM)
VMEM = pl.BlockSpec(memory_space=pltpu.VMEM)
SMEM = pl.BlockSpec(memory_space=pltpu.SMEM)


def in_hbm(array):
    return pltpu.with_memory_space_constraint(array, pltpu.HBM)


def dot(a, b):
    return jnp.dot(a, b, preferred_element_type=jnp.float32)


def shift(array, axis, by):
    devices = lax.axis_size(axis)
    pairs = [(i, i + by) for i in range(devices) if 0 <= i + by < devices]
    return lax.ppermute(array, axis, pairs)


def swap(array, bit, axis="tp"):
    return lax.ppermute(array, axis, [(i, i ^ bit) for i in range(lax.axis_size(axis))])


def block(i, n=1):
    return pl.ds(i * BLK, n * BLK)


def allowed(doc_ref, key_block, query_block):
    return (key_block >= 0) & (doc_ref[jnp.maximum(key_block, 0)] == doc_ref[query_block])


def causal(width):
    key = lax.broadcasted_iota(jnp.int32, (BLK, width), 0)
    query = lax.broadcasted_iota(jnp.int32, (BLK, width), 1) % BLK
    return key <= query


def forward_kernel(window, blocks, places, first_part, last_part, doc_ref, qt_ref, *refs):
    refs = list(refs)
    before = None if first_part else [refs.pop(0) for _ in range(3)]
    kv_refs = refs[:-7]
    *out_refs, k_all, vt_all, s_all, p_all = refs[-7:]
    width = qt_ref.shape[1]
    heads = width // HEAD_SIZE
    first = lax.axis_index("ctx") * blocks
    at = 0
    for ref in kv_refs:
        rows = ref.shape[0]
        k_all[pl.ds(at, rows), :] = ref[:, :HEAD_SIZE]
        vt_all[:, pl.ds(at, rows)] = ref[:, HEAD_SIZE:].T
        at += rows
    for b in range(blocks):
        qt = qt_ref[block(b), :]
        if first_part:
            out, top, total = None, jnp.full((1, width), LOW, jnp.float32), None
        else:
            out, top, total = before[0][block(b), :], *(r[pl.ds(b, 1), :] for r in before[1:])
        earlier = top
        inside = [i for i, place in enumerate(places) if b <= place < b + window]
        start, stop = inside[0], inside[-1] + 1
        ok = {i: allowed(doc_ref, first - (window - 1) + places[i], first + b) for i in inside}
        for i in inside:
            s = dot(k_all[block(i), :], qt) * SCALE2
            if places[i] == b + window - 1:
                s = jnp.where(causal(width), s, LOW)
            s_all[block(i - start), :] = s
            top = jnp.maximum(top, jnp.max(s, axis=0, keepdims=True) + jnp.where(ok[i], 0.0, LOW))
        sums = jnp.zeros((1, width), jnp.float32)
        for i in inside:
            p = jnp.exp2(s_all[block(i - start), :] - jnp.where(ok[i], top, HIGH))
            sums += jnp.sum(p, axis=0, keepdims=True)
            p_all[block(i - start), :] = p.astype(jnp.bfloat16)
        fresh = dot(vt_all[:, block(start, stop - start)], p_all[block(0, stop - start), :])
        if first_part:
            out, total = fresh, sums
        else:
            factor = jnp.exp2(earlier - top)
            out, total = out * factor + fresh, total * factor + sums
        if last_part:
            attn_ref, ot_ref, lse_ref = out_refs
            out = out / total
            ot_ref[block(b), :] = out.astype(jnp.bfloat16)
            lse_ref[pl.ds(b, 1), :] = top + jnp.log2(total)
            for h in range(heads):
                attn_ref[block(b), block(h)] = out[:, h * BLK:(h + 1) * BLK].T.astype(jnp.bfloat16)
        else:
            out_ref, top_ref, total_ref = out_refs
            out_ref[block(b), :] = out
            top_ref[pl.ds(b, 1), :] = top
            total_ref[pl.ds(b, 1), :] = total


def forward(doc_ids, qt, before, kvs, places, window, last_part, cost):
    rows, width = qt.shape
    blocks = rows // BLK
    held = len(places) * BLK
    used = min(held, window * BLK)
    extra = [] if before is None else list(before)
    stats = jax.ShapeDtypeStruct((blocks, width), jnp.float32)
    if last_part:
        out_shape = [jax.ShapeDtypeStruct((rows, width), jnp.bfloat16)] * 2 + [stats]
    else:
        out_shape = [jax.ShapeDtypeStruct((rows, width), jnp.float32), stats, stats]
    return pl.pallas_call(
        functools.partial(forward_kernel, window, blocks, places, before is None, last_part),
        out_shape=out_shape,
        in_specs=[SMEM] + [VMEM] * (1 + len(extra) + len(kvs)),
        out_specs=[VMEM] * 3,
        scratch_shapes=[
            pltpu.VMEM((held, HEAD_SIZE), jnp.bfloat16),
            pltpu.VMEM((HEAD_SIZE, held), jnp.bfloat16),
            pltpu.VMEM((used, width), jnp.float32),
            pltpu.VMEM((used, width), jnp.bfloat16),
        ],
        compiler_params=pltpu.CompilerParams(vmem_limit_bytes=VMEM_LIMIT),
        cost_estimate=cost,
        name="forward",
    )(doc_ids, qt, *extra, *kvs)


def backward_kernel(
    window, blocks, places, first_part, last_part, taking,
    doc_ref, qt_ref, q_rows_ref, ot_ref, lse_ref, g_ref, *refs
):
    refs = list(refs)
    before_ref = None if first_part else refs.pop(0)
    taken_ref = None if taking is None else refs.pop(0)
    n = (len(refs) - 9) // 2
    kv_refs, dq_ref, dkv_refs = refs[:n], refs[n], refs[n + 1:2 * n + 1]
    k_all, kt_all, v_all, g_rows, gt, p_all, ds_all, dkv_all = refs[2 * n + 1:]
    width = qt_ref.shape[1]
    heads = width // HEAD_SIZE
    me = lax.axis_index("ctx")
    first = me * blocks
    at = 0
    for ref in kv_refs:
        rows = ref.shape[0]
        k_all[pl.ds(at, rows), :] = ref[:, :HEAD_SIZE]
        kt_all[:, pl.ds(at, rows)] = ref[:, :HEAD_SIZE].T
        v_all[pl.ds(at, rows), :] = ref[:, HEAD_SIZE:]
        at += rows
    dkv_all[...] = jnp.zeros_like(dkv_all)
    for b in range(blocks):
        for h in range(heads):
            g = g_ref[block(b), block(h)]
            g_rows[block(h), :] = g
            gt[:, block(h)] = g.T
        qt = qt_ref[block(b), :]
        delta = jnp.sum(
            gt[...].astype(jnp.float32) * ot_ref[block(b), :].astype(jnp.float32),
            axis=0, keepdims=True,
        )
        lse = lse_ref[pl.ds(b, 1), :]
        inside = [i for i, place in enumerate(places) if b <= place < b + window]
        if not inside:
            if first_part:
                dq_ref[block(b), :] = jnp.zeros((BLK, width), jnp.float32)
            else:
                dq_ref[block(b), :] = before_ref[block(b), :]
            continue
        start, stop = inside[0], inside[-1] + 1
        for i in inside:
            ok = allowed(doc_ref, first - (window - 1) + places[i], first + b)
            s = dot(k_all[block(i), :], qt) * SCALE2
            if places[i] == b + window - 1:
                s = jnp.where(causal(width), s, LOW)
            p = jnp.exp2(s - jnp.where(ok, lse, HIGH))
            p_all[block(i - start), :] = p.astype(jnp.bfloat16)
            dp = dot(v_all[block(i), :], gt[...])
            ds_all[block(i - start), :] = (p * (dp - delta)).astype(jnp.bfloat16)
        mine, used = block(start, stop - start), block(0, stop - start)
        q_rows = q_rows_ref[pl.ds(b * width, width), :]
        dkv_all[mine, :HEAD_SIZE] += dot(ds_all[used, :], q_rows) * SCALE
        dkv_all[mine, HEAD_SIZE:] += dot(p_all[used, :], g_rows[...])
        dqt = dot(kt_all[:, mine], ds_all[used, :]) * SCALE
        if not first_part:
            dqt += before_ref[block(b), :]
        if last_part:
            for h in range(heads):
                dq_ref[block(b), block(h)] = dqt[:, h * BLK:(h + 1) * BLK].T.astype(jnp.bfloat16)
        else:
            dq_ref[block(b), :] = dqt
    at = 0
    for ref in dkv_refs:
        rows = ref.shape[0]
        total = dkv_all[pl.ds(at, rows), :]
        at += rows
        if taken_ref is not None and ref is dkv_refs[-1]:
            total += jnp.where(me % 2 == taking, taken_ref[...].astype(jnp.float32), 0.0)
        ref[...] = total.astype(ref.dtype)


def backward(doc_ids, qt, q_rows, ot, lse, g, before, taken, kvs, places, window, last_part):
    rows, width = qt.shape
    blocks = rows // BLK
    held = len(places) * BLK
    used = min(held, window * BLK)
    extra = [] if before is None else [before]
    extra += [] if taken is None else [taken[0]]
    kind = jnp.float32 if last_part else jnp.bfloat16
    dq_kind = jnp.bfloat16 if last_part else jnp.float32
    return pl.pallas_call(
        functools.partial(
            backward_kernel, window, blocks, places, before is None, last_part,
            None if taken is None else taken[1],
        ),
        out_shape=[jax.ShapeDtypeStruct((rows, width), dq_kind)]
        + [jax.ShapeDtypeStruct(kv.shape, kind) for kv in kvs],
        in_specs=[SMEM] + [VMEM] * (5 + len(extra) + len(kvs)),
        out_specs=[VMEM] * (1 + len(kvs)),
        scratch_shapes=[
            pltpu.VMEM((held, HEAD_SIZE), jnp.bfloat16),
            pltpu.VMEM((HEAD_SIZE, held), jnp.bfloat16),
            pltpu.VMEM((held, HEAD_SIZE), jnp.bfloat16),
            pltpu.VMEM((width, HEAD_SIZE), jnp.bfloat16),
            pltpu.VMEM((HEAD_SIZE, width), jnp.bfloat16),
            pltpu.VMEM((used, width), jnp.bfloat16),
            pltpu.VMEM((used, width), jnp.bfloat16),
            pltpu.VMEM((held, 2 * HEAD_SIZE), jnp.float32),
        ],
        compiler_params=pltpu.CompilerParams(vmem_limit_bytes=VMEM_LIMIT),
        cost_estimate=COST,
        name="backward",
    )(doc_ids, qt, q_rows, ot, lse, g, *extra, *kvs)


def part_of(w_ref, which, part):
    me = lax.axis_index("tp") ^ which
    return w_ref[:, pl.ds(pl.multiple_of(me * part, BLK), part)]


def features_in_kernel(which, *refs):
    *cots, w_ref, out_ref = refs
    part = cots[0].shape[1]
    total = None if len(cots) == len(which) else cots[-1][...]
    for j, cot in zip(which, cots):
        product = lax.dot_general(
            cot[...], part_of(w_ref, j, part), (((1,), (1,)), ((), ())),
            preferred_element_type=jnp.float32,
        )
        total = product if total is None else total + product
    out_ref[...] = total.astype(out_ref.dtype)


def features_in(which, cots, weight, base, dtype):
    rows, part = cots[0].shape
    depth = weight.shape[0]
    extra = [] if base is None else [base]
    return pl.pallas_call(
        functools.partial(features_in_kernel, which),
        out_shape=jax.ShapeDtypeStruct((rows, depth), dtype),
        in_specs=[VMEM] * (len(cots) + len(extra) + 1),
        out_specs=VMEM,
        compiler_params=pltpu.CompilerParams(vmem_limit_bytes=VMEM_LIMIT),
        cost_estimate=COST,
        name="features_in",
    )(*cots, *extra, weight)


def features_out_kernel(which, attn_ref, *refs):
    *extra, w_ref, out_ref = refs
    total = dot(attn_ref[...], part_of(w_ref, which, out_ref.shape[1]))
    for ref in extra:
        total = total + ref[...].astype(jnp.float32)
    out_ref[...] = total.astype(out_ref.dtype)


def features_out(which, attn, weight, part, extra=(), dtype=jnp.bfloat16):
    rows, depth = attn.shape
    return pl.pallas_call(
        functools.partial(features_out_kernel, which),
        out_shape=jax.ShapeDtypeStruct((rows, part), dtype),
        in_specs=[VMEM] * (2 + len(extra)),
        out_specs=VMEM,
        compiler_params=pltpu.CompilerParams(vmem_limit_bytes=VMEM_LIMIT),
        cost_estimate=COST,
        name="features_out",
    )(attn, *extra, weight)


def join_kernel(k_hbm, v_hbm, whole_ref, last_ref, k, v, sems):
    copies = [
        pltpu.make_async_copy(k_hbm, k, sems.at[0]),
        pltpu.make_async_copy(v_hbm, v, sems.at[1]),
    ]
    for copy in copies:
        copy.start()
    for copy in copies:
        copy.wait()
    skipped = k.shape[0] - last_ref.shape[0]
    whole_ref[:, :HEAD_SIZE] = k[...]
    whole_ref[:, HEAD_SIZE:] = v[...]
    last_ref[:, :HEAD_SIZE] = k[skipped:, :]
    last_ref[:, HEAD_SIZE:] = v[skipped:, :]


def join(keys, values, last):
    rows, width = keys.shape
    return pl.pallas_call(
        join_kernel,
        out_shape=[jax.ShapeDtypeStruct((n, 2 * width), keys.dtype) for n in (rows, last)],
        in_specs=[HBM] * 2,
        out_specs=[VMEM] * 2,
        scratch_shapes=[pltpu.VMEM(keys.shape, keys.dtype)] * 2 + [pltpu.SemaphoreType.DMA((2,))],
        compiler_params=pltpu.CompilerParams(vmem_limit_bytes=VMEM_LIMIT),
        cost_estimate=COST,
        name="join",
    )(in_hbm(keys), in_hbm(values))


def prepare_kernel(
    q_hbm, cot_hbm, cot_c_ref, w_hbm, near_ref, w_ref, qt_ref, q_rows_ref, q_ref, cot_ref, sems
):
    part = cot_ref.shape[1]
    rows, width = q_ref.shape
    me = lax.axis_index("tp")
    pairs = [(q_hbm, q_ref), (cot_hbm, cot_ref)]
    for j in range(4):
        columns = pl.ds(pl.multiple_of((me ^ j) * part, BLK), part)
        pairs.append((w_hbm.at[:, columns], w_ref.at[:, columns]))
    copies = [pltpu.make_async_copy(*pair, sems.at[i]) for i, pair in enumerate(pairs)]
    for copy in copies:
        copy.start()
    copies[0].wait()
    for b in range(rows // BLK):
        for h in range(width // BLK):
            q = q_ref[block(b), block(h)]
            qt_ref[block(b), block(h)] = q.T
            q_rows_ref[pl.ds(b * width + h * BLK, BLK), :] = q
    copies[1].wait()
    for j, cot in ((0, cot_ref), (1, cot_c_ref)):
        copies[2 + j].wait()
        product = lax.dot_general(
            cot[...], part_of(w_ref, j, part), (((1,), (1,)), ((), ())),
            preferred_element_type=jnp.float32,
        )
        near_ref[...] = product if j == 0 else near_ref[...] + product
    copies[4].wait()
    copies[5].wait()


def prepare(q, cot, cot_c, weight):
    rows, width = q.shape
    blocks = rows // BLK
    return pl.pallas_call(
        prepare_kernel,
        out_shape=[
            jax.ShapeDtypeStruct((rows, width), jnp.float32),
            jax.ShapeDtypeStruct(weight.shape, weight.dtype),
            jax.ShapeDtypeStruct((rows, width), q.dtype),
            jax.ShapeDtypeStruct((blocks * width, BLK), q.dtype),
        ],
        in_specs=[HBM, HBM, VMEM, HBM],
        out_specs=[VMEM] * 4,
        scratch_shapes=[
            pltpu.VMEM(q.shape, q.dtype),
            pltpu.VMEM(cot.shape, cot.dtype),
            pltpu.SemaphoreType.DMA((6,)),
        ],
        compiler_params=pltpu.CompilerParams(vmem_limit_bytes=VMEM_LIMIT),
        cost_estimate=COST,
        name="prepare",
    )(in_hbm(q), in_hbm(cot), cot_c, in_hbm(weight))


def on_device(queries, keys, values, out_weight, cotangent, doc_ids):
    rows = queries.shape[0]
    part = cotangent.shape[1]
    ctx_count = lax.axis_size("ctx")
    blocks = rows // BLK
    window = min(8 * blocks, blocks * ctx_count // 2)
    needs = []
    left = window - 1
    while left > 0:
        needs.append(min(left, blocks))
        left -= needs[-1]
    odd = lax.axis_index("ctx") % 2
    key_value, tail = join(keys, values, needs[-1] * BLK)
    key_value, tail, cot = lax.optimization_barrier((key_value, tail, cotangent))
    cot_y = swap(cot, 2)
    held = [key_value, None]
    held += [
        shift(tail if n < blocks else key_value, "ctx", s)
        for s, n in enumerate(needs[1:], start=2)
    ]
    held[1] = swap(jnp.where(odd == 0, key_value, held[2]), 1, "ctx")
    near, weight, qt, q_rows = prepare(queries, cot, swap(cot, 1), out_weight)
    def places_of(shards):
        places = []
        for s in shards:
            top = window - 1 - (s - 1) * blocks if s > 0 else window - 1 + blocks
            places += range(top - (needs[s - 1] if s > 0 else blocks), top)
        return tuple(places)

    def part_back(shards, before, taken, last_part):
        return backward(
            doc_ids, qt, q_rows, ot, lse, grad_attn, before, taken,
            [held[s] for s in shards], places_of(shards), window, last_part,
        )

    shards = list(range(len(needs), 1, -1)) + [0]
    state = forward(
        doc_ids, qt, None, [held[s] for s in shards], places_of(shards), window, False, LONG
    )
    attn, ot, lse = forward(doc_ids, qt, state, [held[1]], places_of([1]), window, True, COST)
    attn, cot_y = lax.optimization_barrier((attn, cot_y))
    cot_d = swap(cot_y, 1)
    grad_attn = features_in((2, 3), [cot_y, cot_d], weight, near, jnp.bfloat16)
    out_a = features_out(3, attn, weight, part)

    odds, evens = [list(range(len(needs), 0, -1))[(len(needs) - 1 - i) % 2::2] for i in (0, 1)]
    dq, *odd_parts = part_back(odds, None, None, False)
    taken = swap(odd_parts[-1], 1, "ctx")
    dq, out_a = lax.optimization_barrier((dq, swap(out_a, 1)))
    out_b = features_out(2, attn, weight, part, [out_a])
    from_y = swap(out_b, 2)
    dq, *even_parts = part_back(evens, dq, (taken, 1), False)
    dq, own = part_back([0], dq, (taken, 0), True)
    parts = dict(zip(odds, odd_parts)) | dict(zip(evens, even_parts))
    backs = {s: shift(parts[s], "ctx", -s) for s in range(2, len(held))}
    out_c = features_out(1, attn, weight, part)
    out_d = features_out(0, attn, weight, part, [swap(out_c, 1)], jnp.float32)
    backs, out_d = lax.optimization_barrier((backs, out_d))
    for s, back in backs.items():
        back = back.astype(jnp.float32)
        own = own + jnp.pad(back, ((rows - back.shape[0], 0), (0, 0)))
    mixed = (out_d + from_y.astype(jnp.float32)).astype(jnp.bfloat16)
    return (
        mixed,
        dq,
        own[:, :HEAD_SIZE].astype(jnp.bfloat16),
        own[:, HEAD_SIZE:].astype(jnp.bfloat16),
    )


def solution(mesh):
    return jax.shard_map(
        on_device,
        mesh=mesh,
        in_specs=(
            P("ctx", "tp"),
            P("ctx", "tp"),
            P("ctx", "tp"),
            P("tp", None),
            P("ctx", "tp"),
            P(),
        ),
        out_specs=(P("ctx", "tp"), P("ctx", "tp"), P("ctx", "tp"), P("ctx", "tp")),
        check_vma=False,
    )
```

time: 72.4 us -> 50.4 us (0.70)
  waiting for transfers between devices: 16.8 us -> 7.61 us
  Pallas kernels: 25.9 us -> 19.3 us
  local copies, waits for them, and re-layouts: 4 us -> 0.67 us
  starting transfers between devices: 23.2 us -> 20.6 us
    ppermute x8 -> x6, waiting for transfers between devices: 16.7 us -> 5.73 us  [shift(): return lax.ppermute(array, axis, pairs)]
    pallas_call x8 -> x12, Pallas kernels: 25.9 us -> 19.3 us  [the longest x3 6.8 us: backward(): pl.pallas_call(functools.partial(backward_kernel, window, blocks, places,...]
    ppermute x8 -> x6, starting transfers between devices: 18.5 us -> 14.1 us  [shift(): return lax.ppermute(array, axis, pairs)]
    unnamed x7 -> x2, local copies, waits for them, and re-layouts: 2.48 us -> 0.01 us
    ppermute x6 -> x8, waiting for transfers between devices: 0.02 us -> 1.89 us  [swap(): lax.ppermute(array, axis, [(i, i ^ bit) for i in range(lax.axis_size(axis...]
    ppermute x6 -> x8, starting transfers between devices: 4.72 us -> 6.57 us  [swap(): lax.ppermute(array, axis, [(i, i ^ bit) for i in range(lax.axis_size(axis...]
    concatenate x1 -> x0, local copies, waits for them, and re-layouts: 0.86 us -> none  [on_device(): key_value = jnp.concatenate([keys, values], axis=1)]
  transfers between devices with their start and end apart: 14 -> 14, of which waited for: 2 -> 2; matrix products, arithmetic and copies ran while one was open for 4% -> 1% of each run, Pallas kernels for 36% -> 37%
where the time goes in v2:
time: 50.4 us; the launch traced here: 50.1 us
  starting transfers between devices  20.6 us (41%)
  Pallas kernels  19.3 us (38%)
  waiting for transfers between devices  7.61 us (15%)
  other arithmetic  1.03 us (2%)
  between operations  0.85 us (2%)
  local copies, waits for them, and re-layouts  0.67 us (1%)
    ppermute x6, starting transfers between devices, shift(): return lax.ppermute(array, axis, pairs)  14.1 us
    pallas_call x3, Pallas kernels, backward(): pl.pallas_call(functools.partial(backward_kernel, window, blocks, places,...  6.8 us
    ppermute x8, starting transfers between devices, swap(): lax.ppermute(array, axis, [(i, i ^ bit) for i in range(lax.axis_size(axis...  6.57 us
    ppermute x6, waiting for transfers between devices, shift(): return lax.ppermute(array, axis, pairs)  5.73 us
    pallas_call x2, Pallas kernels, forward(): pl.pallas_call(functools.partial(forward_kernel, window, blocks, places,...  4.16 us
    pallas_call x1, Pallas kernels, prepare(): pl.pallas_call(prepare_kernel, out_shape=[jax.ShapeDtypeStruct((rows, wid...  3.43 us
    pallas_call x4, Pallas kernels, features_out(): pl.pallas_call(functools.partial(features_out_kernel, which), out_shape=j...  2.78 us
    ppermute x8, waiting for transfers between devices, swap(): lax.ppermute(array, axis, [(i, i ^ bit) for i in range(lax.axis_size(axis...  1.89 us
  transfers between devices with their start and end apart: 14, of which 2 were waited for; matrix products, arithmetic and copies ran while one was open for 1% of the time, Pallas kernels for 37%

profile of v2, /device:TPU:0, one launch (start us, length us, event | category | flops | bytes accessed | tf_op | source)
XLA Modules:
  0.0 50.1 jit_solution(6315659835013866174)
XLA Ops:
  0.6 0.9 %join.1 = (bf16[256,256]{1,0:T(8,128)(2,1)S(1)}, bf16[128,256]{1,0:T(8,128)(2,1)S(1)}) custom-call(bf16[256,128]{1,0:T(8,128)(2,1)} %k_hbm.1, bf16[256,128]{1,0:T(8,128)(2,1)} %v_hbm.1), custom_call_target="tpu_custom_call" | custom-call | flops 1048576 | bytes 1024 | tf_op jit(solution)/shard_map/join/pallas_call | solution.py:320
  1.6 0.5 %collective-permute-start = (bf16[256,1280]{1,0:T(8,128)(2,1)}, bf16[256,1280]{1,0:T(8,128)(2,1)S(1)}, u32[]{:S(2)}, u32[]{:S(2)}) collective-permute-start(bf16[256,1280]{1,0:T(8,128)(2,1)} %cot_hbm), channel_id=1, source_target_pairs={{0,1},{1,0},{2,3},{3,2},{4,5},{5,4},{6,7},{7,6},{8,9},{9,8},{10,11... | collective-permute-start | bytes 1966088 | tf_op jit(solution)/shard_map/ppermute | solution.py:42
  2.1 2.6 %collective-permute-start.5 = (bf16[256,1280]{1,0:T(8,128)(2,1)}, bf16[256,1280]{1,0:T(8,128)(2,1)S(1)}, u32[]{:S(2)}, u32[]{:S(2)}) collective-permute-start(bf16[256,1280]{1,0:T(8,128)(2,1)} %cot_hbm), channel_id=1, source_target_pairs={{0,2},{1,3},{2,0},{3,1},{4,6},{5,7},{6,4},{7,5},{8,10},{9,11},{10,... | collective-permute-start | bytes 1966088 | tf_op jit(solution)/shard_map/ppermute | solution.py:42
  4.7 3.5 %collective-permute-start.3 = (bf16[256,256]{1,0:T(8,128)(2,1)S(1)}, bf16[256,256]{1,0:T(8,128)(2,1)S(1)}, u32[]{:S(2)}, u32[]{:S(2)}) collective-permute-start(bf16[256,256]{1,0:T(8,128)(2,1)S(1)} %get-tuple-element.41.refs_3_.refs_2_), channel_id=1, source_target_pairs={{0,8},{4,12},{8,16},{12,20},{16,24},{20,28},{1,9},{5,13},{9,17},{1... | collective-permute-start | bytes 393224 | tf_op jit(solution)/shard_map/ppermute | solution.py:38
  8.2 4.4 %collective-permute-start.2 = (bf16[256,256]{1,0:T(8,128)(2,1)S(1)}, bf16[256,256]{1,0:T(8,128)(2,1)S(1)}, u32[]{:S(2)}, u32[]{:S(2)}) collective-permute-start(bf16[256,256]{1,0:T(8,128)(2,1)S(1)} %get-tuple-element.41.refs_3_.refs_2_), channel_id=1, source_target_pairs={{0,12},{4,16},{8,20},{12,24},{16,28},{1,13},{5,17},{9,21},{13,25},... | collective-permute-start | bytes 393224 | tf_op jit(solution)/shard_map/ppermute | solution.py:38
  12.6 2.3 %collective-permute-start.1 = (bf16[128,256]{1,0:T(8,128)(2,1)S(1)}, bf16[128,256]{1,0:T(8,128)(2,1)S(1)}, u32[]{:S(2)}, u32[]{:S(2)}) collective-permute-start(bf16[128,256]{1,0:T(8,128)(2,1)S(1)} %get-tuple-element.40), channel_id=1, source_target_pairs={{0,16},{4,20},{8,24},{12,28},{1,17},{5,21},{9,25},{13,29},{2,18},{... | collective-permute-start | bytes 196616 | tf_op jit(solution)/shard_map/ppermute | solution.py:38
  14.9 0.0 collective-permute-done.3.refs_2_.refs_3_
  14.9 0.0 copy-start
  14.9 0.6 %collective-permute-start.4 = (bf16[256,256]{1,0:T(8,128)(2,1)S(1)}, bf16[256,256]{1,0:T(8,128)(2,1)S(1)}, u32[]{:S(2)}, u32[]{:S(2)}) collective-permute-start(bf16[256,256]{1,0:T(8,128)(2,1)S(1)} %broadcast_select_fusion), channel_id=1, source_target_pairs={{0,4},{4,0},{8,12},{12,8},{16,20},{20,16},{24,28},{28,24},{1,5},{5... | collective-permute-start | bytes 393224 | tf_op jit(solution)/shard_map/ppermute | solution.py:42
  15.6 0.0 collective-permute-done.cot_c_ref
  15.6 3.4 %prepare.1 = (f32[256,640]{1,0:T(8,128)S(1)}, bf16[640,5120]{1,0:T(8,128)(2,1)S(1)}, bf16[256,640]{1,0:T(8,128)(2,1)S(1)}, bf16[1280,128]{1,0:T(8,128)(2,1)S(1)}) custom-call(bf16[256,640]{1,0:T(8,128)(2,1)} %q_hbm.1, bf16[256,1280]{1,0:T(8,128)(2,1)} %cot_hbm, bf16[256,1280]{1,0:T(8,128)(2,1)S(1)} %collective-permute-done.cot_c_ref, bf16[640,5120]{1,0:T(8,128)(2,1)} %w_hbm.1), custom_call_target="tpu_custom_call" | custom-call | flops 1048576 | bytes 1024 | tf_op jit(solution)/shard_map/prepare/pallas_call | solution.py:366
  19.0 0.0 collective-permute-done.1.refs_0_.refs_2_
  19.0 0.0 collective-permute-done.2.refs_1_.refs_0_
  19.0 0.0 copy-done
  19.0 2.6 %forward.2 = (f32[256,640]{1,0:T(8,128)S(1)}, f32[2,640]{1,0:T(2,128)S(1)}, f32[2,640]{1,0:T(2,128)S(1)}) custom-call(s32[16]{0:T(128)S(1)} %copy-done, bf16[256,640]{1,0:T(8,128)(2,1)S(1)} %get-tuple-element.38.qt_ref, bf16[128,256]{1,0:T(8,128)(2,1)S(1)} %collective-permute-done.1.refs_0_.refs_2_, ...), custom_call_target="tpu_custom_call" | custom-call | flops 2147483648 | bytes 1024 | tf_op jit(solution)/shard_map/forward/pallas_call | solution.py:125
  21.6 0.0 collective-permute-done.4.refs_3_.refs_1_
  21.6 1.6 %forward.3 = (bf16[256,640]{1,0:T(8,128)(2,1)S(1)}, bf16[256,640]{1,0:T(8,128)(2,1)S(1)}, f32[2,640]{1,0:T(2,128)S(1)}) custom-call(s32[16]{0:T(128)S(1)} %copy-done, bf16[256,640]{1,0:T(8,128)(2,1)S(1)} %get-tuple-element.38.qt_ref, f32[256,640]{1,0:T(8,128)S(1)} %get-tuple-element.42.refs_0_, f32[2,640]{1,0:T(2,128)S(1)} %get-tuple-element.43.refs_1_, ...), custom_call_target="tpu_custom_call" | custom-call | flops 1048576 | bytes 1024 | tf_op jit(solution)/shard_map/forward/pallas_call | solution.py:125
  23.2 0.0 collective-permute-done.5.refs_0_
  23.2 0.1 collective-permute-start.6
  23.3 0.7 %features_out.4 = bf16[256,1280]{1,0:T(8,128)(2,1)S(1)} custom-call(bf16[256,640]{1,0:T(8,128)(2,1)S(1)} %get-tuple-element.52.attn_ref, bf16[640,5120]{1,0:T(8,128)(2,1)S(1)} %get-tuple-element.50.refs_3_.refs_0_.refs_1_), custom_call_target="tpu_custom_call" | custom-call | flops 1048576 | bytes 1024 | tf_op jit(solution)/shard_map/features_out/pallas_call | solution.py:291
  24.0 0.6 %collective-permute-start.7 = (bf16[256,1280]{1,0:T(8,128)(2,1)S(1)}, bf16[256,1280]{1,0:T(8,128)(2,1)S(1)}, u32[]{:S(2)}, u32[]{:S(2)}) collective-permute-start(bf16[256,1280]{1,0:T(8,128)(2,1)S(1)} %features_out.4), channel_id=1, source_target_pairs={{0,1},{1,0},{2,3},{3,2},{4,5},{5,4},{6,7},{7,6},{8,9},{9,8},{10,11... | collective-permute-start | bytes 1966088 | tf_op jit(solution)/shard_map/ppermute | solution.py:42
  24.6 0.7 %features_out.5 = bf16[256,1280]{1,0:T(8,128)(2,1)S(1)} custom-call(bf16[256,640]{1,0:T(8,128)(2,1)S(1)} %get-tuple-element.52.attn_ref, bf16[640,5120]{1,0:T(8,128)(2,1)S(1)} %get-tuple-element.50.refs_3_.refs_0_.refs_1_), custom_call_target="tpu_custom_call" | custom-call | flops 1048576 | bytes 1024 | tf_op jit(solution)/shard_map/features_out/pallas_call | solution.py:291
  25.3 0.1 collective-permute-start.12
  25.4 0.0 collective-permute-done.6.refs_1_
  25.4 1.2 %features_in.1.g_ref = bf16[256,640]{1,0:T(8,128)(2,1)S(1)} custom-call(bf16[256,1280]{1,0:T(8,128)(2,1)S(1)} %collective-permute-done.5.refs_0_, bf16[256,1280]{1,0:T(8,128)(2,1)S(1)} %collective-permute-done.6.refs_1_, f32[256,640]{1,0:T(8,128)S(1)} %get-tuple-element.49.refs_2_, bf16[640,5120]{1,0:T(8,128)(2,1)S(1)} %get-tuple-element.50.refs_3_.refs_0_.refs_1_), custom_call_target="tpu_custom_call" | custom-call | flops 1048576 | bytes 1024 | tf_op jit(solution)/shard_map/features_in/pallas_call | solution.py:270
  26.6 2.5 %backward.3 = (f32[256,640]{1,0:T(8,128)S(1)}, bf16[256,256]{1,0:T(8,128)(2,1)S(1)}, bf16[256,256]{1,0:T(8,128)(2,1)S(1)}) custom-call(s32[16]{0:T(128)S(1)} %copy-done, bf16[256,640]{1,0:T(8,128)(2,1)S(1)} %get-tuple-element.38.qt_ref, bf16[1280,128]{1,0:T(8,128)(2,1)S(1)} %get-tuple-element.39.q_rows_ref, bf16[256,640]{1,0:T(8,128)(2,1)S(1)} %get-tuple-element.45.ot_ref, ...), custom_call_target="tpu_custom_call" | custom-call | flops 1048576 | bytes 1024 | tf_op jit(solution)/shard_map/backward/pallas_call | solution.py:223
  29.1 1.5 %collective-permute-start.8 = (bf16[256,256]{1,0:T(8,128)(2,1)S(1)}, bf16[256,256]{1,0:T(8,128)(2,1)S(1)}, u32[]{:S(2)}, u32[]{:S(2)}) collective-permute-start(bf16[256,256]{1,0:T(8,128)(2,1)S(1)} %get-tuple-element.54), channel_id=1, source_target_pairs={{0,4},{4,0},{8,12},{12,8},{16,20},{20,16},{24,28},{28,24},{1,5},{5... | collective-permute-start | bytes 393224 | tf_op jit(solution)/shard_map/ppermute | solution.py:42
  30.6 0.0 collective-permute-done.7.refs_0_
  30.6 0.7 %features_out.7 = bf16[256,1280]{1,0:T(8,128)(2,1)S(1)} custom-call(bf16[256,640]{1,0:T(8,128)(2,1)S(1)} %get-tuple-element.52.attn_ref, bf16[256,1280]{1,0:T(8,128)(2,1)S(1)} %collective-permute-done.7.refs_0_, bf16[640,5120]{1,0:T(8,128)(2,1)S(1)} %get-tuple-element.50.refs_3_.refs_0_.refs_1_), custom_call_target="tpu_custom_call" | custom-call | flops 1048576 | bytes 1024 | tf_op jit(solution)/shard_map/features_out/pallas_call | solution.py:291
  31.3 0.6 %collective-permute-start.13 = (bf16[256,1280]{1,0:T(8,128)(2,1)S(1)}, bf16[256,1280]{1,0:T(8,128)(2,1)S(1)}, u32[]{:S(2)}, u32[]{:S(2)}) collective-permute-start(bf16[256,1280]{1,0:T(8,128)(2,1)S(1)} %features_out.7), channel_id=1, source_target_pairs={{0,2},{1,3},{2,0},{3,1},{4,6},{5,7},{6,4},{7,5},{8,10},{9,11},{10,... | collective-permute-start | bytes 1966088 | tf_op jit(solution)/shard_map/ppermute | solution.py:42
  31.9 1.3 %collective-permute-start.10 = (bf16[256,256]{1,0:T(8,128)(2,1)S(1)}, bf16[256,256]{1,0:T(8,128)(2,1)S(1)}, u32[]{:S(2)}, u32[]{:S(2)}) collective-permute-start(bf16[256,256]{1,0:T(8,128)(2,1)S(1)} %get-tuple-element.56), channel_id=1, source_target_pairs={{12,0},{16,4},{20,8},{24,12},{28,16},{13,1},{17,5},{21,9},{25,13},... | collective-permute-start | bytes 393224 | tf_op jit(solution)/shard_map/ppermute | solution.py:38
  33.2 1.8 %collective-permute-done.8.refs_1_ = bf16[256,256]{1,0:T(8,128)(2,1)S(1)} collective-permute-done((bf16[256,256]{1,0:T(8,128)(2,1)S(1)}, bf16[256,256]{1,0:T(8,128)(2,1)S(1)}, u32[]{:S(2)}, u32[]{:S(2)}) %collective-permute-start.8) | collective-permute-done | bytes 131104 | tf_op jit(solution)/shard_map/ppermute | solution.py:42
  35.0 1.9 %backward.4 = (f32[256,640]{1,0:T(8,128)S(1)}, bf16[128,256]{1,0:T(8,128)(2,1)S(1)}, bf16[256,256]{1,0:T(8,128)(2,1)S(1)}) custom-call(s32[16]{0:T(128)S(1)} %copy-done, bf16[256,640]{1,0:T(8,128)(2,1)S(1)} %get-tuple-element.38.qt_ref, bf16[1280,128]{1,0:T(8,128)(2,1)S(1)} %get-tuple-element.39.q_rows_ref, bf16[256,640]{1,0:T(8,128)(2,1)S(1)} %get-tuple-element.45.ot_ref, ...), custom_call_target="tpu_custom_call" | custom-call | flops 1048576 | bytes 1024 | tf_op jit(solution)/shard_map/backward/pallas_call | solution.py:223
  37.0 1.3 %collective-permute-start.9 = (bf16[256,256]{1,0:T(8,128)(2,1)S(1)}, bf16[256,256]{1,0:T(8,128)(2,1)S(1)}, u32[]{:S(2)}, u32[]{:S(2)}) collective-permute-start(bf16[256,256]{1,0:T(8,128)(2,1)S(1)} %get-tuple-element.55), channel_id=1, source_target_pairs={{8,0},{12,4},{16,8},{20,12},{24,16},{28,20},{9,1},{13,5},{17,9},{2... | collective-permute-start | bytes 393224 | tf_op jit(solution)/shard_map/ppermute | solution.py:38
  38.3 1.3 %collective-permute-start.11 = (bf16[128,256]{1,0:T(8,128)(2,1)S(1)}, bf16[128,256]{1,0:T(8,128)(2,1)S(1)}, u32[]{:S(2)}, u32[]{:S(2)}) collective-permute-start(bf16[128,256]{1,0:T(8,128)(2,1)S(1)} %get-tuple-element.57), channel_id=1, source_target_pairs={{16,0},{20,4},{24,8},{28,12},{17,1},{21,5},{25,9},{29,13},{18,2},{... | collective-permute-start | bytes 196616 | tf_op jit(solution)/shard_map/ppermute | solution.py:38
  39.6 0.0 collective-permute-done.12.refs_0_
  39.6 0.7 %features_out.6 = f32[256,1280]{1,0:T(8,128)S(1)} custom-call(bf16[256,640]{1,0:T(8,128)(2,1)S(1)} %get-tuple-element.52.attn_ref, bf16[256,1280]{1,0:T(8,128)(2,1)S(1)} %collective-permute-done.12.refs_0_, bf16[640,5120]{1,0:T(8,128)(2,1)S(1)} %get-tuple-element.50.refs_3_.refs_0_.refs_1_), custom_call_target="tpu_custom_call" | custom-call | flops 1048576 | bytes 1024 | tf_op jit(solution)/shard_map/features_out/pallas_call | solution.py:291
  40.3 2.4 %backward.5 = (bf16[256,640]{1,0:T(8,128)(2,1)}, f32[256,256]{1,0:T(8,128)S(1)}) custom-call(s32[16]{0:T(128)S(1)} %copy-done, bf16[256,640]{1,0:T(8,128)(2,1)S(1)} %get-tuple-element.38.qt_ref, bf16[1280,128]{1,0:T(8,128)(2,1)S(1)} %get-tuple-element.39.q_rows_ref, bf16[256,640]{1,0:T(8,128)(2,1)S(1)} %get-tuple-element.45.ot_ref, ...), custom_call_target="tpu_custom_call" | custom-call | flops 1048576 | bytes 1024 | tf_op jit(solution)/shard_map/backward/pallas_call | solution.py:223
  42.7 0.0 collective-permute-done.10
  42.7 5.7 %collective-permute-done.11 = bf16[128,256]{1,0:T(8,128)(2,1)S(1)} collective-permute-done((bf16[128,256]{1,0:T(8,128)(2,1)S(1)}, bf16[128,256]{1,0:T(8,128)(2,1)S(1)}, u32[]{:S(2)}, u32[]{:S(2)}) %collective-permute-start.11) | collective-permute-done | bytes 65568 | tf_op jit(solution)/shard_map/ppermute | solution.py:38
  48.4 0.0 collective-permute-done.9
  48.4 0.1 add_convert_fusion.1
  48.5 0.7 %fusion = (bf16[256,128]{1,0:T(8,128)(2,1)}, bf16[256,128]{1,0:T(8,128)(2,1)}) fusion(bf16[256,256]{1,0:T(8,128)(2,1)S(1)} %add_convert_fusion.1), kind=kLoop, calls=%fused_computation.3 | loop fusion | bytes 262144 | tf_op jit(solution)/shard_map/slice | solution.py:453
  49.1 0.0 collective-permute-done.13
  49.1 1.0 %add_convert_fusion = bf16[256,1280]{1,0:T(8,128)(2,1)} fusion(f32[256,1280]{1,0:T(8,128)S(1)} %features_out.6, bf16[256,1280]{1,0:T(8,128)(2,1)S(1)} %collective-permute-done.13), kind=kLoop, calls=%fused_computation | loop fusion | flops 983040 | bytes 2621440 | tf_op jit(solution)/shard_map/convert_element_type | solution.py:448
  (1 shorter events, 0.0 us)
Async XLA Ops:
  1.6 14.0 %collective-permute-start = (bf16[256,1280]{1,0:T(8,128)(2,1)}, bf16[256,1280]{1,0:T(8,128)(2,1)S(1)}, u32[]{:S(2)}, u32[]{:S(2)}) collective-permute-start(bf16[256,1280]{1,0:T(8,128)(2,1)} %cot_hbm), channel_id=1, source_target_pairs={{0,1},{1,0},{2,3},{3,2},{4,5},{5,4},{6,7},{7,6},{8,9},{9,8},{10,11... | collective-permute-start | bytes 1966088 | tf_op jit(solution)/shard_map/ppermute | solution.py:42
  2.1 21.2 %collective-permute-start.5 = (bf16[256,1280]{1,0:T(8,128)(2,1)}, bf16[256,1280]{1,0:T(8,128)(2,1)S(1)}, u32[]{:S(2)}, u32[]{:S(2)}) collective-permute-start(bf16[256,1280]{1,0:T(8,128)(2,1)} %cot_hbm), channel_id=1, source_target_pairs={{0,2},{1,3},{2,0},{3,1},{4,6},{5,7},{6,4},{7,5},{8,10},{9,11},{10,... | collective-permute-start | bytes 1966088 | tf_op jit(solution)/shard_map/ppermute | solution.py:42
  4.7 10.2 %collective-permute-start.3 = (bf16[256,256]{1,0:T(8,128)(2,1)S(1)}, bf16[256,256]{1,0:T(8,128)(2,1)S(1)}, u32[]{:S(2)}, u32[]{:S(2)}) collective-permute-start(bf16[256,256]{1,0:T(8,128)(2,1)S(1)} %get-tuple-element.41.refs_3_.refs_2_), channel_id=1, source_target_pairs={{0,8},{4,12},{8,16},{12,20},{16,24},{20,28},{1,9},{5,13},{9,17},{1... | collective-permute-start | bytes 393224 | tf_op jit(solution)/shard_map/ppermute | solution.py:38
  8.2 10.9 %collective-permute-start.2 = (bf16[256,256]{1,0:T(8,128)(2,1)S(1)}, bf16[256,256]{1,0:T(8,128)(2,1)S(1)}, u32[]{:S(2)}, u32[]{:S(2)}) collective-permute-start(bf16[256,256]{1,0:T(8,128)(2,1)S(1)} %get-tuple-element.41.refs_3_.refs_2_), channel_id=1, source_target_pairs={{0,12},{4,16},{8,20},{12,24},{16,28},{1,13},{5,17},{9,21},{13,25},... | collective-permute-start | bytes 393224 | tf_op jit(solution)/shard_map/ppermute | solution.py:38
  12.6 6.4 %collective-permute-start.1 = (bf16[128,256]{1,0:T(8,128)(2,1)S(1)}, bf16[128,256]{1,0:T(8,128)(2,1)S(1)}, u32[]{:S(2)}, u32[]{:S(2)}) collective-permute-start(bf16[128,256]{1,0:T(8,128)(2,1)S(1)} %get-tuple-element.40), channel_id=1, source_target_pairs={{0,16},{4,20},{8,24},{12,28},{1,17},{5,21},{9,25},{13,29},{2,18},{... | collective-permute-start | bytes 196616 | tf_op jit(solution)/shard_map/ppermute | solution.py:38
  14.9 4.1 %copy-start = (s32[16]{0:T(128)S(1)}, s32[16]{0:T(128)}, u32[]{:S(2)}) copy-start(s32[16]{0:T(128)} %doc_ref.9) | copy-start | bytes 196
  14.9 6.7 %collective-permute-start.4 = (bf16[256,256]{1,0:T(8,128)(2,1)S(1)}, bf16[256,256]{1,0:T(8,128)(2,1)S(1)}, u32[]{:S(2)}, u32[]{:S(2)}) collective-permute-start(bf16[256,256]{1,0:T(8,128)(2,1)S(1)} %broadcast_select_fusion), channel_id=1, source_target_pairs={{0,4},{4,0},{8,12},{12,8},{16,20},{20,16},{24,28},{28,24},{1,5},{5... | collective-permute-start | bytes 393224 | tf_op jit(solution)/shard_map/ppermute | solution.py:42
  23.2 2.2 %collective-permute-start.6 = (bf16[256,1280]{1,0:T(8,128)(2,1)S(1)}, bf16[256,1280]{1,0:T(8,128)(2,1)S(1)}, u32[]{:S(2)}, u32[]{:S(2)}) collective-permute-start(bf16[256,1280]{1,0:T(8,128)(2,1)S(1)} %collective-permute-done.5.refs_0_), channel_id=1, source_target_pairs={{0,1},{1,0},{2,3},{3,2},{4,5},{5,4},{6,7},{7,6},{8,9},{9,8},{10,11... | collective-permute-start | bytes 1966088 | tf_op jit(solution)/shard_map/ppermute | solution.py:42
  24.0 6.6 %collective-permute-start.7 = (bf16[256,1280]{1,0:T(8,128)(2,1)S(1)}, bf16[256,1280]{1,0:T(8,128)(2,1)S(1)}, u32[]{:S(2)}, u32[]{:S(2)}) collective-permute-start(bf16[256,1280]{1,0:T(8,128)(2,1)S(1)} %features_out.4), channel_id=1, source_target_pairs={{0,1},{1,0},{2,3},{3,2},{4,5},{5,4},{6,7},{7,6},{8,9},{9,8},{10,11... | collective-permute-start | bytes 1966088 | tf_op jit(solution)/shard_map/ppermute | solution.py:42
  25.3 14.3 %collective-permute-start.12 = (bf16[256,1280]{1,0:T(8,128)(2,1)S(1)}, bf16[256,1280]{1,0:T(8,128)(2,1)S(1)}, u32[]{:S(2)}, u32[]{:S(2)}) collective-permute-start(bf16[256,1280]{1,0:T(8,128)(2,1)S(1)} %features_out.5), channel_id=1, source_target_pairs={{0,1},{1,0},{2,3},{3,2},{4,5},{5,4},{6,7},{7,6},{8,9},{9,8},{10,11... | collective-permute-start | bytes 1966088 | tf_op jit(solution)/shard_map/ppermute | solution.py:42
  29.1 5.9 %collective-permute-start.8 = (bf16[256,256]{1,0:T(8,128)(2,1)S(1)}, bf16[256,256]{1,0:T(8,128)(2,1)S(1)}, u32[]{:S(2)}, u32[]{:S(2)}) collective-permute-start(bf16[256,256]{1,0:T(8,128)(2,1)S(1)} %get-tuple-element.54), channel_id=1, source_target_pairs={{0,4},{4,0},{8,12},{12,8},{16,20},{20,16},{24,28},{28,24},{1,5},{5... | collective-permute-start | bytes 393224 | tf_op jit(solution)/shard_map/ppermute | solution.py:42
  31.3 17.8 %collective-permute-start.13 = (bf16[256,1280]{1,0:T(8,128)(2,1)S(1)}, bf16[256,1280]{1,0:T(8,128)(2,1)S(1)}, u32[]{:S(2)}, u32[]{:S(2)}) collective-permute-start(bf16[256,1280]{1,0:T(8,128)(2,1)S(1)} %features_out.7), channel_id=1, source_target_pairs={{0,2},{1,3},{2,0},{3,1},{4,6},{5,7},{6,4},{7,5},{8,10},{9,11},{10,... | collective-permute-start | bytes 1966088 | tf_op jit(solution)/shard_map/ppermute | solution.py:42
  31.9 10.8 %collective-permute-start.10 = (bf16[256,256]{1,0:T(8,128)(2,1)S(1)}, bf16[256,256]{1,0:T(8,128)(2,1)S(1)}, u32[]{:S(2)}, u32[]{:S(2)}) collective-permute-start(bf16[256,256]{1,0:T(8,128)(2,1)S(1)} %get-tuple-element.56), channel_id=1, source_target_pairs={{12,0},{16,4},{20,8},{24,12},{28,16},{13,1},{17,5},{21,9},{25,13},... | collective-permute-start | bytes 393224 | tf_op jit(solution)/shard_map/ppermute | solution.py:38
  37.0 11.5 %collective-permute-start.9 = (bf16[256,256]{1,0:T(8,128)(2,1)S(1)}, bf16[256,256]{1,0:T(8,128)(2,1)S(1)}, u32[]{:S(2)}, u32[]{:S(2)}) collective-permute-start(bf16[256,256]{1,0:T(8,128)(2,1)S(1)} %get-tuple-element.55), channel_id=1, source_target_pairs={{8,0},{12,4},{16,8},{20,12},{24,16},{28,20},{9,1},{13,5},{17,9},{2... | collective-permute-start | bytes 393224 | tf_op jit(solution)/shard_map/ppermute | solution.py:38
  38.3 10.2 %collective-permute-start.11 = (bf16[128,256]{1,0:T(8,128)(2,1)S(1)}, bf16[128,256]{1,0:T(8,128)(2,1)S(1)}, u32[]{:S(2)}, u32[]{:S(2)}) collective-permute-start(bf16[128,256]{1,0:T(8,128)(2,1)S(1)} %get-tuple-element.57), channel_id=1, source_target_pairs={{16,0},{20,4},{24,8},{28,12},{17,1},{21,5},{25,9},{29,13},{18,2},{... | collective-permute-start | bytes 196616 | tf_op jit(solution)/shard_map/ppermute | solution.py:38

commit v3 on v2

--- a/solution.py
+++ b/solution.py
@@ -19,6 +19,7 @@
 COST = pl.CostEstimate(flops=2**20, bytes_accessed=2**10, transcendentals=0)
 LONG = pl.CostEstimate(flops=2**31, bytes_accessed=2**10, transcendentals=0)
 
+SHORT = pl.CostEstimate(flops=1073741824, bytes_accessed=2**10, transcendentals=0)
 HBM = pl.BlockSpec(memory_space=pltpu.HBM)
 VMEM = pl.BlockSpec(memory_space=pltpu.VMEM)
 SMEM = pl.BlockSpec(memory_space=pltpu.SMEM)
@@ -36,6 +37,11 @@
     devices = lax.axis_size(axis)
     pairs = [(i, i + by) for i in range(devices) if 0 <= i + by < devices]
     return lax.ppermute(array, axis, pairs)
+
+
+def turn(array, axis, by):
+    devices = lax.axis_size(axis)
+    return lax.ppermute(array, axis, [(i, (i + by) % devices) for i in range(devices)])
 
 
 def swap(array, bit, axis="tp"):
@@ -211,14 +217,13 @@
         ref[...] = total.astype(ref.dtype)
 
 
-def backward(doc_ids, qt, q_rows, ot, lse, g, before, taken, kvs, places, window, last_part):
+def backward(doc_ids, qt, q_rows, ot, lse, g, before, taken, kvs, kind, places, window, last_part):
     rows, width = qt.shape
     blocks = rows // BLK
     held = len(places) * BLK
     used = min(held, window * BLK)
     extra = [] if before is None else [before]
     extra += [] if taken is None else [taken[0]]
-    kind = jnp.float32 if last_part else jnp.bfloat16
     dq_kind = jnp.bfloat16 if last_part else jnp.float32
     return pl.pallas_call(
         functools.partial(
@@ -384,6 +389,70 @@
     )(in_hbm(q), in_hbm(cot), cot_c, in_hbm(weight))
 
 
+def add_kernel(*refs):
+    *in_refs, out_ref = refs
+    rows = out_ref.shape[0]
+    out_ref[...] = in_refs[0][...]
+    for ref in in_refs[1:]:
+        count = ref.shape[0]
+        out_ref[pl.ds(rows - count, count), :] += ref[...].astype(jnp.float32)
+
+
+def add_up(arrays, cost):
+    return pl.pallas_call(
+        add_kernel,
+        out_shape=jax.ShapeDtypeStruct(arrays[0].shape, jnp.float32),
+        in_specs=[VMEM] * len(arrays),
+        out_specs=VMEM,
+        compiler_params=pltpu.CompilerParams(vmem_limit_bytes=VMEM_LIMIT),
+        cost_estimate=cost,
+        name="add_up",
+    )(*arrays)
+
+
+def finish_kernel(out_ref, other_ref, own_ref, back_ref, mixed_hbm, dk_hbm, dv_hbm,
+                  mixed, dk, dv, sems):
+    half = mixed.shape[0] // 2
+    copies = [pltpu.make_async_copy(dk, dk_hbm, sems.at[0])]
+    copies.append(pltpu.make_async_copy(dv, dv_hbm, sems.at[1]))
+    total = own_ref[...] + back_ref[...].astype(jnp.float32)
+    dk[...] = total[:, :HEAD_SIZE].astype(dk.dtype)
+    dv[...] = total[:, HEAD_SIZE:].astype(dv.dtype)
+    copies[0].start()
+    copies[1].start()
+    for i in range(2):
+        rows = pl.ds(i * half, half)
+        mixed[rows, :] = (out_ref[rows, :] + other_ref[rows, :].astype(jnp.float32)).astype(
+            mixed.dtype
+        )
+        copies.append(
+            pltpu.make_async_copy(mixed.at[rows, :], mixed_hbm.at[rows, :], sems.at[2 + i])
+        )
+        copies[-1].start()
+    for copy in copies:
+        copy.wait()
+
+
+def finish(out, other, own, back):
+    rows = own.shape[0]
+    kinds = [
+        jax.ShapeDtypeStruct(out.shape, jnp.bfloat16),
+        jax.ShapeDtypeStruct((rows, HEAD_SIZE), jnp.bfloat16),
+        jax.ShapeDtypeStruct((rows, HEAD_SIZE), jnp.bfloat16),
+    ]
+    return pl.pallas_call(
+        finish_kernel,
+        out_shape=kinds,
+        in_specs=[VMEM] * 4,
+        out_specs=[HBM] * 3,
+        scratch_shapes=[pltpu.VMEM(kind.shape, kind.dtype) for kind in kinds]
+        + [pltpu.SemaphoreType.DMA((4,))],
+        compiler_params=pltpu.CompilerParams(vmem_limit_bytes=VMEM_LIMIT),
+        cost_estimate=COST,
+        name="finish",
+    )(out, other, own, back)
+
+
 def on_device(queries, keys, values, out_weight, cotangent, doc_ids):
     rows = queries.shape[0]
     part = cotangent.shape[1]
@@ -401,7 +470,7 @@
     cot_y = swap(cot, 2)
     held = [key_value, None]
     held += [
-        shift(tail if n < blocks else key_value, "ctx", s)
+        (shift if s % 2 else turn)(tail if n < blocks else key_value, "ctx", s)
         for s, n in enumerate(needs[1:], start=2)
     ]
     held[1] = swap(jnp.where(odd == 0, key_value, held[2]), 1, "ctx")
@@ -416,7 +485,8 @@
     def part_back(shards, before, taken, last_part):
         return backward(
             doc_ids, qt, q_rows, ot, lse, grad_attn, before, taken,
-            [held[s] for s in shards], places_of(shards), window, last_part,
+            [held[s] for s in shards], jnp.bfloat16 if shards[0] else jnp.float32,
+            places_of(shards), window, last_part,
         )
 
     shards = list(range(len(needs), 1, -1)) + [0]
@@ -429,29 +499,20 @@
     grad_attn = features_in((2, 3), [cot_y, cot_d], weight, near, jnp.bfloat16)
     out_a = features_out(3, attn, weight, part)
 
-    odds, evens = [list(range(len(needs), 0, -1))[(len(needs) - 1 - i) % 2::2] for i in (0, 1)]
-    dq, *odd_parts = part_back(odds, None, None, False)
-    taken = swap(odd_parts[-1], 1, "ctx")
-    dq, out_a = lax.optimization_barrier((dq, swap(out_a, 1)))
-    out_b = features_out(2, attn, weight, part, [out_a])
+    out_b = features_out(2, attn, weight, part, [swap(out_a, 1)])
     from_y = swap(out_b, 2)
-    dq, *even_parts = part_back(evens, dq, (taken, 1), False)
+    most = list(range(len(needs), 2, -1))
+    dq, *parts = part_back(most + [1], None, None, False)
+    taken = swap(parts[-1], 1, "ctx")
+    parts = dict(zip(most, parts))
+    dq, parts[2] = part_back([2], dq, (taken, 1), False)
     dq, own = part_back([0], dq, (taken, 0), True)
-    parts = dict(zip(odds, odd_parts)) | dict(zip(evens, even_parts))
-    backs = {s: shift(parts[s], "ctx", -s) for s in range(2, len(held))}
+    backs = {s: turn(parts[s], "ctx", -s) for s in range(2, len(held))}
     out_c = features_out(1, attn, weight, part)
     out_d = features_out(0, attn, weight, part, [swap(out_c, 1)], jnp.float32)
-    backs, out_d = lax.optimization_barrier((backs, out_d))
-    for s, back in backs.items():
-        back = back.astype(jnp.float32)
-        own = own + jnp.pad(back, ((rows - back.shape[0], 0), (0, 0)))
-    mixed = (out_d + from_y.astype(jnp.float32)).astype(jnp.bfloat16)
-    return (
-        mixed,
-        dq,
-        own[:, :HEAD_SIZE].astype(jnp.bfloat16),
-        own[:, HEAD_SIZE:].astype(jnp.bfloat16),
-    )
+    own = add_up([own] + [backs[s] for s in most], SHORT)
+    mixed, dk, dv = finish(out_d, from_y, own, backs[2])
+    return (mixed, dq, dk, dv)
 
 
 def solution(mesh):

time: 50.4 us -> 46.1 us (0.915)
  waiting for transfers between devices: 7.61 us -> 4.61 us
  other arithmetic: 1.03 us -> 0.02 us
  Pallas kernels: 19.3 us -> 20.3 us
  local copies, waits for them, and re-layouts: 0.67 us -> 0.01 us
    ppermute x6 -> x1, starting transfers between devices: 14.1 us -> 4.4 us  [shift(): return lax.ppermute(array, axis, pairs)]
    ppermute x0 -> x5, starting transfers between devices: none -> 8.18 us  [turn(): lax.ppermute(array, axis, [(i, (i + by) % devices) for i in range(devices)])]
    ppermute x6 -> x1, waiting for transfers between devices: 5.73 us -> 0.01 us  [shift(): return lax.ppermute(array, axis, pairs)]
    ppermute x8, waiting for transfers between devices: 1.89 us -> 4.45 us  [swap(): lax.ppermute(array, axis, [(i, i ^ bit) for i in range(lax.axis_size(axis...]
    ppermute x8, starting transfers between devices: 6.57 us -> 7.62 us  [swap(): lax.ppermute(array, axis, [(i, i ^ bit) for i in range(lax.axis_size(axis...]
    pallas_call x0 -> x2, Pallas kernels: none -> 1.02 us  [the longest x1 0.99 us: finish(): pl.pallas_call(finish_kernel, out_shape=kinds, in_specs=[VMEM] * 4, out_s...]
    convert_element_type x1 -> x0, other arithmetic: 0.95 us -> none  [on_device(): mixed = (out_d + from_y.astype(jnp.float32)).astype(jnp.bfloat16)]
    slice x1 -> x0, local copies, waits for them, and re-layouts: 0.66 us -> none  [on_device(): own[:, HEAD_SIZE:].astype(jnp.bfloat16)]
  transfers between devices with their start and end apart: 14 -> 14, of which waited for: 2 -> 3; matrix products, arithmetic and copies ran while one was open for 1% -> 0% of each run, Pallas kernels for 37% -> 39%
where the time goes in v3:
time: 46.1 us; the launch traced here: 45.9 us
  Pallas kernels  20.3 us (44%)
  starting transfers between devices  20.2 us (44%)
  waiting for transfers between devices  4.61 us (10%)
  between operations  0.8 us (2%)
    ppermute x5, starting transfers between devices, turn(): lax.ppermute(array, axis, [(i, (i + by) % devices) for i in range(devices)])  8.18 us
    ppermute x8, starting transfers between devices, swap(): lax.ppermute(array, axis, [(i, i ^ bit) for i in range(lax.axis_size(axis...  7.62 us
    pallas_call x3, Pallas kernels, backward(): pl.pallas_call(functools.partial(backward_kernel, window, blocks, places,...  6.78 us
    ppermute x8, waiting for transfers between devices, swap(): lax.ppermute(array, axis, [(i, i ^ bit) for i in range(lax.axis_size(axis...  4.45 us
    ppermute x1, starting transfers between devices, shift(): return lax.ppermute(array, axis, pairs)  4.4 us
    pallas_call x2, Pallas kernels, forward(): pl.pallas_call(functools.partial(forward_kernel, window, blocks, places,...  4.16 us
    pallas_call x1, Pallas kernels, prepare(): pl.pallas_call(prepare_kernel, out_shape=[jax.ShapeDtypeStruct((rows, wid...  3.43 us
    pallas_call x4, Pallas kernels, features_out(): pl.pallas_call(functools.partial(features_out_kernel, which), out_shape=j...  2.78 us
  transfers between devices with their start and end apart: 14, of which 3 were waited for; matrix products, arithmetic and copies ran while one was open for 0% of the time, Pallas kernels for 39%

profile of v3, /device:TPU:0, one launch (start us, length us, event | category | flops | bytes accessed | tf_op | source)
XLA Modules:
  0.0 45.9 jit_solution(12080021224040032538)
XLA Ops:
  0.6 0.0 copy-start
  0.6 0.9 %join.1 = (bf16[256,256]{1,0:T(8,128)(2,1)S(1)}, bf16[128,256]{1,0:T(8,128)(2,1)S(1)}) custom-call(bf16[256,128]{1,0:T(8,128)(2,1)} %k_hbm.1, bf16[256,128]{1,0:T(8,128)(2,1)} %v_hbm.1), custom_call_target="tpu_custom_call" | custom-call | flops 1048576 | bytes 1024 | tf_op jit(solution)/shard_map/join/pallas_call | solution.py:325
  1.6 0.5 %collective-permute-start = (bf16[256,1280]{1,0:T(8,128)(2,1)}, bf16[256,1280]{1,0:T(8,128)(2,1)S(1)}, u32[]{:S(2)}, u32[]{:S(2)}) collective-permute-start(bf16[256,1280]{1,0:T(8,128)(2,1)} %cot_hbm), channel_id=1, source_target_pairs={{0,1},{1,0},{2,3},{3,2},{4,5},{5,4},{6,7},{7,6},{8,9},{9,8},{10,11... | collective-permute-start | bytes 1966088 | tf_op jit(solution)/shard_map/ppermute | solution.py:48
  2.1 2.6 %collective-permute-start.5 = (bf16[256,1280]{1,0:T(8,128)(2,1)}, bf16[256,1280]{1,0:T(8,128)(2,1)S(1)}, u32[]{:S(2)}, u32[]{:S(2)}) collective-permute-start(bf16[256,1280]{1,0:T(8,128)(2,1)} %cot_hbm), channel_id=1, source_target_pairs={{0,2},{1,3},{2,0},{3,1},{4,6},{5,7},{6,4},{7,5},{8,10},{9,11},{10,... | collective-permute-start | bytes 1966088 | tf_op jit(solution)/shard_map/ppermute | solution.py:48
  4.7 1.6 %collective-permute-start.3 = (bf16[256,256]{1,0:T(8,128)(2,1)S(1)}, bf16[256,256]{1,0:T(8,128)(2,1)S(1)}, u32[]{:S(2)}, u32[]{:S(2)}) collective-permute-start(bf16[256,256]{1,0:T(8,128)(2,1)S(1)} %get-tuple-element.37.refs_3_.refs_2_), channel_id=1, source_target_pairs={{0,8},{4,12},{8,16},{12,20},{16,24},{20,28},{24,0},{28,4},{1,9},{5... | collective-permute-start | bytes 393224 | tf_op jit(solution)/shard_map/ppermute | solution.py:44
  6.3 4.4 %collective-permute-start.2 = (bf16[256,256]{1,0:T(8,128)(2,1)S(1)}, bf16[256,256]{1,0:T(8,128)(2,1)S(1)}, u32[]{:S(2)}, u32[]{:S(2)}) collective-permute-start(bf16[256,256]{1,0:T(8,128)(2,1)S(1)} %get-tuple-element.37.refs_3_.refs_2_), channel_id=1, source_target_pairs={{0,12},{4,16},{8,20},{12,24},{16,28},{1,13},{5,17},{9,21},{13,25},... | collective-permute-start | bytes 393224 | tf_op jit(solution)/shard_map/ppermute | solution.py:39
  10.7 1.3 %collective-permute-start.1 = (bf16[128,256]{1,0:T(8,128)(2,1)S(1)}, bf16[128,256]{1,0:T(8,128)(2,1)S(1)}, u32[]{:S(2)}, u32[]{:S(2)}) collective-permute-start(bf16[128,256]{1,0:T(8,128)(2,1)S(1)} %get-tuple-element.36), channel_id=1, source_target_pairs={{0,16},{4,20},{8,24},{12,28},{16,0},{20,4},{24,8},{28,12},{1,17},{... | collective-permute-start | bytes 196616 | tf_op jit(solution)/shard_map/ppermute | solution.py:44
  12.0 0.1 collective-permute-done.3.refs_2_
  12.1 1.6 %collective-permute-start.4 = (bf16[256,256]{1,0:T(8,128)(2,1)S(1)}, bf16[256,256]{1,0:T(8,128)(2,1)S(1)}, u32[]{:S(2)}, u32[]{:S(2)}) collective-permute-start(bf16[256,256]{1,0:T(8,128)(2,1)S(1)} %broadcast_select_fusion), channel_id=1, source_target_pairs={{0,4},{4,0},{8,12},{12,8},{16,20},{20,16},{24,28},{28,24},{1,5},{5... | collective-permute-start | bytes 393224 | tf_op jit(solution)/shard_map/ppermute | solution.py:48
  13.7 0.0 collective-permute-done.cot_c_ref
  13.7 3.4 %prepare.1 = (f32[256,640]{1,0:T(8,128)S(1)}, bf16[640,5120]{1,0:T(8,128)(2,1)S(1)}, bf16[256,640]{1,0:T(8,128)(2,1)S(1)}, bf16[1280,128]{1,0:T(8,128)(2,1)S(1)}) custom-call(bf16[256,640]{1,0:T(8,128)(2,1)} %q_hbm.1, bf16[256,1280]{1,0:T(8,128)(2,1)} %cot_hbm, bf16[256,1280]{1,0:T(8,128)(2,1)S(1)} %collective-permute-done.cot_c_ref, bf16[640,5120]{1,0:T(8,128)(2,1)} %w_hbm.1), custom_call_target="tpu_custom_call" | custom-call | flops 1048576 | bytes 1024 | tf_op jit(solution)/shard_map/prepare/pallas_call | solution.py:371
  17.1 0.0 collective-permute-done.1.refs_0_
  17.1 0.0 collective-permute-done.2.refs_1_
  17.1 0.0 copy-done
  17.2 2.6 %forward.2 = (f32[256,640]{1,0:T(8,128)S(1)}, f32[2,640]{1,0:T(2,128)S(1)}, f32[2,640]{1,0:T(2,128)S(1)}) custom-call(s32[16]{0:T(128)S(1)} %copy-done, bf16[256,640]{1,0:T(8,128)(2,1)S(1)} %get-tuple-element.35.qt_ref, bf16[128,256]{1,0:T(8,128)(2,1)S(1)} %collective-permute-done.1.refs_0_, bf16[256,256]{1,0:T(8,128)(2,1)S(1)} %collective-permute-done.2.refs_1_, ...), custom_call_target="tpu_custom_call" | custom-call | flops 2147483648 | bytes 1024 | tf_op jit(solution)/shard_map/forward/pallas_call | solution.py:131
  19.7 0.0 collective-permute-done.4.refs_3_.refs_2_
  19.8 1.6 %forward.3 = (bf16[256,640]{1,0:T(8,128)(2,1)S(1)}, bf16[256,640]{1,0:T(8,128)(2,1)S(1)}, f32[2,640]{1,0:T(2,128)S(1)}) custom-call(s32[16]{0:T(128)S(1)} %copy-done, bf16[256,640]{1,0:T(8,128)(2,1)S(1)} %get-tuple-element.35.qt_ref, f32[256,640]{1,0:T(8,128)S(1)} %get-tuple-element.38.refs_0_, f32[2,640]{1,0:T(2,128)S(1)} %get-tuple-element.39.refs_1_, ...), custom_call_target="tpu_custom_call" | custom-call | flops 1048576 | bytes 1024 | tf_op jit(solution)/shard_map/forward/pallas_call | solution.py:131
  21.3 0.0 collective-permute-done.5.refs_0_
  21.4 0.7 %features_out.6 = bf16[256,1280]{1,0:T(8,128)(2,1)S(1)} custom-call(bf16[256,640]{1,0:T(8,128)(2,1)S(1)} %get-tuple-element.42.attn_ref, bf16[640,5120]{1,0:T(8,128)(2,1)S(1)} %get-tuple-element.43.refs_0_.refs_1_.refs_3_), custom_call_target="tpu_custom_call" | custom-call | flops 1048576 | bytes 1024 | tf_op jit(solution)/shard_map/features_out/pallas_call | solution.py:296
  22.1 0.1 collective-permute-start.7
  22.1 0.5 %collective-permute-start.9 = (bf16[256,1280]{1,0:T(8,128)(2,1)S(1)}, bf16[256,1280]{1,0:T(8,128)(2,1)S(1)}, u32[]{:S(2)}, u32[]{:S(2)}) collective-permute-start(bf16[256,1280]{1,0:T(8,128)(2,1)S(1)} %collective-permute-done.5.refs_0_), channel_id=1, source_target_pairs={{0,1},{1,0},{2,3},{3,2},{4,5},{5,4},{6,7},{7,6},{8,9},{9,8},{10,11... | collective-permute-start | bytes 1966088 | tf_op jit(solution)/shard_map/ppermute | solution.py:48
  22.6 0.7 %features_out.4 = bf16[256,1280]{1,0:T(8,128)(2,1)S(1)} custom-call(bf16[256,640]{1,0:T(8,128)(2,1)S(1)} %get-tuple-element.42.attn_ref, bf16[640,5120]{1,0:T(8,128)(2,1)S(1)} %get-tuple-element.43.refs_0_.refs_1_.refs_3_), custom_call_target="tpu_custom_call" | custom-call | flops 1048576 | bytes 1024 | tf_op jit(solution)/shard_map/features_out/pallas_call | solution.py:296
  23.3 0.1 collective-permute-start.6
  23.5 0.7 %collective-permute-done.7.refs_0_ = bf16[256,1280]{1,0:T(8,128)(2,1)S(1)} collective-permute-done((bf16[256,1280]{1,0:T(8,128)(2,1)S(1)}, bf16[256,1280]{1,0:T(8,128)(2,1)S(1)}, u32[]{:S(2)}, u32[]{:S(2)}) %collective-permute-start.7) | collective-permute-done | bytes 655392 | tf_op jit(solution)/shard_map/ppermute | solution.py:48
  24.2 0.7 %features_out.7 = bf16[256,1280]{1,0:T(8,128)(2,1)S(1)} custom-call(bf16[256,640]{1,0:T(8,128)(2,1)S(1)} %get-tuple-element.42.attn_ref, bf16[256,1280]{1,0:T(8,128)(2,1)S(1)} %collective-permute-done.7.refs_0_, bf16[640,5120]{1,0:T(8,128)(2,1)S(1)} %get-tuple-element.43.refs_0_.refs_1_.refs_3_), custom_call_target="tpu_custom_call" | custom-call | flops 1048576 | bytes 1024 | tf_op jit(solution)/shard_map/features_out/pallas_call | solution.py:296
  24.9 0.7 %collective-permute-start.8 = (bf16[256,1280]{1,0:T(8,128)(2,1)S(1)}, bf16[256,1280]{1,0:T(8,128)(2,1)S(1)}, u32[]{:S(2)}, u32[]{:S(2)}) collective-permute-start(bf16[256,1280]{1,0:T(8,128)(2,1)S(1)} %features_out.7), channel_id=1, source_target_pairs={{0,2},{1,3},{2,0},{3,1},{4,6},{5,7},{6,4},{7,5},{8,10},{9,11},{10,... | collective-permute-start | bytes 1966088 | tf_op jit(solution)/shard_map/ppermute | solution.py:48
  25.6 0.0 collective-permute-done.9.refs_1_
  25.6 1.2 %features_in.1.g_ref = bf16[256,640]{1,0:T(8,128)(2,1)S(1)} custom-call(bf16[256,1280]{1,0:T(8,128)(2,1)S(1)} %collective-permute-done.5.refs_0_, bf16[256,1280]{1,0:T(8,128)(2,1)S(1)} %collective-permute-done.9.refs_1_, f32[256,640]{1,0:T(8,128)S(1)} %get-tuple-element.48.refs_2_, bf16[640,5120]{1,0:T(8,128)(2,1)S(1)} %get-tuple-element.43.refs_0_.refs_1_.refs_3_), custom_call_target="tpu_custom_call" | custom-call | flops 1048576 | bytes 1024 | tf_op jit(solution)/shard_map/features_in/pallas_call | solution.py:275
  26.8 2.7 %backward.3 = (f32[256,640]{1,0:T(8,128)S(1)}, bf16[128,256]{1,0:T(8,128)(2,1)S(1)}, bf16[256,256]{1,0:T(8,128)(2,1)S(1)}, bf16[256,256]{1,0:T(8,128)(2,1)S(1)}) custom-call(s32[16]{0:T(128)S(1)} %copy-done, bf16[256,640]{1,0:T(8,128)(2,1)S(1)} %get-tuple-element.35.qt_ref, bf16[1280,128]{1,0:T(8,128)(2,1)S(1)} %get-tuple-element.44.q_rows_ref, ...), custom_call_target="tpu_custom_call" | custom-call | flops 1048576 | bytes 1024 | tf_op jit(solution)/shard_map/backward/pallas_call | solution.py:228
  29.5 1.6 %collective-permute-start.10 = (bf16[256,256]{1,0:T(8,128)(2,1)S(1)}, bf16[256,256]{1,0:T(8,128)(2,1)S(1)}, u32[]{:S(2)}, u32[]{:S(2)}) collective-permute-start(bf16[256,256]{1,0:T(8,128)(2,1)S(1)} %get-tuple-element.50), channel_id=1, source_target_pairs={{0,4},{4,0},{8,12},{12,8},{16,20},{20,16},{24,28},{28,24},{1,5},{5... | collective-permute-start | bytes 393224 | tf_op jit(solution)/shard_map/ppermute | solution.py:48
  31.1 2.6 %collective-permute-start.12 = (bf16[256,256]{1,0:T(8,128)(2,1)S(1)}, bf16[256,256]{1,0:T(8,128)(2,1)S(1)}, u32[]{:S(2)}, u32[]{:S(2)}) collective-permute-start(bf16[256,256]{1,0:T(8,128)(2,1)S(1)} %get-tuple-element.54), channel_id=1, source_target_pairs={{0,20},{4,24},{8,28},{12,0},{16,4},{20,8},{24,12},{28,16},{1,21},{... | collective-permute-start | bytes 393224 | tf_op jit(solution)/shard_map/ppermute | solution.py:44
  33.6 0.3 collective-permute-start.11
  33.9 3.7 %collective-permute-done.10.refs_1_ = bf16[256,256]{1,0:T(8,128)(2,1)S(1)} collective-permute-done((bf16[256,256]{1,0:T(8,128)(2,1)S(1)}, bf16[256,256]{1,0:T(8,128)(2,1)S(1)}, u32[]{:S(2)}, u32[]{:S(2)}) %collective-permute-start.10) | collective-permute-done | bytes 131104 | tf_op jit(solution)/shard_map/ppermute | solution.py:48
  37.6 1.7 %backward.4 = (f32[256,640]{1,0:T(8,128)S(1)}, bf16[256,256]{1,0:T(8,128)(2,1)S(1)}) custom-call(s32[16]{0:T(128)S(1)} %copy-done, bf16[256,640]{1,0:T(8,128)(2,1)S(1)} %get-tuple-element.35.qt_ref, bf16[1280,128]{1,0:T(8,128)(2,1)S(1)} %get-tuple-element.44.q_rows_ref, bf16[256,640]{1,0:T(8,128)(2,1)S(1)} %get-tuple-element.45.ot_ref, ...), custom_call_target="tpu_custom_call" | custom-call | flops 1048576 | bytes 1024 | tf_op jit(solution)/shard_map/backward/pallas_call | solution.py:228
  39.3 2.4 %collective-permute-start.13 = (bf16[256,256]{1,0:T(8,128)(2,1)S(1)}, bf16[256,256]{1,0:T(8,128)(2,1)S(1)}, u32[]{:S(2)}, u32[]{:S(2)}) collective-permute-start(bf16[256,256]{1,0:T(8,128)(2,1)S(1)} %get-tuple-element.55), channel_id=1, source_target_pairs={{0,24},{4,28},{8,0},{12,4},{16,8},{20,12},{24,16},{28,20},{1,25},{... | collective-permute-start | bytes 393224 | tf_op jit(solution)/shard_map/ppermute | solution.py:44
  41.8 0.0 collective-permute-done.6.refs_0_
  41.8 0.7 %features_out.5.out_ref = f32[256,1280]{1,0:T(8,128)S(1)} custom-call(bf16[256,640]{1,0:T(8,128)(2,1)S(1)} %get-tuple-element.42.attn_ref, bf16[256,1280]{1,0:T(8,128)(2,1)S(1)} %collective-permute-done.6.refs_0_, bf16[640,5120]{1,0:T(8,128)(2,1)S(1)} %get-tuple-element.43.refs_0_.refs_1_.refs_3_), custom_call_target="tpu_custom_call" | custom-call | flops 1048576 | bytes 1024 | tf_op jit(solution)/shard_map/features_out/pallas_call | solution.py:296
  42.5 2.4 %backward.5 = (bf16[256,640]{1,0:T(8,128)(2,1)}, f32[256,256]{1,0:T(8,128)S(1)}) custom-call(s32[16]{0:T(128)S(1)} %copy-done, bf16[256,640]{1,0:T(8,128)(2,1)S(1)} %get-tuple-element.35.qt_ref, bf16[1280,128]{1,0:T(8,128)(2,1)S(1)} %get-tuple-element.44.q_rows_ref, bf16[256,640]{1,0:T(8,128)(2,1)S(1)} %get-tuple-element.45.ot_ref, ...), custom_call_target="tpu_custom_call" | custom-call | flops 1048576 | bytes 1024 | tf_op jit(solution)/shard_map/backward/pallas_call | solution.py:228
  44.9 0.0 collective-permute-done.11.refs_1_
  44.9 0.0 collective-permute-done.12.refs_2_
  44.9 0.0 collective-permute-done.13.back_ref
  45.0 0.0 collective-permute-done.8.other_ref
  45.0 1.0 %finish.1 = (bf16[256,1280]{1,0:T(8,128)(2,1)}, bf16[256,128]{1,0:T(8,128)(2,1)}, bf16[256,128]{1,0:T(8,128)(2,1)}) custom-call(f32[256,1280]{1,0:T(8,128)S(1)} %features_out.5.out_ref, bf16[256,1280]{1,0:T(8,128)(2,1)S(1)} %collective-permute-done.8.other_ref, f32[256,256]{1,0:T(8,128)S(1)} %add_up.1.own_ref, ...), custom_call_target="tpu_custom_call" | custom-call | flops 1048576 | bytes 1024 | tf_op jit(solution)/shard_map/finish/pallas_call | solution.py:443
  (2 shorter events, 0.1 us)
Async XLA Ops:
  0.6 16.5 %copy-start = (s32[16]{0:T(128)S(1)}, s32[16]{0:T(128)}, u32[]{:S(2)}) copy-start(s32[16]{0:T(128)} %doc_ref.9) | copy-start | bytes 196
  1.6 12.1 %collective-permute-start = (bf16[256,1280]{1,0:T(8,128)(2,1)}, bf16[256,1280]{1,0:T(8,128)(2,1)S(1)}, u32[]{:S(2)}, u32[]{:S(2)}) collective-permute-start(bf16[256,1280]{1,0:T(8,128)(2,1)} %cot_hbm), channel_id=1, source_target_pairs={{0,1},{1,0},{2,3},{3,2},{4,5},{5,4},{6,7},{7,6},{8,9},{9,8},{10,11... | collective-permute-start | bytes 1966088 | tf_op jit(solution)/shard_map/ppermute | solution.py:48
  2.1 19.3 %collective-permute-start.5 = (bf16[256,1280]{1,0:T(8,128)(2,1)}, bf16[256,1280]{1,0:T(8,128)(2,1)S(1)}, u32[]{:S(2)}, u32[]{:S(2)}) collective-permute-start(bf16[256,1280]{1,0:T(8,128)(2,1)} %cot_hbm), channel_id=1, source_target_pairs={{0,2},{1,3},{2,0},{3,1},{4,6},{5,7},{6,4},{7,5},{8,10},{9,11},{10,... | collective-permute-start | bytes 1966088 | tf_op jit(solution)/shard_map/ppermute | solution.py:48
  4.7 7.4 %collective-permute-start.3 = (bf16[256,256]{1,0:T(8,128)(2,1)S(1)}, bf16[256,256]{1,0:T(8,128)(2,1)S(1)}, u32[]{:S(2)}, u32[]{:S(2)}) collective-permute-start(bf16[256,256]{1,0:T(8,128)(2,1)S(1)} %get-tuple-element.37.refs_3_.refs_2_), channel_id=1, source_target_pairs={{0,8},{4,12},{8,16},{12,20},{16,24},{20,28},{24,0},{28,4},{1,9},{5... | collective-permute-start | bytes 393224 | tf_op jit(solution)/shard_map/ppermute | solution.py:44
  6.3 10.9 %collective-permute-start.2 = (bf16[256,256]{1,0:T(8,128)(2,1)S(1)}, bf16[256,256]{1,0:T(8,128)(2,1)S(1)}, u32[]{:S(2)}, u32[]{:S(2)}) collective-permute-start(bf16[256,256]{1,0:T(8,128)(2,1)S(1)} %get-tuple-element.37.refs_3_.refs_2_), channel_id=1, source_target_pairs={{0,12},{4,16},{8,20},{12,24},{16,28},{1,13},{5,17},{9,21},{13,25},... | collective-permute-start | bytes 393224 | tf_op jit(solution)/shard_map/ppermute | solution.py:39
  10.7 6.5 %collective-permute-start.1 = (bf16[128,256]{1,0:T(8,128)(2,1)S(1)}, bf16[128,256]{1,0:T(8,128)(2,1)S(1)}, u32[]{:S(2)}, u32[]{:S(2)}) collective-permute-start(bf16[128,256]{1,0:T(8,128)(2,1)S(1)} %get-tuple-element.36), channel_id=1, source_target_pairs={{0,16},{4,20},{8,24},{12,28},{16,0},{20,4},{24,8},{28,12},{1,17},{... | collective-permute-start | bytes 196616 | tf_op jit(solution)/shard_map/ppermute | solution.py:44
  12.1 7.6 %collective-permute-start.4 = (bf16[256,256]{1,0:T(8,128)(2,1)S(1)}, bf16[256,256]{1,0:T(8,128)(2,1)S(1)}, u32[]{:S(2)}, u32[]{:S(2)}) collective-permute-start(bf16[256,256]{1,0:T(8,128)(2,1)S(1)} %broadcast_select_fusion), channel_id=1, source_target_pairs={{0,4},{4,0},{8,12},{12,8},{16,20},{20,16},{24,28},{28,24},{1,5},{5... | collective-permute-start | bytes 393224 | tf_op jit(solution)/shard_map/ppermute | solution.py:48
  22.1 2.2 %collective-permute-start.7 = (bf16[256,1280]{1,0:T(8,128)(2,1)S(1)}, bf16[256,1280]{1,0:T(8,128)(2,1)S(1)}, u32[]{:S(2)}, u32[]{:S(2)}) collective-permute-start(bf16[256,1280]{1,0:T(8,128)(2,1)S(1)} %features_out.6), channel_id=1, source_target_pairs={{0,1},{1,0},{2,3},{3,2},{4,5},{5,4},{6,7},{7,6},{8,9},{9,8},{10,11... | collective-permute-start | bytes 1966088 | tf_op jit(solution)/shard_map/ppermute | solution.py:48
  22.1 3.5 %collective-permute-start.9 = (bf16[256,1280]{1,0:T(8,128)(2,1)S(1)}, bf16[256,1280]{1,0:T(8,128)(2,1)S(1)}, u32[]{:S(2)}, u32[]{:S(2)}) collective-permute-start(bf16[256,1280]{1,0:T(8,128)(2,1)S(1)} %collective-permute-done.5.refs_0_), channel_id=1, source_target_pairs={{0,1},{1,0},{2,3},{3,2},{4,5},{5,4},{6,7},{7,6},{8,9},{9,8},{10,11... | collective-permute-start | bytes 1966088 | tf_op jit(solution)/shard_map/ppermute | solution.py:48
  23.3 18.4 %collective-permute-start.6 = (bf16[256,1280]{1,0:T(8,128)(2,1)S(1)}, bf16[256,1280]{1,0:T(8,128)(2,1)S(1)}, u32[]{:S(2)}, u32[]{:S(2)}) collective-permute-start(bf16[256,1280]{1,0:T(8,128)(2,1)S(1)} %features_out.4), channel_id=1, source_target_pairs={{0,1},{1,0},{2,3},{3,2},{4,5},{5,4},{6,7},{7,6},{8,9},{9,8},{10,11... | collective-permute-start | bytes 1966088 | tf_op jit(solution)/shard_map/ppermute | solution.py:48
  24.9 20.0 %collective-permute-start.8 = (bf16[256,1280]{1,0:T(8,128)(2,1)S(1)}, bf16[256,1280]{1,0:T(8,128)(2,1)S(1)}, u32[]{:S(2)}, u32[]{:S(2)}) collective-permute-start(bf16[256,1280]{1,0:T(8,128)(2,1)S(1)} %features_out.7), channel_id=1, source_target_pairs={{0,2},{1,3},{2,0},{3,1},{4,6},{5,7},{6,4},{7,5},{8,10},{9,11},{10,... | collective-permute-start | bytes 1966088 | tf_op jit(solution)/shard_map/ppermute | solution.py:48
  29.5 8.1 %collective-permute-start.10 = (bf16[256,256]{1,0:T(8,128)(2,1)S(1)}, bf16[256,256]{1,0:T(8,128)(2,1)S(1)}, u32[]{:S(2)}, u32[]{:S(2)}) collective-permute-start(bf16[256,256]{1,0:T(8,128)(2,1)S(1)} %get-tuple-element.50), channel_id=1, source_target_pairs={{0,4},{4,0},{8,12},{12,8},{16,20},{20,16},{24,28},{28,24},{1,5},{5... | collective-permute-start | bytes 393224 | tf_op jit(solution)/shard_map/ppermute | solution.py:48
  31.1 13.8 %collective-permute-start.12 = (bf16[256,256]{1,0:T(8,128)(2,1)S(1)}, bf16[256,256]{1,0:T(8,128)(2,1)S(1)}, u32[]{:S(2)}, u32[]{:S(2)}) collective-permute-start(bf16[256,256]{1,0:T(8,128)(2,1)S(1)} %get-tuple-element.54), channel_id=1, source_target_pairs={{0,20},{4,24},{8,28},{12,0},{16,4},{20,8},{24,12},{28,16},{1,21},{... | collective-permute-start | bytes 393224 | tf_op jit(solution)/shard_map/ppermute | solution.py:44
  33.6 11.3 %collective-permute-start.11 = (bf16[128,256]{1,0:T(8,128)(2,1)S(1)}, bf16[128,256]{1,0:T(8,128)(2,1)S(1)}, u32[]{:S(2)}, u32[]{:S(2)}) collective-permute-start(bf16[128,256]{1,0:T(8,128)(2,1)S(1)} %get-tuple-element.53), channel_id=1, source_target_pairs={{0,16},{4,20},{8,24},{12,28},{16,0},{20,4},{24,8},{28,12},{1,17},{... | collective-permute-start | bytes 196616 | tf_op jit(solution)/shard_map/ppermute | solution.py:44
  39.3 5.6 %collective-permute-start.13 = (bf16[256,256]{1,0:T(8,128)(2,1)S(1)}, bf16[256,256]{1,0:T(8,128)(2,1)S(1)}, u32[]{:S(2)}, u32[]{:S(2)}) collective-permute-start(bf16[256,256]{1,0:T(8,128)(2,1)S(1)} %get-tuple-element.55), channel_id=1, source_target_pairs={{0,24},{4,28},{8,0},{12,4},{16,8},{20,12},{24,16},{28,20},{1,25},{... | collective-permute-start | bytes 393224 | tf_op jit(solution)/shard_map/ppermute | solution.py:44

commit v4 on v3

--- a/solution.py
+++ b/solution.py
@@ -105,11 +105,11 @@
             out, total = out * factor + fresh, total * factor + sums
         if last_part:
             attn_ref, ot_ref, lse_ref = out_refs
-            out = out / total
-            ot_ref[block(b), :] = out.astype(jnp.bfloat16)
+            out = (out / total).astype(jnp.bfloat16)
+            ot_ref[block(b), :] = out
             lse_ref[pl.ds(b, 1), :] = top + jnp.log2(total)
             for h in range(heads):
-                attn_ref[block(b), block(h)] = out[:, h * BLK:(h + 1) * BLK].T.astype(jnp.bfloat16)
+                attn_ref[block(b), block(h)] = out[:, h * BLK:(h + 1) * BLK].T
         else:
             out_ref, top_ref, total_ref = out_refs
             out_ref[block(b), :] = out
@@ -147,14 +147,14 @@
 
 def backward_kernel(
     window, blocks, places, first_part, last_part, taking,
-    doc_ref, qt_ref, q_rows_ref, ot_ref, lse_ref, g_ref, *refs
+    doc_ref, qt_ref, q_rows_ref, lse_ref, gt_ref, g_rows_ref, delta_ref, *refs
 ):
     refs = list(refs)
     before_ref = None if first_part else refs.pop(0)
     taken_ref = None if taking is None else refs.pop(0)
-    n = (len(refs) - 9) // 2
+    n = (len(refs) - 7) // 2
     kv_refs, dq_ref, dkv_refs = refs[:n], refs[n], refs[n + 1:2 * n + 1]
-    k_all, kt_all, v_all, g_rows, gt, p_all, ds_all, dkv_all = refs[2 * n + 1:]
+    k_all, kt_all, v_all, p_all, ds_all, dkv_all = refs[2 * n + 1:]
     width = qt_ref.shape[1]
     heads = width // HEAD_SIZE
     me = lax.axis_index("ctx")
@@ -168,15 +168,8 @@
         at += rows
     dkv_all[...] = jnp.zeros_like(dkv_all)
     for b in range(blocks):
-        for h in range(heads):
-            g = g_ref[block(b), block(h)]
-            g_rows[block(h), :] = g
-            gt[:, block(h)] = g.T
-        qt = qt_ref[block(b), :]
-        delta = jnp.sum(
-            gt[...].astype(jnp.float32) * ot_ref[block(b), :].astype(jnp.float32),
-            axis=0, keepdims=True,
-        )
+        qt, gt = qt_ref[block(b), :], gt_ref[block(b), :]
+        delta = delta_ref[pl.ds(b, 1), :]
         lse = lse_ref[pl.ds(b, 1), :]
         inside = [i for i, place in enumerate(places) if b <= place < b + window]
         if not inside:
@@ -193,18 +186,19 @@
                 s = jnp.where(causal(width), s, LOW)
             p = jnp.exp2(s - jnp.where(ok, lse, HIGH))
             p_all[block(i - start), :] = p.astype(jnp.bfloat16)
-            dp = dot(v_all[block(i), :], gt[...])
+            dp = dot(v_all[block(i), :], gt)
             ds_all[block(i - start), :] = (p * (dp - delta)).astype(jnp.bfloat16)
         mine, used = block(start, stop - start), block(0, stop - start)
-        q_rows = q_rows_ref[pl.ds(b * width, width), :]
-        dkv_all[mine, :HEAD_SIZE] += dot(ds_all[used, :], q_rows) * SCALE
-        dkv_all[mine, HEAD_SIZE:] += dot(p_all[used, :], g_rows[...])
+        stacked = pl.ds(b * width, width)
+        dkv_all[mine, :HEAD_SIZE] += dot(ds_all[used, :], q_rows_ref[stacked, :]) * SCALE
+        dkv_all[mine, HEAD_SIZE:] += dot(p_all[used, :], g_rows_ref[stacked, :])
         dqt = dot(kt_all[:, mine], ds_all[used, :]) * SCALE
         if not first_part:
             dqt += before_ref[block(b), :]
         if last_part:
+            dqt = dqt.astype(jnp.bfloat16)
             for h in range(heads):
-                dq_ref[block(b), block(h)] = dqt[:, h * BLK:(h + 1) * BLK].T.astype(jnp.bfloat16)
+                dq_ref[block(b), block(h)] = dqt[:, h * BLK:(h + 1) * BLK].T
         else:
             dq_ref[block(b), :] = dqt
     at = 0
@@ -217,7 +211,7 @@
         ref[...] = total.astype(ref.dtype)
 
 
-def backward(doc_ids, qt, q_rows, ot, lse, g, before, taken, kvs, kind, places, window, last_part):
+def backward(doc_ids, qt, q_rows, lse, grads, before, taken, kvs, kind, places, window, last_part):
     rows, width = qt.shape
     blocks = rows // BLK
     held = len(places) * BLK
@@ -232,14 +226,12 @@
         ),
         out_shape=[jax.ShapeDtypeStruct((rows, width), dq_kind)]
         + [jax.ShapeDtypeStruct(kv.shape, kind) for kv in kvs],
-        in_specs=[SMEM] + [VMEM] * (5 + len(extra) + len(kvs)),
+        in_specs=[SMEM] + [VMEM] * (6 + len(extra) + len(kvs)),
         out_specs=[VMEM] * (1 + len(kvs)),
         scratch_shapes=[
             pltpu.VMEM((held, HEAD_SIZE), jnp.bfloat16),
             pltpu.VMEM((HEAD_SIZE, held), jnp.bfloat16),
             pltpu.VMEM((held, HEAD_SIZE), jnp.bfloat16),
-            pltpu.VMEM((width, HEAD_SIZE), jnp.bfloat16),
-            pltpu.VMEM((HEAD_SIZE, width), jnp.bfloat16),
             pltpu.VMEM((used, width), jnp.bfloat16),
             pltpu.VMEM((used, width), jnp.bfloat16),
             pltpu.VMEM((held, 2 * HEAD_SIZE), jnp.float32),
@@ -247,7 +239,7 @@
         compiler_params=pltpu.CompilerParams(vmem_limit_bytes=VMEM_LIMIT),
         cost_estimate=COST,
         name="backward",
-    )(doc_ids, qt, q_rows, ot, lse, g, *extra, *kvs)
+    )(doc_ids, qt, q_rows, lse, *grads, *extra, *kvs)
 
 
 def part_of(w_ref, which, part):
@@ -256,31 +248,43 @@
 
 
 def features_in_kernel(which, *refs):
-    *cots, w_ref, out_ref = refs
-    part = cots[0].shape[1]
-    total = None if len(cots) == len(which) else cots[-1][...]
+    *cots, near_ref, w_ref, ot_ref, gt_ref, g_rows_ref, delta_ref = refs
+    rows, part = cots[0].shape
+    width = near_ref.shape[1]
+    total = near_ref[...]
     for j, cot in zip(which, cots):
-        product = lax.dot_general(
+        total += lax.dot_general(
             cot[...], part_of(w_ref, j, part), (((1,), (1,)), ((), ())),
             preferred_element_type=jnp.float32,
         )
-        total = product if total is None else total + product
-    out_ref[...] = total.astype(out_ref.dtype)
-
-
-def features_in(which, cots, weight, base, dtype):
-    rows, part = cots[0].shape
-    depth = weight.shape[0]
-    extra = [] if base is None else [base]
+    grad = total.astype(jnp.bfloat16)
+    for b in range(rows // BLK):
+        for h in range(width // BLK):
+            g = grad[b * BLK:(b + 1) * BLK, h * BLK:(h + 1) * BLK]
+            g_rows_ref[pl.ds(b * width + h * BLK, BLK), :] = g
+            gt_ref[block(b), block(h)] = g.T
+        delta_ref[pl.ds(b, 1), :] = jnp.sum(
+            gt_ref[block(b), :].astype(jnp.float32) * ot_ref[block(b), :].astype(jnp.float32),
+            axis=0, keepdims=True,
+        )
+
+
+def features_in(which, cots, weight, near, ot):
+    rows, width = near.shape
+    blocks = rows // BLK
     return pl.pallas_call(
         functools.partial(features_in_kernel, which),
-        out_shape=jax.ShapeDtypeStruct((rows, depth), dtype),
-        in_specs=[VMEM] * (len(cots) + len(extra) + 1),
-        out_specs=VMEM,
+        out_shape=[
+            jax.ShapeDtypeStruct((rows, width), jnp.bfloat16),
+            jax.ShapeDtypeStruct((blocks * width, BLK), jnp.bfloat16),
+            jax.ShapeDtypeStruct((blocks, width), jnp.float32),
+        ],
+        in_specs=[VMEM] * (len(cots) + 3),
+        out_specs=[VMEM] * 3,
         compiler_params=pltpu.CompilerParams(vmem_limit_bytes=VMEM_LIMIT),
         cost_estimate=COST,
         name="features_in",
-    )(*cots, *extra, weight)
+    )(*cots, near, weight, ot)
 
 
 def features_out_kernel(which, attn_ref, *refs):
@@ -484,7 +488,7 @@
 
     def part_back(shards, before, taken, last_part):
         return backward(
-            doc_ids, qt, q_rows, ot, lse, grad_attn, before, taken,
+            doc_ids, qt, q_rows, lse, grads, before, taken,
             [held[s] for s in shards], jnp.bfloat16 if shards[0] else jnp.float32,
             places_of(shards), window, last_part,
         )
@@ -496,7 +500,7 @@
     attn, ot, lse = forward(doc_ids, qt, state, [held[1]], places_of([1]), window, True, COST)
     attn, cot_y = lax.optimization_barrier((attn, cot_y))
     cot_d = swap(cot_y, 1)
-    grad_attn = features_in((2, 3), [cot_y, cot_d], weight, near, jnp.bfloat16)
+    grads = features_in((2, 3), [cot_y, cot_d], weight, near, ot)
     out_a = features_out(3, attn, weight, part)
 
     out_b = features_out(2, attn, weight, part, [swap(out_a, 1)])

time: 46.1 us -> 45.9 us (level)
  transfers between devices with their start and end apart: 14 -> 14, of which waited for: 3 -> 3; matrix products, arithmetic and copies ran while one was open for 0% -> 0% of each run, Pallas kernels for 39% -> 38%
where the time goes in v4:
time: 45.9 us; the launch traced here: 45.7 us
  starting transfers between devices  20.2 us (44%)
  Pallas kernels  20.1 us (44%)
  waiting for transfers between devices  4.58 us (10%)
  between operations  0.8 us (2%)
    ppermute x5, starting transfers between devices, turn(): lax.ppermute(array, axis, [(i, (i + by) % devices) for i in range(devices)])  8.19 us
    ppermute x8, starting transfers between devices, swap(): lax.ppermute(array, axis, [(i, i ^ bit) for i in range(lax.axis_size(axis...  7.64 us
    pallas_call x3, Pallas kernels, backward(): pl.pallas_call(functools.partial(backward_kernel, window, blocks, places,...  6.51 us
    ppermute x8, waiting for transfers between devices, swap(): lax.ppermute(array, axis, [(i, i ^ bit) for i in range(lax.axis_size(axis...  4.43 us
    ppermute x1, starting transfers between devices, shift(): return lax.ppermute(array, axis, pairs)  4.4 us
    pallas_call x2, Pallas kernels, forward(): pl.pallas_call(functools.partial(forward_kernel, window, blocks, places,...  4.14 us
    pallas_call x1, Pallas kernels, prepare(): pl.pallas_call(prepare_kernel, out_shape=[jax.ShapeDtypeStruct((rows, wid...  3.43 us
    pallas_call x4, Pallas kernels, features_out(): pl.pallas_call(functools.partial(features_out_kernel, which), out_shape=j...  2.77 us
  transfers between devices with their start and end apart: 14, of which 3 were waited for; matrix products, arithmetic and copies ran while one was open for 0% of the time, Pallas kernels for 38%

profile of v4, /device:TPU:0, one launch (start us, length us, event | category | flops | bytes accessed | tf_op | source)
XLA Modules:
  0.0 45.7 jit_solution(3303823342112861967)
XLA Ops:
  0.6 0.0 copy-start
  0.6 0.9 %join.1 = (bf16[256,256]{1,0:T(8,128)(2,1)S(1)}, bf16[128,256]{1,0:T(8,128)(2,1)S(1)}) custom-call(bf16[256,128]{1,0:T(8,128)(2,1)} %k_hbm.1, bf16[256,128]{1,0:T(8,128)(2,1)} %v_hbm.1), custom_call_target="tpu_custom_call" | custom-call | flops 1048576 | bytes 1024 | tf_op jit(solution)/shard_map/join/pallas_call | solution.py:329
  1.6 0.5 %collective-permute-start = (bf16[256,1280]{1,0:T(8,128)(2,1)}, bf16[256,1280]{1,0:T(8,128)(2,1)S(1)}, u32[]{:S(2)}, u32[]{:S(2)}) collective-permute-start(bf16[256,1280]{1,0:T(8,128)(2,1)} %cot_hbm), channel_id=1, source_target_pairs={{0,1},{1,0},{2,3},{3,2},{4,5},{5,4},{6,7},{7,6},{8,9},{9,8},{10,11... | collective-permute-start | bytes 1966088 | tf_op jit(solution)/shard_map/ppermute | solution.py:48
  2.1 2.6 %collective-permute-start.5 = (bf16[256,1280]{1,0:T(8,128)(2,1)}, bf16[256,1280]{1,0:T(8,128)(2,1)S(1)}, u32[]{:S(2)}, u32[]{:S(2)}) collective-permute-start(bf16[256,1280]{1,0:T(8,128)(2,1)} %cot_hbm), channel_id=1, source_target_pairs={{0,2},{1,3},{2,0},{3,1},{4,6},{5,7},{6,4},{7,5},{8,10},{9,11},{10,... | collective-permute-start | bytes 1966088 | tf_op jit(solution)/shard_map/ppermute | solution.py:48
  4.7 1.6 %collective-permute-start.3 = (bf16[256,256]{1,0:T(8,128)(2,1)S(1)}, bf16[256,256]{1,0:T(8,128)(2,1)S(1)}, u32[]{:S(2)}, u32[]{:S(2)}) collective-permute-start(bf16[256,256]{1,0:T(8,128)(2,1)S(1)} %get-tuple-element.40.refs_3_.refs_2_), channel_id=1, source_target_pairs={{0,8},{4,12},{8,16},{12,20},{16,24},{20,28},{24,0},{28,4},{1,9},{5... | collective-permute-start | bytes 393224 | tf_op jit(solution)/shard_map/ppermute | solution.py:44
  6.3 4.4 %collective-permute-start.2 = (bf16[256,256]{1,0:T(8,128)(2,1)S(1)}, bf16[256,256]{1,0:T(8,128)(2,1)S(1)}, u32[]{:S(2)}, u32[]{:S(2)}) collective-permute-start(bf16[256,256]{1,0:T(8,128)(2,1)S(1)} %get-tuple-element.40.refs_3_.refs_2_), channel_id=1, source_target_pairs={{0,12},{4,16},{8,20},{12,24},{16,28},{1,13},{5,17},{9,21},{13,25},... | collective-permute-start | bytes 393224 | tf_op jit(solution)/shard_map/ppermute | solution.py:39
  10.7 1.3 %collective-permute-start.1 = (bf16[128,256]{1,0:T(8,128)(2,1)S(1)}, bf16[128,256]{1,0:T(8,128)(2,1)S(1)}, u32[]{:S(2)}, u32[]{:S(2)}) collective-permute-start(bf16[128,256]{1,0:T(8,128)(2,1)S(1)} %get-tuple-element.39), channel_id=1, source_target_pairs={{0,16},{4,20},{8,24},{12,28},{16,0},{20,4},{24,8},{28,12},{1,17},{... | collective-permute-start | bytes 196616 | tf_op jit(solution)/shard_map/ppermute | solution.py:44
  12.0 0.1 collective-permute-done.3.refs_2_
  12.1 1.6 %collective-permute-start.4 = (bf16[256,256]{1,0:T(8,128)(2,1)S(1)}, bf16[256,256]{1,0:T(8,128)(2,1)S(1)}, u32[]{:S(2)}, u32[]{:S(2)}) collective-permute-start(bf16[256,256]{1,0:T(8,128)(2,1)S(1)} %broadcast_select_fusion), channel_id=1, source_target_pairs={{0,4},{4,0},{8,12},{12,8},{16,20},{20,16},{24,28},{28,24},{1,5},{5... | collective-permute-start | bytes 393224 | tf_op jit(solution)/shard_map/ppermute | solution.py:48
  13.7 0.0 collective-permute-done.cot_c_ref
  13.7 3.4 %prepare.1 = (f32[256,640]{1,0:T(8,128)S(1)}, bf16[640,5120]{1,0:T(8,128)(2,1)S(1)}, bf16[256,640]{1,0:T(8,128)(2,1)S(1)}, bf16[1280,128]{1,0:T(8,128)(2,1)S(1)}) custom-call(bf16[256,640]{1,0:T(8,128)(2,1)} %q_hbm.1, bf16[256,1280]{1,0:T(8,128)(2,1)} %cot_hbm, bf16[256,1280]{1,0:T(8,128)(2,1)S(1)} %collective-permute-done.cot_c_ref, bf16[640,5120]{1,0:T(8,128)(2,1)} %w_hbm.1), custom_call_target="tpu_custom_call" | custom-call | flops 1048576 | bytes 1024 | tf_op jit(solution)/shard_map/prepare/pallas_call | solution.py:375
  17.1 0.0 collective-permute-done.1.refs_0_
  17.1 0.0 collective-permute-done.2.refs_1_
  17.1 0.0 copy-done
  17.2 2.6 %forward.2 = (f32[256,640]{1,0:T(8,128)S(1)}, f32[2,640]{1,0:T(2,128)S(1)}, f32[2,640]{1,0:T(2,128)S(1)}) custom-call(s32[16]{0:T(128)S(1)} %copy-done, bf16[256,640]{1,0:T(8,128)(2,1)S(1)} %get-tuple-element.38.qt_ref, bf16[128,256]{1,0:T(8,128)(2,1)S(1)} %collective-permute-done.1.refs_0_, bf16[256,256]{1,0:T(8,128)(2,1)S(1)} %collective-permute-done.2.refs_1_, ...), custom_call_target="tpu_custom_call" | custom-call | flops 2147483648 | bytes 1024 | tf_op jit(solution)/shard_map/forward/pallas_call | solution.py:131
  19.7 0.0 collective-permute-done.4.refs_3_.refs_2_
  19.8 1.6 %forward.3 = (bf16[256,640]{1,0:T(8,128)(2,1)S(1)}, bf16[256,640]{1,0:T(8,128)(2,1)S(1)}, f32[2,640]{1,0:T(2,128)S(1)}) custom-call(s32[16]{0:T(128)S(1)} %copy-done, bf16[256,640]{1,0:T(8,128)(2,1)S(1)} %get-tuple-element.38.qt_ref, f32[256,640]{1,0:T(8,128)S(1)} %get-tuple-element.41.refs_0_, f32[2,640]{1,0:T(2,128)S(1)} %get-tuple-element.42.refs_1_, ...), custom_call_target="tpu_custom_call" | custom-call | flops 1048576 | bytes 1024 | tf_op jit(solution)/shard_map/forward/pallas_call | solution.py:131
  21.3 0.0 collective-permute-done.5.refs_0_
  21.3 0.7 %features_out.6 = bf16[256,1280]{1,0:T(8,128)(2,1)S(1)} custom-call(bf16[256,640]{1,0:T(8,128)(2,1)S(1)} %get-tuple-element.45.attn_ref, bf16[640,5120]{1,0:T(8,128)(2,1)S(1)} %get-tuple-element.46.refs_0_.refs_1_.refs_3_), custom_call_target="tpu_custom_call" | custom-call | flops 1048576 | bytes 1024 | tf_op jit(solution)/shard_map/features_out/pallas_call | solution.py:300
  22.0 0.1 collective-permute-start.7
  22.1 0.5 %collective-permute-start.9 = (bf16[256,1280]{1,0:T(8,128)(2,1)S(1)}, bf16[256,1280]{1,0:T(8,128)(2,1)S(1)}, u32[]{:S(2)}, u32[]{:S(2)}) collective-permute-start(bf16[256,1280]{1,0:T(8,128)(2,1)S(1)} %collective-permute-done.5.refs_0_), channel_id=1, source_target_pairs={{0,1},{1,0},{2,3},{3,2},{4,5},{5,4},{6,7},{7,6},{8,9},{9,8},{10,11... | collective-permute-start | bytes 1966088 | tf_op jit(solution)/shard_map/ppermute | solution.py:48
  22.6 0.7 %features_out.4 = bf16[256,1280]{1,0:T(8,128)(2,1)S(1)} custom-call(bf16[256,640]{1,0:T(8,128)(2,1)S(1)} %get-tuple-element.45.attn_ref, bf16[640,5120]{1,0:T(8,128)(2,1)S(1)} %get-tuple-element.46.refs_0_.refs_1_.refs_3_), custom_call_target="tpu_custom_call" | custom-call | flops 1048576 | bytes 1024 | tf_op jit(solution)/shard_map/features_out/pallas_call | solution.py:300
  23.3 0.1 collective-permute-start.6
  23.4 0.7 %collective-permute-done.7.refs_0_ = bf16[256,1280]{1,0:T(8,128)(2,1)S(1)} collective-permute-done((bf16[256,1280]{1,0:T(8,128)(2,1)S(1)}, bf16[256,1280]{1,0:T(8,128)(2,1)S(1)}, u32[]{:S(2)}, u32[]{:S(2)}) %collective-permute-start.7) | collective-permute-done | bytes 655392 | tf_op jit(solution)/shard_map/ppermute | solution.py:48
  24.2 0.7 %features_out.7 = bf16[256,1280]{1,0:T(8,128)(2,1)S(1)} custom-call(bf16[256,640]{1,0:T(8,128)(2,1)S(1)} %get-tuple-element.45.attn_ref, bf16[256,1280]{1,0:T(8,128)(2,1)S(1)} %collective-permute-done.7.refs_0_, bf16[640,5120]{1,0:T(8,128)(2,1)S(1)} %get-tuple-element.46.refs_0_.refs_1_.refs_3_), custom_call_target="tpu_custom_call" | custom-call | flops 1048576 | bytes 1024 | tf_op jit(solution)/shard_map/features_out/pallas_call | solution.py:300
  24.9 0.7 %collective-permute-start.8 = (bf16[256,1280]{1,0:T(8,128)(2,1)S(1)}, bf16[256,1280]{1,0:T(8,128)(2,1)S(1)}, u32[]{:S(2)}, u32[]{:S(2)}) collective-permute-start(bf16[256,1280]{1,0:T(8,128)(2,1)S(1)} %features_out.7), channel_id=1, source_target_pairs={{0,2},{1,3},{2,0},{3,1},{4,6},{5,7},{6,4},{7,5},{8,10},{9,11},{10,... | collective-permute-start | bytes 1966088 | tf_op jit(solution)/shard_map/ppermute | solution.py:48
  25.6 0.0 collective-permute-done.9.refs_1_
  25.6 1.3 %features_in.1 = (bf16[256,640]{1,0:T(8,128)(2,1)S(1)}, bf16[1280,128]{1,0:T(8,128)(2,1)S(1)}, f32[2,640]{1,0:T(2,128)S(1)}) custom-call(bf16[256,1280]{1,0:T(8,128)(2,1)S(1)} %collective-permute-done.5.refs_0_, bf16[256,1280]{1,0:T(8,128)(2,1)S(1)} %collective-permute-done.9.refs_1_, f32[256,640]{1,0:T(8,128)S(1)} %get-tuple-element.50.refs_2_, ...), custom_call_target="tpu_custom_call" | custom-call | flops 1048576 | bytes 1024 | tf_op jit(solution)/shard_map/features_in/pallas_call | solution.py:275
  26.9 2.6 %backward.3 = (f32[256,640]{1,0:T(8,128)S(1)}, bf16[128,256]{1,0:T(8,128)(2,1)S(1)}, bf16[256,256]{1,0:T(8,128)(2,1)S(1)}, bf16[256,256]{1,0:T(8,128)(2,1)S(1)}) custom-call(s32[16]{0:T(128)S(1)} %copy-done, bf16[256,640]{1,0:T(8,128)(2,1)S(1)} %get-tuple-element.38.qt_ref, bf16[1280,128]{1,0:T(8,128)(2,1)S(1)} %get-tuple-element.47.q_rows_ref, ...), custom_call_target="tpu_custom_call" | custom-call | flops 1048576 | bytes 1024 | tf_op jit(solution)/shard_map/backward/pallas_call | solution.py:222
  29.5 1.5 %collective-permute-start.10 = (bf16[256,256]{1,0:T(8,128)(2,1)S(1)}, bf16[256,256]{1,0:T(8,128)(2,1)S(1)}, u32[]{:S(2)}, u32[]{:S(2)}) collective-permute-start(bf16[256,256]{1,0:T(8,128)(2,1)S(1)} %get-tuple-element.56), channel_id=1, source_target_pairs={{0,4},{4,0},{8,12},{12,8},{16,20},{20,16},{24,28},{28,24},{1,5},{5... | collective-permute-start | bytes 393224 | tf_op jit(solution)/shard_map/ppermute | solution.py:48
  31.1 2.6 %collective-permute-start.12 = (bf16[256,256]{1,0:T(8,128)(2,1)S(1)}, bf16[256,256]{1,0:T(8,128)(2,1)S(1)}, u32[]{:S(2)}, u32[]{:S(2)}) collective-permute-start(bf16[256,256]{1,0:T(8,128)(2,1)S(1)} %get-tuple-element.60), channel_id=1, source_target_pairs={{0,20},{4,24},{8,28},{12,0},{16,4},{20,8},{24,12},{28,16},{1,21},{... | collective-permute-start | bytes 393224 | tf_op jit(solution)/shard_map/ppermute | solution.py:44
  33.6 0.3 collective-permute-start.11
  34.0 3.7 %collective-permute-done.10.refs_1_ = bf16[256,256]{1,0:T(8,128)(2,1)S(1)} collective-permute-done((bf16[256,256]{1,0:T(8,128)(2,1)S(1)}, bf16[256,256]{1,0:T(8,128)(2,1)S(1)}, u32[]{:S(2)}, u32[]{:S(2)}) %collective-permute-start.10) | collective-permute-done | bytes 131104 | tf_op jit(solution)/shard_map/ppermute | solution.py:48
  37.6 1.6 %backward.4 = (f32[256,640]{1,0:T(8,128)S(1)}, bf16[256,256]{1,0:T(8,128)(2,1)S(1)}) custom-call(s32[16]{0:T(128)S(1)} %copy-done, bf16[256,640]{1,0:T(8,128)(2,1)S(1)} %get-tuple-element.38.qt_ref, bf16[1280,128]{1,0:T(8,128)(2,1)S(1)} %get-tuple-element.47.q_rows_ref, f32[2,640]{1,0:T(2,128)S(1)} %get-tuple-element.48.lse_ref, ...), custom_call_target="tpu_custom_call" | custom-call | flops 1048576 | bytes 1024 | tf_op jit(solution)/shard_map/backward/pallas_call | solution.py:222
  39.3 2.4 %collective-permute-start.13 = (bf16[256,256]{1,0:T(8,128)(2,1)S(1)}, bf16[256,256]{1,0:T(8,128)(2,1)S(1)}, u32[]{:S(2)}, u32[]{:S(2)}) collective-permute-start(bf16[256,256]{1,0:T(8,128)(2,1)S(1)} %get-tuple-element.61), channel_id=1, source_target_pairs={{0,24},{4,28},{8,0},{12,4},{16,8},{20,12},{24,16},{28,20},{1,25},{... | collective-permute-start | bytes 393224 | tf_op jit(solution)/shard_map/ppermute | solution.py:44
  41.7 0.0 collective-permute-done.6.refs_0_
  41.7 0.7 %features_out.5.out_ref = f32[256,1280]{1,0:T(8,128)S(1)} custom-call(bf16[256,640]{1,0:T(8,128)(2,1)S(1)} %get-tuple-element.45.attn_ref, bf16[256,1280]{1,0:T(8,128)(2,1)S(1)} %collective-permute-done.6.refs_0_, bf16[640,5120]{1,0:T(8,128)(2,1)S(1)} %get-tuple-element.46.refs_0_.refs_1_.refs_3_), custom_call_target="tpu_custom_call" | custom-call | flops 1048576 | bytes 1024 | tf_op jit(solution)/shard_map/features_out/pallas_call | solution.py:300
  42.4 2.3 %backward.5 = (bf16[256,640]{1,0:T(8,128)(2,1)}, f32[256,256]{1,0:T(8,128)S(1)}) custom-call(s32[16]{0:T(128)S(1)} %copy-done, bf16[256,640]{1,0:T(8,128)(2,1)S(1)} %get-tuple-element.38.qt_ref, bf16[1280,128]{1,0:T(8,128)(2,1)S(1)} %get-tuple-element.47.q_rows_ref, f32[2,640]{1,0:T(2,128)S(1)} %get-tuple-element.48.lse_ref, ...), custom_call_target="tpu_custom_call" | custom-call | flops 1048576 | bytes 1024 | tf_op jit(solution)/shard_map/backward/pallas_call | solution.py:222
  44.7 0.0 collective-permute-done.11.refs_1_
  44.7 0.0 collective-permute-done.12.refs_2_
  44.7 0.0 collective-permute-done.13.back_ref
  44.7 0.0 collective-permute-done.8.other_ref
  44.8 1.0 %finish.1 = (bf16[256,1280]{1,0:T(8,128)(2,1)}, bf16[256,128]{1,0:T(8,128)(2,1)}, bf16[256,128]{1,0:T(8,128)(2,1)}) custom-call(f32[256,1280]{1,0:T(8,128)S(1)} %features_out.5.out_ref, bf16[256,1280]{1,0:T(8,128)(2,1)S(1)} %collective-permute-done.8.other_ref, f32[256,256]{1,0:T(8,128)S(1)} %add_up.1.own_ref, ...), custom_call_target="tpu_custom_call" | custom-call | flops 1048576 | bytes 1024 | tf_op jit(solution)/shard_map/finish/pallas_call | solution.py:447
  (2 shorter events, 0.1 us)
Async XLA Ops:
  0.6 16.5 %copy-start = (s32[16]{0:T(128)S(1)}, s32[16]{0:T(128)}, u32[]{:S(2)}) copy-start(s32[16]{0:T(128)} %doc_ref.9) | copy-start | bytes 196
  1.6 12.1 %collective-permute-start = (bf16[256,1280]{1,0:T(8,128)(2,1)}, bf16[256,1280]{1,0:T(8,128)(2,1)S(1)}, u32[]{:S(2)}, u32[]{:S(2)}) collective-permute-start(bf16[256,1280]{1,0:T(8,128)(2,1)} %cot_hbm), channel_id=1, source_target_pairs={{0,1},{1,0},{2,3},{3,2},{4,5},{5,4},{6,7},{7,6},{8,9},{9,8},{10,11... | collective-permute-start | bytes 1966088 | tf_op jit(solution)/shard_map/ppermute | solution.py:48
  2.1 19.2 %collective-permute-start.5 = (bf16[256,1280]{1,0:T(8,128)(2,1)}, bf16[256,1280]{1,0:T(8,128)(2,1)S(1)}, u32[]{:S(2)}, u32[]{:S(2)}) collective-permute-start(bf16[256,1280]{1,0:T(8,128)(2,1)} %cot_hbm), channel_id=1, source_target_pairs={{0,2},{1,3},{2,0},{3,1},{4,6},{5,7},{6,4},{7,5},{8,10},{9,11},{10,... | collective-permute-start | bytes 1966088 | tf_op jit(solution)/shard_map/ppermute | solution.py:48
  4.7 7.4 %collective-permute-start.3 = (bf16[256,256]{1,0:T(8,128)(2,1)S(1)}, bf16[256,256]{1,0:T(8,128)(2,1)S(1)}, u32[]{:S(2)}, u32[]{:S(2)}) collective-permute-start(bf16[256,256]{1,0:T(8,128)(2,1)S(1)} %get-tuple-element.40.refs_3_.refs_2_), channel_id=1, source_target_pairs={{0,8},{4,12},{8,16},{12,20},{16,24},{20,28},{24,0},{28,4},{1,9},{5... | collective-permute-start | bytes 393224 | tf_op jit(solution)/shard_map/ppermute | solution.py:44
  6.3 10.9 %collective-permute-start.2 = (bf16[256,256]{1,0:T(8,128)(2,1)S(1)}, bf16[256,256]{1,0:T(8,128)(2,1)S(1)}, u32[]{:S(2)}, u32[]{:S(2)}) collective-permute-start(bf16[256,256]{1,0:T(8,128)(2,1)S(1)} %get-tuple-element.40.refs_3_.refs_2_), channel_id=1, source_target_pairs={{0,12},{4,16},{8,20},{12,24},{16,28},{1,13},{5,17},{9,21},{13,25},... | collective-permute-start | bytes 393224 | tf_op jit(solution)/shard_map/ppermute | solution.py:39
  10.7 6.5 %collective-permute-start.1 = (bf16[128,256]{1,0:T(8,128)(2,1)S(1)}, bf16[128,256]{1,0:T(8,128)(2,1)S(1)}, u32[]{:S(2)}, u32[]{:S(2)}) collective-permute-start(bf16[128,256]{1,0:T(8,128)(2,1)S(1)} %get-tuple-element.39), channel_id=1, source_target_pairs={{0,16},{4,20},{8,24},{12,28},{16,0},{20,4},{24,8},{28,12},{1,17},{... | collective-permute-start | bytes 196616 | tf_op jit(solution)/shard_map/ppermute | solution.py:44
  12.1 7.6 %collective-permute-start.4 = (bf16[256,256]{1,0:T(8,128)(2,1)S(1)}, bf16[256,256]{1,0:T(8,128)(2,1)S(1)}, u32[]{:S(2)}, u32[]{:S(2)}) collective-permute-start(bf16[256,256]{1,0:T(8,128)(2,1)S(1)} %broadcast_select_fusion), channel_id=1, source_target_pairs={{0,4},{4,0},{8,12},{12,8},{16,20},{20,16},{24,28},{28,24},{1,5},{5... | collective-permute-start | bytes 393224 | tf_op jit(solution)/shard_map/ppermute | solution.py:48
  22.0 2.2 %collective-permute-start.7 = (bf16[256,1280]{1,0:T(8,128)(2,1)S(1)}, bf16[256,1280]{1,0:T(8,128)(2,1)S(1)}, u32[]{:S(2)}, u32[]{:S(2)}) collective-permute-start(bf16[256,1280]{1,0:T(8,128)(2,1)S(1)} %features_out.6), channel_id=1, source_target_pairs={{0,1},{1,0},{2,3},{3,2},{4,5},{5,4},{6,7},{7,6},{8,9},{9,8},{10,11... | collective-permute-start | bytes 1966088 | tf_op jit(solution)/shard_map/ppermute | solution.py:48
  22.1 3.5 %collective-permute-start.9 = (bf16[256,1280]{1,0:T(8,128)(2,1)S(1)}, bf16[256,1280]{1,0:T(8,128)(2,1)S(1)}, u32[]{:S(2)}, u32[]{:S(2)}) collective-permute-start(bf16[256,1280]{1,0:T(8,128)(2,1)S(1)} %collective-permute-done.5.refs_0_), channel_id=1, source_target_pairs={{0,1},{1,0},{2,3},{3,2},{4,5},{5,4},{6,7},{7,6},{8,9},{9,8},{10,11... | collective-permute-start | bytes 1966088 | tf_op jit(solution)/shard_map/ppermute | solution.py:48
  23.3 18.4 %collective-permute-start.6 = (bf16[256,1280]{1,0:T(8,128)(2,1)S(1)}, bf16[256,1280]{1,0:T(8,128)(2,1)S(1)}, u32[]{:S(2)}, u32[]{:S(2)}) collective-permute-start(bf16[256,1280]{1,0:T(8,128)(2,1)S(1)} %features_out.4), channel_id=1, source_target_pairs={{0,1},{1,0},{2,3},{3,2},{4,5},{5,4},{6,7},{7,6},{8,9},{9,8},{10,11... | collective-permute-start | bytes 1966088 | tf_op jit(solution)/shard_map/ppermute | solution.py:48
  24.9 19.9 %collective-permute-start.8 = (bf16[256,1280]{1,0:T(8,128)(2,1)S(1)}, bf16[256,1280]{1,0:T(8,128)(2,1)S(1)}, u32[]{:S(2)}, u32[]{:S(2)}) collective-permute-start(bf16[256,1280]{1,0:T(8,128)(2,1)S(1)} %features_out.7), channel_id=1, source_target_pairs={{0,2},{1,3},{2,0},{3,1},{4,6},{5,7},{6,4},{7,5},{8,10},{9,11},{10,... | collective-permute-start | bytes 1966088 | tf_op jit(solution)/shard_map/ppermute | solution.py:48
  29.5 8.1 %collective-permute-start.10 = (bf16[256,256]{1,0:T(8,128)(2,1)S(1)}, bf16[256,256]{1,0:T(8,128)(2,1)S(1)}, u32[]{:S(2)}, u32[]{:S(2)}) collective-permute-start(bf16[256,256]{1,0:T(8,128)(2,1)S(1)} %get-tuple-element.56), channel_id=1, source_target_pairs={{0,4},{4,0},{8,12},{12,8},{16,20},{20,16},{24,28},{28,24},{1,5},{5... | collective-permute-start | bytes 393224 | tf_op jit(solution)/shard_map/ppermute | solution.py:48
  31.1 13.6 %collective-permute-start.12 = (bf16[256,256]{1,0:T(8,128)(2,1)S(1)}, bf16[256,256]{1,0:T(8,128)(2,1)S(1)}, u32[]{:S(2)}, u32[]{:S(2)}) collective-permute-start(bf16[256,256]{1,0:T(8,128)(2,1)S(1)} %get-tuple-element.60), channel_id=1, source_target_pairs={{0,20},{4,24},{8,28},{12,0},{16,4},{20,8},{24,12},{28,16},{1,21},{... | collective-permute-start | bytes 393224 | tf_op jit(solution)/shard_map/ppermute | solution.py:44
  33.6 11.0 %collective-permute-start.11 = (bf16[128,256]{1,0:T(8,128)(2,1)S(1)}, bf16[128,256]{1,0:T(8,128)(2,1)S(1)}, u32[]{:S(2)}, u32[]{:S(2)}) collective-permute-start(bf16[128,256]{1,0:T(8,128)(2,1)S(1)} %get-tuple-element.59), channel_id=1, source_target_pairs={{0,16},{4,20},{8,24},{12,28},{16,0},{20,4},{24,8},{28,12},{1,17},{... | collective-permute-start | bytes 196616 | tf_op jit(solution)/shard_map/ppermute | solution.py:44
  39.3 5.5 %collective-permute-start.13 = (bf16[256,256]{1,0:T(8,128)(2,1)S(1)}, bf16[256,256]{1,0:T(8,128)(2,1)S(1)}, u32[]{:S(2)}, u32[]{:S(2)}) collective-permute-start(bf16[256,256]{1,0:T(8,128)(2,1)S(1)} %get-tuple-element.61), channel_id=1, source_target_pairs={{0,24},{4,28},{8,0},{12,4},{16,8},{20,12},{24,16},{28,20},{1,25},{... | collective-permute-start | bytes 393224 | tf_op jit(solution)/shard_map/ppermute | solution.py:44

commit v5 on v4

--- a/solution.py
+++ b/solution.py
@@ -15,6 +15,8 @@
 LOW = -1e30
 HIGH = 1e30
 VMEM_LIMIT = 16 * 1024 * 1024
+
+PAD = 16
 
 COST = pl.CostEstimate(flops=2**20, bytes_accessed=2**10, transcendentals=0)
 LONG = pl.CostEstimate(flops=2**31, bytes_accessed=2**10, transcendentals=0)
@@ -72,9 +74,9 @@
     first = lax.axis_index("ctx") * blocks
     at = 0
     for ref in kv_refs:
-        rows = ref.shape[0]
-        k_all[pl.ds(at, rows), :] = ref[:, :HEAD_SIZE]
-        vt_all[:, pl.ds(at, rows)] = ref[:, HEAD_SIZE:].T
+        rows = ref.shape[0] // BLK * BLK
+        k_all[pl.ds(at, rows), :] = ref[:rows, :HEAD_SIZE]
+        vt_all[:, pl.ds(at, rows)] = ref[:rows, HEAD_SIZE:].T
         at += rows
     for b in range(blocks):
         qt = qt_ref[block(b), :]
@@ -161,10 +163,10 @@
     first = me * blocks
     at = 0
     for ref in kv_refs:
-        rows = ref.shape[0]
-        k_all[pl.ds(at, rows), :] = ref[:, :HEAD_SIZE]
-        kt_all[:, pl.ds(at, rows)] = ref[:, :HEAD_SIZE].T
-        v_all[pl.ds(at, rows), :] = ref[:, HEAD_SIZE:]
+        rows = ref.shape[0] // BLK * BLK
+        k_all[pl.ds(at, rows), :] = ref[:rows, :HEAD_SIZE]
+        kt_all[:, pl.ds(at, rows)] = ref[:rows, :HEAD_SIZE].T
+        v_all[pl.ds(at, rows), :] = ref[:rows, HEAD_SIZE:]
         at += rows
     dkv_all[...] = jnp.zeros_like(dkv_all)
     for b in range(blocks):
@@ -225,7 +227,7 @@
             None if taken is None else taken[1],
         ),
         out_shape=[jax.ShapeDtypeStruct((rows, width), dq_kind)]
-        + [jax.ShapeDtypeStruct(kv.shape, kind) for kv in kvs],
+        + [jax.ShapeDtypeStruct((kv.shape[0] // BLK * BLK, kv.shape[1]), kind) for kv in kvs],
         in_specs=[SMEM] + [VMEM] * (6 + len(extra) + len(kvs)),
         out_specs=[VMEM] * (1 + len(kvs)),
         scratch_shapes=[
@@ -308,7 +310,7 @@
     )(attn, *extra, weight)
 
 
-def join_kernel(k_hbm, v_hbm, whole_ref, last_ref, k, v, sems):
+def join_kernel(k_hbm, v_hbm, whole_ref, last_ref, padded_ref, k, v, sems):
     copies = [
         pltpu.make_async_copy(k_hbm, k, sems.at[0]),
         pltpu.make_async_copy(v_hbm, v, sems.at[1]),
@@ -322,15 +324,17 @@
     whole_ref[:, HEAD_SIZE:] = v[...]
     last_ref[:, :HEAD_SIZE] = k[skipped:, :]
     last_ref[:, HEAD_SIZE:] = v[skipped:, :]
+    padded_ref[:k.shape[0], :] = whole_ref[...]
+    padded_ref[k.shape[0]:, :] = jnp.zeros_like(padded_ref[k.shape[0]:, :])
 
 
 def join(keys, values, last):
     rows, width = keys.shape
     return pl.pallas_call(
         join_kernel,
-        out_shape=[jax.ShapeDtypeStruct((n, 2 * width), keys.dtype) for n in (rows, last)],
+        out_shape=[jax.ShapeDtypeStruct((n, 2 * width), keys.dtype) for n in (rows, last, rows + PAD)],
         in_specs=[HBM] * 2,
-        out_specs=[VMEM] * 2,
+        out_specs=[VMEM] * 3,
         scratch_shapes=[pltpu.VMEM(keys.shape, keys.dtype)] * 2 + [pltpu.SemaphoreType.DMA((2,))],
         compiler_params=pltpu.CompilerParams(vmem_limit_bytes=VMEM_LIMIT),
         cost_estimate=COST,
@@ -469,12 +473,12 @@
         needs.append(min(left, blocks))
         left -= needs[-1]
     odd = lax.axis_index("ctx") % 2
-    key_value, tail = join(keys, values, needs[-1] * BLK)
-    key_value, tail, cot = lax.optimization_barrier((key_value, tail, cotangent))
+    key_value, tail, padded = join(keys, values, needs[-1] * BLK)
+    key_value, tail, padded, cot = lax.optimization_barrier((key_value, tail, padded, cotangent))
     cot_y = swap(cot, 2)
     held = [key_value, None]
     held += [
-        (shift if s % 2 else turn)(tail if n < blocks else key_value, "ctx", s)
+        shift(padded, "ctx", s) if s % 2 else turn(tail if n < blocks else key_value, "ctx", s)
         for s, n in enumerate(needs[1:], start=2)
     ]
     held[1] = swap(jnp.where(odd == 0, key_value, held[2]), 1, "ctx")

time: 45.9 us -> 46.3 us (level)
  no operation moved by 1% of the time
where the time goes in v5:
time: 46.3 us; the launch traced here: 46.1 us
  starting transfers between devices  20.6 us (44%)
  Pallas kernels  20.1 us (43%)
  waiting for transfers between devices  4.58 us (10%)
  between operations  0.8 us (2%)
    ppermute x5, starting transfers between devices, turn(): lax.ppermute(array, axis, [(i, (i + by) % devices) for i in range(devices)])  8.53 us
    ppermute x8, starting transfers between devices, swap(): lax.ppermute(array, axis, [(i, i ^ bit) for i in range(lax.axis_size(axis...  7.64 us
    pallas_call x3, Pallas kernels, backward(): pl.pallas_call(functools.partial(backward_kernel, window, blocks, places,...  6.51 us
    ppermute x8, waiting for transfers between devices, swap(): lax.ppermute(array, axis, [(i, i ^ bit) for i in range(lax.axis_size(axis...  4.43 us
    ppermute x1, starting transfers between devices, shift(): return lax.ppermute(array, axis, pairs)  4.4 us
    pallas_call x2, Pallas kernels, forward(): pl.pallas_call(functools.partial(forward_kernel, window, blocks, places,...  4.14 us
    pallas_call x1, Pallas kernels, prepare(): pl.pallas_call(prepare_kernel, out_shape=[jax.ShapeDtypeStruct((rows, wid...  3.43 us
    pallas_call x4, Pallas kernels, features_out(): pl.pallas_call(functools.partial(features_out_kernel, which), out_shape=j...  2.77 us
  transfers between devices with their start and end apart: 14, of which 3 were waited for; matrix products, arithmetic and copies ran while one was open for 0% of the time, Pallas kernels for 38%

profile of v5, /device:TPU:0, one launch (start us, length us, event | category | flops | bytes accessed | tf_op | source)
XLA Modules:
  0.0 46.1 jit_solution(16449074625228773296)
XLA Ops:
  0.6 0.0 copy-start
  0.6 0.9 %join.1 = (bf16[256,256]{1,0:T(8,128)(2,1)S(1)}, bf16[128,256]{1,0:T(8,128)(2,1)S(1)}, bf16[272,256]{1,0:T(8,128)(2,1)S(1)}) custom-call(bf16[256,128]{1,0:T(8,128)(2,1)} %k_hbm.1, bf16[256,128]{1,0:T(8,128)(2,1)} %v_hbm.1), custom_call_target="tpu_custom_call" | custom-call | flops 1048576 | bytes 1024 | tf_op jit(solution)/shard_map/join/pallas_call | solution.py:333
  1.6 0.5 %collective-permute-start = (bf16[256,1280]{1,0:T(8,128)(2,1)}, bf16[256,1280]{1,0:T(8,128)(2,1)S(1)}, u32[]{:S(2)}, u32[]{:S(2)}) collective-permute-start(bf16[256,1280]{1,0:T(8,128)(2,1)} %cot_hbm), channel_id=1, source_target_pairs={{0,1},{1,0},{2,3},{3,2},{4,5},{5,4},{6,7},{7,6},{8,9},{9,8},{10,11... | collective-permute-start | bytes 1966088 | tf_op jit(solution)/shard_map/ppermute | solution.py:50
  2.1 2.6 %collective-permute-start.5 = (bf16[256,1280]{1,0:T(8,128)(2,1)}, bf16[256,1280]{1,0:T(8,128)(2,1)S(1)}, u32[]{:S(2)}, u32[]{:S(2)}) collective-permute-start(bf16[256,1280]{1,0:T(8,128)(2,1)} %cot_hbm), channel_id=1, source_target_pairs={{0,2},{1,3},{2,0},{3,1},{4,6},{5,7},{6,4},{7,5},{8,10},{9,11},{10,... | collective-permute-start | bytes 1966088 | tf_op jit(solution)/shard_map/ppermute | solution.py:50
  4.7 1.6 %collective-permute-start.3 = (bf16[256,256]{1,0:T(8,128)(2,1)S(1)}, bf16[256,256]{1,0:T(8,128)(2,1)S(1)}, u32[]{:S(2)}, u32[]{:S(2)}) collective-permute-start(bf16[256,256]{1,0:T(8,128)(2,1)S(1)} %get-tuple-element.44.refs_3_.refs_2_), channel_id=1, source_target_pairs={{0,8},{4,12},{8,16},{12,20},{16,24},{20,28},{24,0},{28,4},{1,9},{5... | collective-permute-start | bytes 393224 | tf_op jit(solution)/shard_map/ppermute | solution.py:46
  6.3 4.4 %collective-permute-start.2 = (bf16[272,256]{1,0:T(8,128)(2,1)S(1)}, bf16[272,256]{1,0:T(8,128)(2,1)S(1)}, u32[]{:S(2)}, u32[]{:S(2)}) collective-permute-start(bf16[272,256]{1,0:T(8,128)(2,1)S(1)} %get-tuple-element.43), channel_id=1, source_target_pairs={{0,12},{4,16},{8,20},{12,24},{16,28},{1,13},{5,17},{9,21},{13,25},... | collective-permute-start | bytes 417800 | tf_op jit(solution)/shard_map/ppermute | solution.py:41
  10.7 1.3 %collective-permute-start.1 = (bf16[128,256]{1,0:T(8,128)(2,1)S(1)}, bf16[128,256]{1,0:T(8,128)(2,1)S(1)}, u32[]{:S(2)}, u32[]{:S(2)}) collective-permute-start(bf16[128,256]{1,0:T(8,128)(2,1)S(1)} %get-tuple-element.42), channel_id=1, source_target_pairs={{0,16},{4,20},{8,24},{12,28},{16,0},{20,4},{24,8},{28,12},{1,17},{... | collective-permute-start | bytes 196616 | tf_op jit(solution)/shard_map/ppermute | solution.py:46
  12.0 0.1 collective-permute-done.3.refs_2_
  12.1 1.6 %collective-permute-start.4 = (bf16[256,256]{1,0:T(8,128)(2,1)S(1)}, bf16[256,256]{1,0:T(8,128)(2,1)S(1)}, u32[]{:S(2)}, u32[]{:S(2)}) collective-permute-start(bf16[256,256]{1,0:T(8,128)(2,1)S(1)} %broadcast_select_fusion), channel_id=1, source_target_pairs={{0,4},{4,0},{8,12},{12,8},{16,20},{20,16},{24,28},{28,24},{1,5},{5... | collective-permute-start | bytes 393224 | tf_op jit(solution)/shard_map/ppermute | solution.py:50
  13.7 0.0 collective-permute-done.cot_c_ref
  13.7 3.4 %prepare.1 = (f32[256,640]{1,0:T(8,128)S(1)}, bf16[640,5120]{1,0:T(8,128)(2,1)S(1)}, bf16[256,640]{1,0:T(8,128)(2,1)S(1)}, bf16[1280,128]{1,0:T(8,128)(2,1)S(1)}) custom-call(bf16[256,640]{1,0:T(8,128)(2,1)} %q_hbm.1, bf16[256,1280]{1,0:T(8,128)(2,1)} %cot_hbm, bf16[256,1280]{1,0:T(8,128)(2,1)S(1)} %collective-permute-done.cot_c_ref, bf16[640,5120]{1,0:T(8,128)(2,1)} %w_hbm.1), custom_call_target="tpu_custom_call" | custom-call | flops 1048576 | bytes 1024 | tf_op jit(solution)/shard_map/prepare/pallas_call | solution.py:379
  17.1 0.0 collective-permute-done.1.refs_0_
  17.1 0.0 collective-permute-done.2.refs_1_
  17.2 0.0 copy-done
  17.2 2.6 %forward.2 = (f32[256,640]{1,0:T(8,128)S(1)}, f32[2,640]{1,0:T(2,128)S(1)}, f32[2,640]{1,0:T(2,128)S(1)}) custom-call(s32[16]{0:T(128)S(1)} %copy-done, bf16[256,640]{1,0:T(8,128)(2,1)S(1)} %get-tuple-element.41.qt_ref, bf16[128,256]{1,0:T(8,128)(2,1)S(1)} %collective-permute-done.1.refs_0_, bf16[272,256]{1,0:T(8,128)(2,1)S(1)} %collective-permute-done.2.refs_1_, ...), custom_call_target="tpu_custom_call" | custom-call | flops 2147483648 | bytes 1024 | tf_op jit(solution)/shard_map/forward/pallas_call | solution.py:133
  19.7 0.0 collective-permute-done.4.refs_3_.refs_2_
  19.8 1.6 %forward.3 = (bf16[256,640]{1,0:T(8,128)(2,1)S(1)}, bf16[256,640]{1,0:T(8,128)(2,1)S(1)}, f32[2,640]{1,0:T(2,128)S(1)}) custom-call(s32[16]{0:T(128)S(1)} %copy-done, bf16[256,640]{1,0:T(8,128)(2,1)S(1)} %get-tuple-element.41.qt_ref, f32[256,640]{1,0:T(8,128)S(1)} %get-tuple-element.45.refs_0_, f32[2,640]{1,0:T(2,128)S(1)} %get-tuple-element.46.refs_1_, ...), custom_call_target="tpu_custom_call" | custom-call | flops 1048576 | bytes 1024 | tf_op jit(solution)/shard_map/forward/pallas_call | solution.py:133
  21.3 0.0 collective-permute-done.5.refs_0_
  21.3 0.7 %features_out.6 = bf16[256,1280]{1,0:T(8,128)(2,1)S(1)} custom-call(bf16[256,640]{1,0:T(8,128)(2,1)S(1)} %get-tuple-element.49.attn_ref, bf16[640,5120]{1,0:T(8,128)(2,1)S(1)} %get-tuple-element.50.refs_0_.refs_1_.refs_3_), custom_call_target="tpu_custom_call" | custom-call | flops 1048576 | bytes 1024 | tf_op jit(solution)/shard_map/features_out/pallas_call | solution.py:302
  22.0 0.1 collective-permute-start.7
  22.1 0.5 %collective-permute-start.9 = (bf16[256,1280]{1,0:T(8,128)(2,1)S(1)}, bf16[256,1280]{1,0:T(8,128)(2,1)S(1)}, u32[]{:S(2)}, u32[]{:S(2)}) collective-permute-start(bf16[256,1280]{1,0:T(8,128)(2,1)S(1)} %collective-permute-done.5.refs_0_), channel_id=1, source_target_pairs={{0,1},{1,0},{2,3},{3,2},{4,5},{5,4},{6,7},{7,6},{8,9},{9,8},{10,11... | collective-permute-start | bytes 1966088 | tf_op jit(solution)/shard_map/ppermute | solution.py:50
  22.6 0.7 %features_out.4 = bf16[256,1280]{1,0:T(8,128)(2,1)S(1)} custom-call(bf16[256,640]{1,0:T(8,128)(2,1)S(1)} %get-tuple-element.49.attn_ref, bf16[640,5120]{1,0:T(8,128)(2,1)S(1)} %get-tuple-element.50.refs_0_.refs_1_.refs_3_), custom_call_target="tpu_custom_call" | custom-call | flops 1048576 | bytes 1024 | tf_op jit(solution)/shard_map/features_out/pallas_call | solution.py:302
  23.3 0.1 collective-permute-start.6
  23.4 0.7 %collective-permute-done.7.refs_0_ = bf16[256,1280]{1,0:T(8,128)(2,1)S(1)} collective-permute-done((bf16[256,1280]{1,0:T(8,128)(2,1)S(1)}, bf16[256,1280]{1,0:T(8,128)(2,1)S(1)}, u32[]{:S(2)}, u32[]{:S(2)}) %collective-permute-start.7) | collective-permute-done | bytes 655392 | tf_op jit(solution)/shard_map/ppermute | solution.py:50
  24.2 0.7 %features_out.7 = bf16[256,1280]{1,0:T(8,128)(2,1)S(1)} custom-call(bf16[256,640]{1,0:T(8,128)(2,1)S(1)} %get-tuple-element.49.attn_ref, bf16[256,1280]{1,0:T(8,128)(2,1)S(1)} %collective-permute-done.7.refs_0_, bf16[640,5120]{1,0:T(8,128)(2,1)S(1)} %get-tuple-element.50.refs_0_.refs_1_.refs_3_), custom_call_target="tpu_custom_call" | custom-call | flops 1048576 | bytes 1024 | tf_op jit(solution)/shard_map/features_out/pallas_call | solution.py:302
  24.9 0.7 %collective-permute-start.8 = (bf16[256,1280]{1,0:T(8,128)(2,1)S(1)}, bf16[256,1280]{1,0:T(8,128)(2,1)S(1)}, u32[]{:S(2)}, u32[]{:S(2)}) collective-permute-start(bf16[256,1280]{1,0:T(8,128)(2,1)S(1)} %features_out.7), channel_id=1, source_target_pairs={{0,2},{1,3},{2,0},{3,1},{4,6},{5,7},{6,4},{7,5},{8,10},{9,11},{10,... | collective-permute-start | bytes 1966088 | tf_op jit(solution)/shard_map/ppermute | solution.py:50
  25.6 0.0 collective-permute-done.9.refs_1_
  25.6 1.3 %features_in.1 = (bf16[256,640]{1,0:T(8,128)(2,1)S(1)}, bf16[1280,128]{1,0:T(8,128)(2,1)S(1)}, f32[2,640]{1,0:T(2,128)S(1)}) custom-call(bf16[256,1280]{1,0:T(8,128)(2,1)S(1)} %collective-permute-done.5.refs_0_, bf16[256,1280]{1,0:T(8,128)(2,1)S(1)} %collective-permute-done.9.refs_1_, f32[256,640]{1,0:T(8,128)S(1)} %get-tuple-element.54.refs_2_, ...), custom_call_target="tpu_custom_call" | custom-call | flops 1048576 | bytes 1024 | tf_op jit(solution)/shard_map/features_in/pallas_call | solution.py:277
  26.9 2.6 %backward.3 = (f32[256,640]{1,0:T(8,128)S(1)}, bf16[128,256]{1,0:T(8,128)(2,1)S(1)}, bf16[256,256]{1,0:T(8,128)(2,1)S(1)}, bf16[256,256]{1,0:T(8,128)(2,1)S(1)}) custom-call(s32[16]{0:T(128)S(1)} %copy-done, bf16[256,640]{1,0:T(8,128)(2,1)S(1)} %get-tuple-element.41.qt_ref, bf16[1280,128]{1,0:T(8,128)(2,1)S(1)} %get-tuple-element.51.q_rows_ref, ...), custom_call_target="tpu_custom_call" | custom-call | flops 1048576 | bytes 1024 | tf_op jit(solution)/shard_map/backward/pallas_call | solution.py:224
  29.5 1.6 %collective-permute-start.10 = (bf16[256,256]{1,0:T(8,128)(2,1)S(1)}, bf16[256,256]{1,0:T(8,128)(2,1)S(1)}, u32[]{:S(2)}, u32[]{:S(2)}) collective-permute-start(bf16[256,256]{1,0:T(8,128)(2,1)S(1)} %get-tuple-element.60), channel_id=1, source_target_pairs={{0,4},{4,0},{8,12},{12,8},{16,20},{20,16},{24,28},{28,24},{1,5},{5... | collective-permute-start | bytes 393224 | tf_op jit(solution)/shard_map/ppermute | solution.py:50
  31.1 2.6 %collective-permute-start.12 = (bf16[256,256]{1,0:T(8,128)(2,1)S(1)}, bf16[256,256]{1,0:T(8,128)(2,1)S(1)}, u32[]{:S(2)}, u32[]{:S(2)}) collective-permute-start(bf16[256,256]{1,0:T(8,128)(2,1)S(1)} %get-tuple-element.64), channel_id=1, source_target_pairs={{0,20},{4,24},{8,28},{12,0},{16,4},{20,8},{24,12},{28,16},{1,21},{... | collective-permute-start | bytes 393224 | tf_op jit(solution)/shard_map/ppermute | solution.py:46
  33.7 0.3 collective-permute-start.11
  34.0 3.7 %collective-permute-done.10.refs_1_ = bf16[256,256]{1,0:T(8,128)(2,1)S(1)} collective-permute-done((bf16[256,256]{1,0:T(8,128)(2,1)S(1)}, bf16[256,256]{1,0:T(8,128)(2,1)S(1)}, u32[]{:S(2)}, u32[]{:S(2)}) %collective-permute-start.10) | collective-permute-done | bytes 131104 | tf_op jit(solution)/shard_map/ppermute | solution.py:50
  37.7 1.6 %backward.4 = (f32[256,640]{1,0:T(8,128)S(1)}, bf16[256,256]{1,0:T(8,128)(2,1)S(1)}) custom-call(s32[16]{0:T(128)S(1)} %copy-done, bf16[256,640]{1,0:T(8,128)(2,1)S(1)} %get-tuple-element.41.qt_ref, bf16[1280,128]{1,0:T(8,128)(2,1)S(1)} %get-tuple-element.51.q_rows_ref, f32[2,640]{1,0:T(2,128)S(1)} %get-tuple-element.52.lse_ref, ...), custom_call_target="tpu_custom_call" | custom-call | flops 1048576 | bytes 1024 | tf_op jit(solution)/shard_map/backward/pallas_call | solution.py:224
  39.3 2.8 %collective-permute-start.13 = (bf16[256,256]{1,0:T(8,128)(2,1)S(1)}, bf16[256,256]{1,0:T(8,128)(2,1)S(1)}, u32[]{:S(2)}, u32[]{:S(2)}) collective-permute-start(bf16[256,256]{1,0:T(8,128)(2,1)S(1)} %get-tuple-element.65), channel_id=1, source_target_pairs={{0,24},{4,28},{8,0},{12,4},{16,8},{20,12},{24,16},{28,20},{1,25},{... | collective-permute-start | bytes 393224 | tf_op jit(solution)/shard_map/ppermute | solution.py:46
  42.1 0.0 collective-permute-done.6.refs_0_
  42.1 0.7 %features_out.5.out_ref = f32[256,1280]{1,0:T(8,128)S(1)} custom-call(bf16[256,640]{1,0:T(8,128)(2,1)S(1)} %get-tuple-element.49.attn_ref, bf16[256,1280]{1,0:T(8,128)(2,1)S(1)} %collective-permute-done.6.refs_0_, bf16[640,5120]{1,0:T(8,128)(2,1)S(1)} %get-tuple-element.50.refs_0_.refs_1_.refs_3_), custom_call_target="tpu_custom_call" | custom-call | flops 1048576 | bytes 1024 | tf_op jit(solution)/shard_map/features_out/pallas_call | solution.py:302
  42.8 2.3 %backward.5 = (bf16[256,640]{1,0:T(8,128)(2,1)}, f32[256,256]{1,0:T(8,128)S(1)}) custom-call(s32[16]{0:T(128)S(1)} %copy-done, bf16[256,640]{1,0:T(8,128)(2,1)S(1)} %get-tuple-element.41.qt_ref, bf16[1280,128]{1,0:T(8,128)(2,1)S(1)} %get-tuple-element.51.q_rows_ref, f32[2,640]{1,0:T(2,128)S(1)} %get-tuple-element.52.lse_ref, ...), custom_call_target="tpu_custom_call" | custom-call | flops 1048576 | bytes 1024 | tf_op jit(solution)/shard_map/backward/pallas_call | solution.py:224
  45.1 0.0 collective-permute-done.11.refs_1_
  45.1 0.0 collective-permute-done.12.refs_2_
  45.1 0.0 collective-permute-done.13.back_ref
  45.1 0.0 collective-permute-done.8.other_ref
  45.1 1.0 %finish.1 = (bf16[256,1280]{1,0:T(8,128)(2,1)}, bf16[256,128]{1,0:T(8,128)(2,1)}, bf16[256,128]{1,0:T(8,128)(2,1)}) custom-call(f32[256,1280]{1,0:T(8,128)S(1)} %features_out.5.out_ref, bf16[256,1280]{1,0:T(8,128)(2,1)S(1)} %collective-permute-done.8.other_ref, f32[256,256]{1,0:T(8,128)S(1)} %add_up.1.own_ref, ...), custom_call_target="tpu_custom_call" | custom-call | flops 1048576 | bytes 1024 | tf_op jit(solution)/shard_map/finish/pallas_call | solution.py:451
  (2 shorter events, 0.1 us)
Async XLA Ops:
  0.6 16.5 %copy-start = (s32[16]{0:T(128)S(1)}, s32[16]{0:T(128)}, u32[]{:S(2)}) copy-start(s32[16]{0:T(128)} %doc_ref.9) | copy-start | bytes 196
  1.6 12.1 %collective-permute-start = (bf16[256,1280]{1,0:T(8,128)(2,1)}, bf16[256,1280]{1,0:T(8,128)(2,1)S(1)}, u32[]{:S(2)}, u32[]{:S(2)}) collective-permute-start(bf16[256,1280]{1,0:T(8,128)(2,1)} %cot_hbm), channel_id=1, source_target_pairs={{0,1},{1,0},{2,3},{3,2},{4,5},{5,4},{6,7},{7,6},{8,9},{9,8},{10,11... | collective-permute-start | bytes 1966088 | tf_op jit(solution)/shard_map/ppermute | solution.py:50
  2.1 19.2 %collective-permute-start.5 = (bf16[256,1280]{1,0:T(8,128)(2,1)}, bf16[256,1280]{1,0:T(8,128)(2,1)S(1)}, u32[]{:S(2)}, u32[]{:S(2)}) collective-permute-start(bf16[256,1280]{1,0:T(8,128)(2,1)} %cot_hbm), channel_id=1, source_target_pairs={{0,2},{1,3},{2,0},{3,1},{4,6},{5,7},{6,4},{7,5},{8,10},{9,11},{10,... | collective-permute-start | bytes 1966088 | tf_op jit(solution)/shard_map/ppermute | solution.py:50
  4.7 7.4 %collective-permute-start.3 = (bf16[256,256]{1,0:T(8,128)(2,1)S(1)}, bf16[256,256]{1,0:T(8,128)(2,1)S(1)}, u32[]{:S(2)}, u32[]{:S(2)}) collective-permute-start(bf16[256,256]{1,0:T(8,128)(2,1)S(1)} %get-tuple-element.44.refs_3_.refs_2_), channel_id=1, source_target_pairs={{0,8},{4,12},{8,16},{12,20},{16,24},{20,28},{24,0},{28,4},{1,9},{5... | collective-permute-start | bytes 393224 | tf_op jit(solution)/shard_map/ppermute | solution.py:46
  6.3 10.9 %collective-permute-start.2 = (bf16[272,256]{1,0:T(8,128)(2,1)S(1)}, bf16[272,256]{1,0:T(8,128)(2,1)S(1)}, u32[]{:S(2)}, u32[]{:S(2)}) collective-permute-start(bf16[272,256]{1,0:T(8,128)(2,1)S(1)} %get-tuple-element.43), channel_id=1, source_target_pairs={{0,12},{4,16},{8,20},{12,24},{16,28},{1,13},{5,17},{9,21},{13,25},... | collective-permute-start | bytes 417800 | tf_op jit(solution)/shard_map/ppermute | solution.py:41
  10.7 6.5 %collective-permute-start.1 = (bf16[128,256]{1,0:T(8,128)(2,1)S(1)}, bf16[128,256]{1,0:T(8,128)(2,1)S(1)}, u32[]{:S(2)}, u32[]{:S(2)}) collective-permute-start(bf16[128,256]{1,0:T(8,128)(2,1)S(1)} %get-tuple-element.42), channel_id=1, source_target_pairs={{0,16},{4,20},{8,24},{12,28},{16,0},{20,4},{24,8},{28,12},{1,17},{... | collective-permute-start | bytes 196616 | tf_op jit(solution)/shard_map/ppermute | solution.py:46
  12.1 7.6 %collective-permute-start.4 = (bf16[256,256]{1,0:T(8,128)(2,1)S(1)}, bf16[256,256]{1,0:T(8,128)(2,1)S(1)}, u32[]{:S(2)}, u32[]{:S(2)}) collective-permute-start(bf16[256,256]{1,0:T(8,128)(2,1)S(1)} %broadcast_select_fusion), channel_id=1, source_target_pairs={{0,4},{4,0},{8,12},{12,8},{16,20},{20,16},{24,28},{28,24},{1,5},{5... | collective-permute-start | bytes 393224 | tf_op jit(solution)/shard_map/ppermute | solution.py:50
  22.0 2.2 %collective-permute-start.7 = (bf16[256,1280]{1,0:T(8,128)(2,1)S(1)}, bf16[256,1280]{1,0:T(8,128)(2,1)S(1)}, u32[]{:S(2)}, u32[]{:S(2)}) collective-permute-start(bf16[256,1280]{1,0:T(8,128)(2,1)S(1)} %features_out.6), channel_id=1, source_target_pairs={{0,1},{1,0},{2,3},{3,2},{4,5},{5,4},{6,7},{7,6},{8,9},{9,8},{10,11... | collective-permute-start | bytes 1966088 | tf_op jit(solution)/shard_map/ppermute | solution.py:50
  22.1 3.5 %collective-permute-start.9 = (bf16[256,1280]{1,0:T(8,128)(2,1)S(1)}, bf16[256,1280]{1,0:T(8,128)(2,1)S(1)}, u32[]{:S(2)}, u32[]{:S(2)}) collective-permute-start(bf16[256,1280]{1,0:T(8,128)(2,1)S(1)} %collective-permute-done.5.refs_0_), channel_id=1, source_target_pairs={{0,1},{1,0},{2,3},{3,2},{4,5},{5,4},{6,7},{7,6},{8,9},{9,8},{10,11... | collective-permute-start | bytes 1966088 | tf_op jit(solution)/shard_map/ppermute | solution.py:50
  23.3 18.7 %collective-permute-start.6 = (bf16[256,1280]{1,0:T(8,128)(2,1)S(1)}, bf16[256,1280]{1,0:T(8,128)(2,1)S(1)}, u32[]{:S(2)}, u32[]{:S(2)}) collective-permute-start(bf16[256,1280]{1,0:T(8,128)(2,1)S(1)} %features_out.4), channel_id=1, source_target_pairs={{0,1},{1,0},{2,3},{3,2},{4,5},{5,4},{6,7},{7,6},{8,9},{9,8},{10,11... | collective-permute-start | bytes 1966088 | tf_op jit(solution)/shard_map/ppermute | solution.py:50
  24.9 20.2 %collective-permute-start.8 = (bf16[256,1280]{1,0:T(8,128)(2,1)S(1)}, bf16[256,1280]{1,0:T(8,128)(2,1)S(1)}, u32[]{:S(2)}, u32[]{:S(2)}) collective-permute-start(bf16[256,1280]{1,0:T(8,128)(2,1)S(1)} %features_out.7), channel_id=1, source_target_pairs={{0,2},{1,3},{2,0},{3,1},{4,6},{5,7},{6,4},{7,5},{8,10},{9,11},{10,... | collective-permute-start | bytes 1966088 | tf_op jit(solution)/shard_map/ppermute | solution.py:50
  29.5 8.1 %collective-permute-start.10 = (bf16[256,256]{1,0:T(8,128)(2,1)S(1)}, bf16[256,256]{1,0:T(8,128)(2,1)S(1)}, u32[]{:S(2)}, u32[]{:S(2)}) collective-permute-start(bf16[256,256]{1,0:T(8,128)(2,1)S(1)} %get-tuple-element.60), channel_id=1, source_target_pairs={{0,4},{4,0},{8,12},{12,8},{16,20},{20,16},{24,28},{28,24},{1,5},{5... | collective-permute-start | bytes 393224 | tf_op jit(solution)/shard_map/ppermute | solution.py:50
  31.1 14.0 %collective-permute-start.12 = (bf16[256,256]{1,0:T(8,128)(2,1)S(1)}, bf16[256,256]{1,0:T(8,128)(2,1)S(1)}, u32[]{:S(2)}, u32[]{:S(2)}) collective-permute-start(bf16[256,256]{1,0:T(8,128)(2,1)S(1)} %get-tuple-element.64), channel_id=1, source_target_pairs={{0,20},{4,24},{8,28},{12,0},{16,4},{20,8},{24,12},{28,16},{1,21},{... | collective-permute-start | bytes 393224 | tf_op jit(solution)/shard_map/ppermute | solution.py:46
  33.7 11.4 %collective-permute-start.11 = (bf16[128,256]{1,0:T(8,128)(2,1)S(1)}, bf16[128,256]{1,0:T(8,128)(2,1)S(1)}, u32[]{:S(2)}, u32[]{:S(2)}) collective-permute-start(bf16[128,256]{1,0:T(8,128)(2,1)S(1)} %get-tuple-element.63), channel_id=1, source_target_pairs={{0,16},{4,20},{8,24},{12,28},{16,0},{20,4},{24,8},{28,12},{1,17},{... | collective-permute-start | bytes 196616 | tf_op jit(solution)/shard_map/ppermute | solution.py:46
  39.3 5.8 %collective-permute-start.13 = (bf16[256,256]{1,0:T(8,128)(2,1)S(1)}, bf16[256,256]{1,0:T(8,128)(2,1)S(1)}, u32[]{:S(2)}, u32[]{:S(2)}) collective-permute-start(bf16[256,256]{1,0:T(8,128)(2,1)S(1)} %get-tuple-element.65), channel_id=1, source_target_pairs={{0,24},{4,28},{8,0},{12,4},{16,8},{20,12},{24,16},{28,20},{1,25},{... | collective-permute-start | bytes 393224 | tf_op jit(solution)/shard_map/ppermute | solution.py:46
